TPU v7x, 32 devices: a whole 2x2x4 slice. The times are simulated.
32 devices in a mesh: dp: 4 (over x, core), seq: 8 (over z, y).
Axes of the slice: x: 2, y: 2, z: 4, core: 2. Of those that a mesh axis runs over, the one named last changes fastest.
Arguments:
- tokens: bfloat16 [16384, 1024], P(('dp', 'seq')), may hold values from -6 to 6
- ln_gain: bfloat16 [2, 1024], P(None, ('dp', 'seq')), may hold values from 0.5 to 1.5
- ln_shift: bfloat16 [2, 1024], P(None, ('dp', 'seq')), may hold values from -1.75 to 1.75
- w_gate: bfloat16 [2, 1024, 3072], P(None, None, ('dp', 'seq')), may hold values from -0.1875 to 0.1875
- w_reduce: bfloat16 [2, 1024, 512], P(None, None, ('dp', 'seq')), may hold values from -0.1875 to 0.1875
- decay_rate: bfloat16 [2, 512], P(None, ('dp', 'seq')), may hold values from 4.6386719e-05 to 0.034
- state_scale: bfloat16 [2, 512], P(None, ('dp', 'seq')), may hold values from -8 to 8
- skip_scale: bfloat16 [2, 512], P(None, ('dp', 'seq')), may hold values from -6 to 6
- w_expand: bfloat16 [2, 512, 3072], P(None, None, ('dp', 'seq')), may hold values from -0.25 to 0.25
- w_out: bfloat16 [2, 3072, 1024], P(None, ('dp', 'seq')), may hold values from -0.21875 to 0.21875
- prev_state: float32 [2, 4, 512], P(None, 'dp'), may hold values from -6 to 6
- item_lengths: int32 [4, 4], P('dp'), may hold values from 1 to 3840, 4096 in all within a row
- cotangent: bfloat16 [16384, 1024], P(('dp', 'seq')), may hold values from -6 to 6
Outputs:
- output: bfloat16 [16384, 1024], P(('dp', 'seq'))
- input_grad: bfloat16 [16384, 1024], P(('dp', 'seq'))
- grad_ln_gain: float32 [2, 1024], P(None, ('dp', 'seq'))
- grad_ln_shift: float32 [2, 1024], P(None, ('dp', 'seq'))
- grad_w_gate: float32 [2, 1024, 3072], P(None, None, ('dp', 'seq'))
- grad_w_reduce: float32 [2, 1024, 512], P(None, None, ('dp', 'seq'))
- grad_decay_rate: float32 [2, 512], P(None, ('dp', 'seq'))
- grad_state_scale: float32 [2, 512], P(None, ('dp', 'seq'))
- grad_skip_scale: float32 [2, 512], P(None, ('dp', 'seq'))
- grad_w_expand: float32 [2, 512, 3072], P(None, None, ('dp', 'seq'))
- grad_w_out: float32 [2, 3072, 1024], P(None, ('dp', 'seq'))
Inputs may be any that keep to these rules, and one draw needn't show every extreme that they name: `item_lengths`: each row sums to 4096.
All inputs are finite; a program needn't handle non-finite values.
Results may differ from a plain program's by a relative error of at most 0.017.
Values may be sent and summed in bfloat16 or wider, within the bound.
No kernel may reach another device: no remote copies, remote signals or barrier semaphores. Data moves between devices by JAX's collectives and lax.ppermute only.
A program may use at most 256 MiB of HBM per device.

v0:
```python
import jax
import jax.numpy as jnp
from jax import lax
from jax.sharding import PartitionSpec as P

LAYERS = 2


def prefix(part, axis, combine, identity, reverse):
    count = lax.axis_size(axis)
    place = lax.axis_index(axis)
    ahead = count - 1 - place if reverse else place
    gathered = jax.tree.map(lambda a: lax.all_gather(a, axis), part)
    state = jax.tree.map(lambda a, e: jnp.zeros_like(a) + jnp.asarray(e, a.dtype), part, identity)

    def one(hop, state):
        source = count - 1 - hop if reverse else hop
        return combine(
            state, jax.tree.map(lambda a: lax.dynamic_index_in_dim(a, source, 0, False), gathered)
        )

    return lax.fori_loop(0, ahead, one, state)


def combine_pair(earlier, latter):
    return (earlier[0] * latter[0], latter[0] * earlier[1] + latter[1])


def normalize(stream, gain_vec, shift_vec):
    centre = jnp.mean(stream, axis=-1, keepdims=True)
    centred = stream - centre
    spread = jnp.mean(centred * centred, axis=-1, keepdims=True)
    return centred * lax.rsqrt(spread + 1e-05) * gain_vec + shift_vec


def keep_mask(lengths, row_count):
    positions = lax.axis_index("seq") * row_count + jnp.arange(row_count, dtype=jnp.int32)
    starts = jnp.cumsum(lengths)[:-1]
    hits = jnp.any(positions[:, None] == starts[None, :], axis=1)
    return 1.0 - hits.astype(jnp.float32)[:, None]


def carry_forward(summary):
    arriving = prefix(
        summary, "seq", combine_pair, (jnp.ones_like(summary[0]), jnp.zeros_like(summary[1])), False
    )
    return arriving


def carry_backward(summary):
    arriving = prefix(
        summary, "seq", combine_pair, (jnp.ones_like(summary[0]), jnp.zeros_like(summary[1])), True
    )
    return arriving


def layer_forward(stream, params, keep_rows, start_state):
    gain_vec, shift_vec, w_gate, w_reduce, rate_vec, scale_vec, skip_vec, w_expand, w_out = params
    normed = normalize(stream, gain_vec.astype(jnp.float32), shift_vec.astype(jnp.float32)).astype(
        jnp.bfloat16
    )
    pre_gate = jnp.dot(normed, w_gate, preferred_element_type=jnp.float32)
    pre_reduce = jnp.dot(normed, w_reduce, preferred_element_type=jnp.float32)
    gate_act = jax.nn.gelu(pre_gate)
    reduced = jax.nn.gelu(pre_reduce)
    decay_vec = jnp.exp(-rate_vec.astype(jnp.float32))
    multiplier = decay_vec * keep_rows
    running, local_states = lax.associative_scan(
        combine_pair, (multiplier, (1.0 - decay_vec) * reduced), axis=0
    )
    total_scale = running[-1:]
    carry_scale, carry_state = carry_forward((total_scale, local_states[-1:]))
    state_in = carry_state + carry_scale * start_state
    states = local_states + running * state_in
    mixed = (
        scale_vec.astype(jnp.float32) * states + skip_vec.astype(jnp.float32) * reduced
    ).astype(jnp.bfloat16)
    expanded = jnp.dot(mixed, w_expand, preferred_element_type=jnp.float32)
    joined = (expanded * gate_act).astype(jnp.bfloat16)
    branch = jnp.dot(joined, w_out, preferred_element_type=jnp.float32)
    kept = (
        stream,
        normed,
        pre_gate,
        pre_reduce,
        multiplier,
        total_scale,
        state_in,
        states,
        mixed,
        expanded,
        joined,
    )
    return (stream + branch, kept)


def layer_backward(upstream, params, kept, keep_rows):
    gain_vec, shift_vec, w_gate, w_reduce, rate_vec, scale_vec, skip_vec, w_expand, w_out = params
    (
        stream,
        normed,
        pre_gate,
        pre_reduce,
        multiplier,
        total_scale,
        state_in,
        states,
        mixed,
        expanded,
        joined,
    ) = kept
    decay_vec = jnp.exp(-rate_vec.astype(jnp.float32))
    scale_f = scale_vec.astype(jnp.float32)
    skip_f = skip_vec.astype(jnp.float32)
    upstream_low = upstream.astype(jnp.bfloat16)
    grad_out = jnp.dot(joined.T, upstream_low, preferred_element_type=jnp.float32)
    d_joined = jnp.dot(upstream_low, w_out.T, preferred_element_type=jnp.float32)
    gate_act, gate_pull = jax.vjp(jax.nn.gelu, pre_gate)
    reduced, reduce_pull = jax.vjp(jax.nn.gelu, pre_reduce)
    d_expanded = (d_joined * gate_act).astype(jnp.bfloat16)
    d_gate = d_joined * expanded
    expand_turned = jnp.dot(d_expanded.T, mixed, preferred_element_type=jnp.float32)
    d_mixed = jnp.dot(d_expanded, w_expand.T, preferred_element_type=jnp.float32)
    d_states = scale_f * d_mixed
    following = jnp.concatenate([multiplier[1:], jnp.ones_like(multiplier[:1])], axis=0)
    back_running, back_local = lax.associative_scan(
        combine_pair, (following, d_states), axis=0, reverse=True
    )
    leftover, arriving = carry_backward((total_scale, multiplier[:1] * back_local[:1]))
    state_grad = back_local + back_running * arriving
    d_reduced = (1.0 - decay_vec) * state_grad + skip_f * d_mixed
    before = jnp.concatenate([state_in, states[:-1]], axis=0)
    grad_rate = -decay_vec * jnp.sum(state_grad * (keep_rows * before - reduced), axis=0)
    grad_scale = jnp.sum(d_mixed * states, axis=0)
    grad_skip = jnp.sum(d_mixed * reduced, axis=0)
    d_pre_gate = gate_pull(d_gate)[0].astype(jnp.bfloat16)
    d_pre_reduce = reduce_pull(d_reduced)[0].astype(jnp.bfloat16)
    gate_turned = jnp.dot(d_pre_gate.T, normed, preferred_element_type=jnp.float32)
    reduce_turned = jnp.dot(d_pre_reduce.T, normed, preferred_element_type=jnp.float32)
    d_normed = jnp.dot(d_pre_gate, w_gate.T, preferred_element_type=jnp.float32) + jnp.dot(
        d_pre_reduce, w_reduce.T, preferred_element_type=jnp.float32
    )
    normed_again, norm_pull = jax.vjp(
        normalize, stream, gain_vec.astype(jnp.float32), shift_vec.astype(jnp.float32)
    )
    d_stream, grad_gain, grad_shift = norm_pull(d_normed)
    return (
        upstream + d_stream,
        (
            grad_gain,
            grad_shift,
            gate_turned,
            reduce_turned,
            grad_rate,
            grad_scale,
            grad_skip,
            expand_turned,
            grad_out,
        ),
    )


def local(
    tokens,
    ln_gain,
    ln_shift,
    w_gate,
    w_reduce,
    decay_rate,
    state_scale,
    skip_scale,
    w_expand,
    w_out,
    prev_state,
    item_lengths,
    cotangent,
):
    row_count = tokens.shape[0]
    keep_rows = keep_mask(item_lengths[0], row_count)
    stream = tokens.astype(jnp.float32)
    saved = []
    for layer_index in range(LAYERS):
        params = (
            lax.all_gather(ln_gain[layer_index], ("dp", "seq"), axis=0, tiled=True),
            lax.all_gather(ln_shift[layer_index], ("dp", "seq"), axis=0, tiled=True),
            lax.all_gather(w_gate[layer_index], ("dp", "seq"), axis=1, tiled=True),
            lax.all_gather(w_reduce[layer_index], ("dp", "seq"), axis=1, tiled=True),
            lax.all_gather(decay_rate[layer_index], ("dp", "seq"), axis=0, tiled=True),
            lax.all_gather(state_scale[layer_index], ("dp", "seq"), axis=0, tiled=True),
            lax.all_gather(skip_scale[layer_index], ("dp", "seq"), axis=0, tiled=True),
            lax.all_gather(w_expand[layer_index], ("dp", "seq"), axis=1, tiled=True),
            lax.all_gather(w_out[layer_index], ("dp", "seq"), axis=0, tiled=True),
        )
        stream, kept = layer_forward(stream, params, keep_rows, prev_state[layer_index])
        saved.append((params, kept))
    output = stream.astype(jnp.bfloat16)
    upstream = cotangent.astype(jnp.float32)
    layer_grads = [None] * LAYERS
    for layer_index in reversed(range(LAYERS)):
        params, kept = saved[layer_index]
        params = (
            lax.all_gather(ln_gain[layer_index], ("dp", "seq"), axis=0, tiled=True),
            lax.all_gather(ln_shift[layer_index], ("dp", "seq"), axis=0, tiled=True),
            lax.all_gather(w_gate[layer_index], ("dp", "seq"), axis=1, tiled=True),
            lax.all_gather(w_reduce[layer_index], ("dp", "seq"), axis=1, tiled=True),
            lax.all_gather(decay_rate[layer_index], ("dp", "seq"), axis=0, tiled=True),
            lax.all_gather(state_scale[layer_index], ("dp", "seq"), axis=0, tiled=True),
            lax.all_gather(skip_scale[layer_index], ("dp", "seq"), axis=0, tiled=True),
            lax.all_gather(w_expand[layer_index], ("dp", "seq"), axis=1, tiled=True),
            lax.all_gather(w_out[layer_index], ("dp", "seq"), axis=0, tiled=True),
        )
        upstream, grad_terms = layer_backward(upstream, params, kept, keep_rows)
        summed = (
            lax.psum_scatter(grad_terms[0], ("dp", "seq"), scatter_dimension=0, tiled=True),
            lax.psum_scatter(grad_terms[1], ("dp", "seq"), scatter_dimension=0, tiled=True),
            lax.psum_scatter(grad_terms[2], ("dp", "seq"), scatter_dimension=0, tiled=True),
            lax.psum_scatter(grad_terms[3], ("dp", "seq"), scatter_dimension=0, tiled=True),
            lax.psum_scatter(grad_terms[4], ("dp", "seq"), scatter_dimension=0, tiled=True),
            lax.psum_scatter(grad_terms[5], ("dp", "seq"), scatter_dimension=0, tiled=True),
            lax.psum_scatter(grad_terms[6], ("dp", "seq"), scatter_dimension=0, tiled=True),
            lax.psum_scatter(grad_terms[7], ("dp", "seq"), scatter_dimension=0, tiled=True),
            lax.psum_scatter(grad_terms[8], ("dp", "seq"), scatter_dimension=0, tiled=True),
        )
        (
            grad_gain,
            grad_shift,
            gate_turned,
            reduce_turned,
            grad_rate,
            grad_scale,
            grad_skip,
            expand_turned,
            grad_out,
        ) = summed
        layer_grads[layer_index] = (
            grad_gain,
            grad_shift,
            gate_turned.T,
            reduce_turned.T,
            grad_rate,
            grad_scale,
            grad_skip,
            expand_turned.T,
            grad_out,
        )
    stacked = tuple(
        (
            jnp.stack([layer_grads[layer_index][member] for layer_index in range(LAYERS)], axis=0)
            for member in range(9)
        )
    )
    return (
        output,
        upstream.astype(jnp.bfloat16),
        stacked[0],
        stacked[1],
        stacked[2],
        stacked[3],
        stacked[4],
        stacked[5],
        stacked[6],
        stacked[7],
        stacked[8],
    )


def solution(mesh):
    return jax.shard_map(
        local,
        mesh=mesh,
        in_specs=(
            P(("dp", "seq"), None),
            P(None, ("dp", "seq")),
            P(None, ("dp", "seq")),
            P(None, None, ("dp", "seq")),
            P(None, None, ("dp", "seq")),
            P(None, ("dp", "seq")),
            P(None, ("dp", "seq")),
            P(None, ("dp", "seq")),
            P(None, None, ("dp", "seq")),
            P(None, ("dp", "seq"), None),
            P(None, "dp", None),
            P("dp", None),
            P(("dp", "seq"), None),
        ),
        out_specs=(
            P(("dp", "seq"), None),
            P(("dp", "seq"), None),
            P(None, ("dp", "seq")),
            P(None, ("dp", "seq")),
            P(None, None, ("dp", "seq")),
            P(None, None, ("dp", "seq")),
            P(None, ("dp", "seq")),
            P(None, ("dp", "seq")),
            P(None, ("dp", "seq")),
            P(None, None, ("dp", "seq")),
            P(None, ("dp", "seq"), None),
        ),
        check_vma=False,
    )
```

profile of v0, /device:TPU:8, one launch (start us, length us, event | category | flops | bytes accessed | tf_op | source)
XLA Modules:
  0.0 2246.9 jit_solution(16355329168737074682)
XLA Ops:
  19.2 41.2 %all-reduce.169 = (bf16[512]{0:T(512)(128)(2,1)S(1)}, bf16[1024]{0:T(1024)(128)(2,1)S(1)}, bf16[1024]{0:T(1024)(128)(2,1)S(1)}, bf16[512]{0:T(512)(128)(2,1)S(1)...) all-reduce(bf16[512]{0:T(512)(128)(2,1)S(1)} %dynamic-update-slice., ...), channel_id=3, replica_groups=mesh['dp'=4,'seq'=8] {'dp','seq'}, use_global_device_ids=true, to_apply=%add.149 | all-reduce | flops 7168 | bytes 28672
  215.8 24.6 %all-gather.25 = f32[8,1,512]{2,1,0:T(1,128)S(1)} all-gather(f32[1,1,512]{2,1,0:T(1,128)S(1)} %add_bitcast_fusion.2), channel_id=8, replica_groups=mesh['dp'=4,'seq'=8] {'seq'}, dimensions={0}, use_global_device_ids=true | all-gather | bytes 18432 | tf_op jit(solution)/shard_map/all_gather | solution.py:13
  252.3 26.1 %all-gather.24 = f32[8,1,512]{2,1,0:T(1,128)S(1)} all-gather(f32[1,1,512]{2,1,0:T(1,128)S(1)} %add_bitcast_fusion.3), channel_id=7, replica_groups=mesh['dp'=4,'seq'=8] {'seq'}, dimensions={0}, use_global_device_ids=true | all-gather | bytes 18432 | tf_op jit(solution)/shard_map/all_gather | solution.py:13
  308.6 16.2 all-gather.47.cloned.1.call-done
  490.2 25.8 %all-gather.27 = f32[8,1,512]{2,1,0:T(1,128)S(1)} all-gather(f32[1,1,512]{2,1,0:T(1,128)S(1)} %add_bitcast_fusion), channel_id=19, replica_groups=mesh['dp'=4,'seq'=8] {'seq'}, dimensions={0}, use_global_device_ids=true | all-gather | bytes 18432 | tf_op jit(solution)/shard_map/all_gather | solution.py:13
  516.7 26.2 %all-gather.26 = f32[8,1,512]{2,1,0:T(1,128)S(1)} all-gather(f32[1,1,512]{2,1,0:T(1,128)S(1)} %add_bitcast_fusion.1), channel_id=18, replica_groups=mesh['dp'=4,'seq'=8] {'seq'}, dimensions={0}, use_global_device_ids=true | all-gather | bytes 18432 | tf_op jit(solution)/shard_map/all_gather | solution.py:13
  554.1 9.2 fusion.20
  563.3 14.6 multiply_convert_fusion.1
  752.0 25.9 %all-gather.28 = f32[8,1,512]{2,1,0:T(1,128)S(1)} all-gather(f32[1,1,512]{2,1,0:T(1,128)S(1)} %fusion.125), channel_id=24, replica_groups=mesh['dp'=4,'seq'=8] {'seq'}, dimensions={0}, use_global_device_ids=true | all-gather | bytes 18432 | tf_op jit(solution)/shard_map/all_gather | solution.py:13
  828.4 11.5 multiply_convert_fusion
  1014.5 27.4 %all-gather.29 = f32[8,1,512]{2,1,0:T(1,128)S(1)} all-gather(f32[1,1,512]{2,1,0:T(1,128)S(1)} %fusion.124), channel_id=25, replica_groups=mesh['dp'=4,'seq'=8] {'seq'}, dimensions={0}, use_global_device_ids=true | all-gather | bytes 18432 | tf_op jit(solution)/shard_map/all_gather | solution.py:13
  1059.2 8.9 rev.19
  1101.2 10.2 fusion.170
  1111.4 10.2 fusion.171
  1130.6 10.1 fusion.166
  1151.4 41.6 %all-reduce.168 = (f32[1024]{0:T(1024)S(1)}, f32[1024]{0:T(1024)S(1)}, f32[1024]{0:T(1024)S(1)}, f32[1024]{0:T(1024)S(1)}, f32[512]{0:T(512)S(1)}, /*index=5*/f3...) all-reduce(f32[1024]{0:T(1024)S(1)} %copy-done.84, ...), channel_id=27, replica_groups=mesh['dp'=4,'seq'=8] {'dp','seq'}, use_global_device_ids=true, to_apply=%region_21.22.clone | all-reduce | flops 7168 | bytes 57344
  1207.7 11.3 reduce-scatter.13.cloned.1.call-done
  1219.0 136.6 %reduce-scatter.15.cloned.1.call-done = f32[16,1024]{1,0:T(8,128)} async-done(((f32[512,1024]{1,0:T(8,128)}), f32[16,1024]{1,0:T(8,128)}) %reduce-scatter.15.cloned.1.call-update) | async-done | bytes 65552 | tf_op jit(solution)/shard_map/reduce_scatter | solution.py:217
  1357.2 117.5 %reduce-scatter.17.cloned.1.call-done = f32[96,512]{1,0:T(8,128)} async-done(((f32[3072,512]{1,0:T(8,128)}), f32[96,512]{1,0:T(8,128)}) %reduce-scatter.17.cloned.1.call-update) | async-done | bytes 196624 | tf_op jit(solution)/shard_map/reduce_scatter | solution.py:221
  1474.7 119.9 %reduce-scatter.19.cloned.1.call-done = f32[96,512]{1,0:T(8,128)} async-done(((f32[3072,512]{1,0:T(8,128)}), f32[96,512]{1,0:T(8,128)}) %reduce-scatter.19.cloned.1.call-update) | async-done | bytes 196624 | tf_op jit(solution)/shard_map/reduce_scatter | solution.py:221
  1596.4 158.5 %reduce-scatter.21.cloned.1.call-done = f32[96,1024]{1,0:T(8,128)} async-done(((f32[3072,1024]{1,0:T(8,128)}), f32[96,1024]{1,0:T(8,128)}) %reduce-scatter.21.cloned.1.call-update) | async-done | bytes 393232 | tf_op jit(solution)/shard_map/reduce_scatter | solution.py:222
  1754.9 161.4 %reduce-scatter.23.cloned.1.call-done = f32[96,1024]{1,0:T(8,128)} async-done(((f32[3072,1024]{1,0:T(8,128)}), f32[96,1024]{1,0:T(8,128)}) %reduce-scatter.23.cloned.1.call-update) | async-done | bytes 393232 | tf_op jit(solution)/shard_map/reduce_scatter | solution.py:222
  1918.4 158.3 %reduce-scatter.9.cloned.1.call-done = f32[96,1024]{1,0:T(8,128)} async-done(((f32[3072,1024]{1,0:T(8,128)}), f32[96,1024]{1,0:T(8,128)}) %reduce-scatter.9.cloned.1.call-update) | async-done | bytes 393232 | tf_op jit(solution)/shard_map/reduce_scatter | solution.py:216
  2076.6 161.4 %reduce-scatter.11.cloned.1.call-done = f32[96,1024]{1,0:T(8,128)} async-done(((f32[3072,1024]{1,0:T(8,128)}), f32[96,1024]{1,0:T(8,128)}) %reduce-scatter.11.cloned.1.call-update) | async-done | bytes 393232 | tf_op jit(solution)/shard_map/reduce_scatter | solution.py:216
  (1075 shorter events, 882.2 us)
Async XLA Ops:
  7.2 54.3 %copy-start.153 = (s32[1,4]{1,0:T(1,128)S(1)}, s32[1,4]{1,0:T(1,128)}, u32[]{:S(2)}) copy-start(s32[1,4]{1,0:T(1,128)} %param.32) | copy-start | bytes 52
  7.2 107.0 %all-gather.39.cloned.1.call-start = ((), (), s32[]{:S(2)}) async-start(), calls=%async_computation.16 | async-start | bytes 1081344 | tf_op jit(solution)/shard_map/all_gather | solution.py:187
  8.7 273.6 %all-gather.43.cloned.1.call-start = ((), (), s32[]{:S(2)}) async-start(), calls=%async_computation.18 | async-start | bytes 6488064 | tf_op jit(solution)/shard_map/all_gather | solution.py:186
  10.6 280.6 %all-gather.41.cloned.1.call-start = ((), (), s32[]{:S(2)}) async-start(), calls=%async_computation.17 | async-start | bytes 3244032 | tf_op jit(solution)/shard_map/all_gather | solution.py:191
  12.3 286.7 %all-gather.45.cloned.1.call-start = ((), (), s32[]{:S(2)}) async-start(), calls=%async_computation.19 | async-start | bytes 6488064 | tf_op jit(solution)/shard_map/all_gather | solution.py:192
  14.2 310.6 %all-gather.47.cloned.1.call-start = ((), (), s32[]{:S(2)}) async-start(), calls=%async_computation.20 | async-start | bytes 1081344 | tf_op jit(solution)/shard_map/all_gather | solution.py:187
  14.8 532.8 %all-gather.49.cloned.1.call-start = ((), (), s32[]{:S(2)}) async-start(), calls=%async_computation.21 | async-start | bytes 3244032 | tf_op jit(solution)/shard_map/all_gather | solution.py:191
  15.4 538.8 %all-gather.51.cloned.1.call-start = ((), (), s32[]{:S(2)}) async-start(), calls=%async_computation.22 | async-start | bytes 6488064 | tf_op jit(solution)/shard_map/all_gather | solution.py:186
  16.1 547.2 %all-gather.53.cloned.1.call-start = ((), (), s32[]{:S(2)}) async-start(), calls=%async_computation.23 | async-start | bytes 6488064 | tf_op jit(solution)/shard_map/all_gather | solution.py:192
  16.9 1202.2 %reduce-scatter.13.cloned.1.call-start = ((), (), s32[]{:S(2)}) async-start(), calls=%async_computation.10 | async-start | bytes 2162688 | tf_op jit(solution)/shard_map/reduce_scatter | solution.py:217
  60.9 53.3 %copy-start.93 = (f32[512]{0:T(512)}, f32[512]{0:T(512)S(1)}, u32[]{:S(2)}) copy-start(f32[512]{0:T(512)S(1)} %get-tuple-element.511) | copy-start | bytes 6148
  213.7 64.8 %copy-start.145 = (f32[2,1,512]{2,1,0:T(1,128)S(1)}, f32[2,1,512]{2,1,0:T(1,128)}, u32[]{:S(2)}) copy-start(f32[2,1,512]{2,1,0:T(1,128)} %param.31) | copy-start | bytes 12292
  213.7 64.8 %copy-start.70 = (f32[512]{0:T(512)S(1)}, f32[512]{0:T(512)}, u32[]{:S(2)}) copy-start(f32[512]{0:T(512)} %convert_element_type.139) | copy-start | bytes 6148
  213.7 64.8 %copy-start.97 = (f32[512]{0:T(512)S(1)}, f32[512]{0:T(512)}, u32[]{:S(2)}) copy-start(f32[512]{0:T(512)} %convert_element_type.135) | copy-start | bytes 6148
  473.6 69.6 %copy-start.146 = (f32[2,1,512]{2,1,0:T(1,128)S(1)}, f32[2,1,512]{2,1,0:T(1,128)}, u32[]{:S(2)}) copy-start(f32[2,1,512]{2,1,0:T(1,128)} %param.31) | copy-start | bytes 12292
  473.6 69.6 %copy-start.72 = (f32[512]{0:T(512)S(1)}, f32[512]{0:T(512)}, u32[]{:S(2)}) copy-start(f32[512]{0:T(512)} %convert_element_type.144) | copy-start | bytes 6148
  473.7 69.6 %copy-start.99 = (f32[512]{0:T(512)S(1)}, f32[512]{0:T(512)}, u32[]{:S(2)}) copy-start(f32[512]{0:T(512)} %convert_element_type.140) | copy-start | bytes 6148
  1084.3 271.3 %reduce-scatter.15.cloned.1.call-start = ((), (), s32[]{:S(2)}) async-start(), calls=%async_computation.11 | async-start | bytes 2162688 | tf_op jit(solution)/shard_map/reduce_scatter | solution.py:217
  1087.8 386.9 %reduce-scatter.17.cloned.1.call-start = ((), (), s32[]{:S(2)}) async-start(), calls=%async_computation.12 | async-start | bytes 6488064 | tf_op jit(solution)/shard_map/reduce_scatter | solution.py:221
  1094.4 500.3 %reduce-scatter.19.cloned.1.call-start = ((), (), s32[]{:S(2)}) async-start(), calls=%async_computation.13 | async-start | bytes 6488064 | tf_op jit(solution)/shard_map/reduce_scatter | solution.py:221
  1100.9 654.0 %reduce-scatter.21.cloned.1.call-start = ((), (), s32[]{:S(2)}) async-start(), calls=%async_computation.14 | async-start | bytes 12976128 | tf_op jit(solution)/shard_map/reduce_scatter | solution.py:222
  1111.4 804.9 %reduce-scatter.23.cloned.1.call-start = ((), (), s32[]{:S(2)}) async-start(), calls=%async_computation.15 | async-start | bytes 12976128 | tf_op jit(solution)/shard_map/reduce_scatter | solution.py:222
  1121.7 955.0 %reduce-scatter.9.cloned.1.call-start = ((), (), s32[]{:S(2)}) async-start(), calls=%async_computation.8 | async-start | bytes 12976128 | tf_op jit(solution)/shard_map/reduce_scatter | solution.py:216
  1130.3 1107.8 %reduce-scatter.11.cloned.1.call-start = ((), (), s32[]{:S(2)}) async-start(), calls=%async_computation.9 | async-start | bytes 12976128 | tf_op jit(solution)/shard_map/reduce_scatter | solution.py:216
  (150 other events, 1744.0 us)
Sparse Core Ops, SparseCore 0:
  11.7 54.2 all-gather.38
  68.9 69.6 all-gather.42
  141.5 56.6 all-gather.40
  200.9 69.3 all-gather.44
  273.2 51.5 all-gather.46
  327.5 57.8 all-gather.48
  388.3 69.2 all-gather.50
  460.6 68.0 all-gather.52
  1084.5 134.5 reduce-scatter.12
  1221.2 134.3 reduce-scatter.14
  1361.3 113.3 reduce-scatter.16
  1481.2 113.4 reduce-scatter.18
  1600.7 154.1 reduce-scatter.20
  1761.8 154.4 reduce-scatter.22
  1922.2 154.4 reduce-scatter.8
  2083.6 154.4 reduce-scatter.10
where the time goes:
time: 2270 us; the launch traced here: 2250 us
  waiting for transfers between devices  1040 us (46%)
  local copies, waits for them, and re-layouts  569 us (25%)
  blocking collectives  239 us (11%)
  other arithmetic  219 us (10%)
  matrix products  158 us (7%)
    reduce_scatter x2, waiting for transfers between devices, local(): lax.psum_scatter(grad_terms[8], ('dp', 'seq'), scatter_dimension=0, tiled...  320 us
    reduce_scatter x2, waiting for transfers between devices, local(): lax.psum_scatter(grad_terms[2], ('dp', 'seq'), scatter_dimension=0, tiled...  320 us
    reduce_scatter x2, waiting for transfers between devices, local(): lax.psum_scatter(grad_terms[7], ('dp', 'seq'), scatter_dimension=0, tiled...  237 us
    slice x130, local copies, waits for them, and re-layouts, layer_backward(): lax.associative_scan(combine_pair, (following, d_states), axis=0, reverse...  225 us
    slice x120, local copies, waits for them, and re-layouts, layer_forward(): lax.associative_scan(combine_pair, (multiplier, (1.0 - decay_vec) * reduc...  162 us
    all_gather x6, blocking collectives, prefix(): gathered = jax.tree.map(lambda a: lax.all_gather(a, axis), part)  156 us
    reduce_scatter x2, waiting for transfers between devices, local(): lax.psum_scatter(grad_terms[3], ('dp', 'seq'), scatter_dimension=0, tiled...  148 us
    unnamed x2, blocking collectives  82.8 us
  transfers between devices with their start and end apart: 16, of which 9 were waited for; matrix products, arithmetic and copies ran while one was open for 21% of the time, Pallas kernels for 0%

commit v1 on v0

v1 whole, which is shorter than its diff:
```python
import functools
import itertools
import math

import jax
import jax.numpy as jnp
from jax import lax
from jax.experimental import pallas as pl
from jax.experimental.pallas import tpu as pltpu
from jax.sharding import PartitionSpec as P

LAYERS = 2
JOBS = 2
AXES = ("dp", "seq")
BF = jnp.bfloat16
F32 = jnp.float32
VMEM_LIMIT = 60 << 20
C0 = math.sqrt(2.0 / math.pi)
C1 = 0.044715
SMALL = 7
PAD = 128


class Layout:
    def __init__(self, mesh):
        self.dp, self.seq = mesh.shape["dp"], mesh.shape["seq"]
        self.x, self.c = self.dp // 2, 2
        self.s1 = 4
        self.s0 = self.seq // 4
        self.count = self.dp * self.seq
        self.alt_minor = self.s0 == self.x
        self.swap = self.s0 == self.x or self.s1 == self.x
        if self.alt_minor or not self.swap:
            self.alt, self.nq = self.s0, self.s1
        else:
            self.alt, self.nq = self.s1, self.s0
        self.n1, self.n2 = self.alt, self.x
        self.q = [self.pairs(self.move_q, k) for k in range(self.nq)]
        self.p1 = [self.pairs(self.move_1, k) for k in range(self.n1)]
        self.p2 = [self.pairs(self.move_2, k) for k in range(self.n2)]
        self.core = self.pairs(lambda x, c, a, q, k: (x, c ^ 1, a, q), 0)

    def place(self, x, c, a, q):
        s1, s0 = (q, a) if (self.alt_minor or not self.swap) else (a, q)
        return ((x * 2 + c) * self.s1 + s1) * self.s0 + s0

    def pairs(self, move, k):
        spots = itertools.product(range(self.x), range(2), range(self.alt), range(self.nq))
        return [(self.place(*spot), self.place(*move(*spot, k))) for spot in spots]

    def move_q(self, x, c, a, q, k):
        return (x, c, a, q ^ k)

    def move_1(self, x, c, a, q, k):
        return (x ^ k, c, a, q) if (self.swap and c == 1) else (x, c, a ^ k, q)

    def move_2(self, x, c, a, q, k):
        return (x, c, a ^ k, q) if (self.swap and c == 1) else (x ^ k, c, a, q)

    def natural_rows(self, rows):
        me_dp, me_seq = lax.axis_index("dp"), lax.axis_index("seq")
        mx, mc = me_dp // 2, me_dp % 2
        m1, m0 = me_seq // self.s0, me_seq % self.s0
        minor = self.alt_minor or not self.swap
        ma, mq = (m0, m1) if minor else (m1, m0)
        at = jnp.arange(self.count * rows, dtype=jnp.int32)
        row, at = at % rows, at // rows
        kq, at = at % self.nq, at // self.nq
        k1, at = at % self.n1, at // self.n1
        k2, half = at % self.n2, at // self.n2
        core = mc ^ half
        turned = (core == 1) if self.swap else (core > 1)
        kx = jnp.where(turned, k1, k2)
        ka = jnp.where(turned, k2, k1)
        x, a, q = mx ^ kx, ma ^ ka, mq ^ kq
        s1, s0 = (q, a) if minor else (a, q)
        return (((x * 2 + core) * self.s1 + s1) * self.s0 + s0) * rows + row


def permute(array, pairs):
    return lax.ppermute(array, AXES, pairs)


def cat(*arrays):
    return jnp.concatenate(arrays, axis=0)


def after(array, *others):
    return lax.optimization_barrier((array,) + others)[0]


def gather_job(lay, shard):
    line = cat(shard, *[permute(shard, lay.q[k]) for k in range(1, lay.nq)])
    plane = cat(line, *[permute(line, lay.p1[k]) for k in range(1, lay.n1)])
    own = cat(plane, *[permute(plane, lay.p2[k]) for k in range(1, lay.n2)])
    return own, permute(own, lay.core), line


def add_parts(parts, dtype):
    total = parts[0].astype(F32)
    for part in parts[1:]:
        total = total + part.astype(F32)
    return total.astype(dtype)


def scatter_job(lay, own, other):
    dtype = own.dtype
    held = add_parts([own, permute(other, lay.core)], dtype)
    for pairs, count, kind in ((lay.p2, lay.n2, dtype), (lay.p1, lay.n1, dtype), (lay.q, lay.nq, F32)):
        rows = held.shape[0] // count
        parts = [held[:rows]]
        for k in range(1, count):
            parts.append(permute(held[k * rows : (k + 1) * rows], pairs[k]))
        held = add_parts(parts, kind)
    return held


def dot_nn(a, b):
    return jnp.dot(a, b, preferred_element_type=F32)


def dot_nt(a, b):
    return lax.dot_general(a, b, (((1,), (1,)), ((), ())), preferred_element_type=F32)


def dot_tn(a, b):
    return lax.dot_general(a, b, (((0,), (0,)), ((), ())), preferred_element_type=F32)


def gelu(v):
    return 0.5 * v * (1.0 + jnp.tanh(C0 * (v + C1 * v * v * v)))


def gelu_both(v):
    square = v * v
    t = jnp.tanh(C0 * (v + C1 * v * square))
    half = 0.5 * (1.0 + t)
    slope = half + 0.5 * v * (1.0 - t * t) * (C0 * (1.0 + 3.0 * C1 * square))
    return v * half, slope


def full_spec(shape):
    return pl.BlockSpec(shape, lambda *_: (0,) * len(shape))


SCALARS = pl.BlockSpec(memory_space=pltpu.SMEM)


def enter_kernel(starts_n, scal, x_ref, gain_ref, shift_ref, wr_ref, rate_ref, normed_ref, pre_ref, local_ref):
    x = x_ref[...].astype(F32)
    centred = x - jnp.mean(x, axis=-1, keepdims=True)
    spread = jnp.mean(centred * centred, axis=-1, keepdims=True)
    normed = (centred * lax.rsqrt(spread + 1e-05) * gain_ref[...] + shift_ref[...]).astype(BF)
    normed_ref[...] = normed
    pre = dot_nt(normed, wr_ref[...])
    pre_ref[...] = pre
    rate = rate_ref[...]
    state = (1.0 - jnp.exp(-rate)) * gelu(pre)
    rows = state.shape[0]
    row = lax.broadcasted_iota(jnp.int32, (rows, 1), 0)
    k = 1
    while k < rows:
        open_rows = row >= k
        for s in range(starts_n):
            open_rows = open_rows & ~((row >= scal[s]) & (row < scal[s] + k))
        factor = jnp.where(open_rows, jnp.exp(-float(k) * rate), 0.0)
        state = state + factor * pltpu.roll(state, k, 0)
        k *= 2
    local_ref[...] = state


def enter_call(starts, x, gain, shift, wr, rate):
    rows, width = x.shape
    chan = wr.shape[0]
    return pl.pallas_call(
        functools.partial(enter_kernel, starts.shape[0]),
        out_shape=(
            jax.ShapeDtypeStruct((rows, width), BF),
            jax.ShapeDtypeStruct((rows, chan), F32),
            jax.ShapeDtypeStruct((rows, chan), F32),
        ),
        in_specs=[SCALARS] + [pl.BlockSpec(memory_space=pltpu.VMEM)] * 5,
        out_specs=(pl.BlockSpec(memory_space=pltpu.VMEM),) * 3,
        compiler_params=pltpu.CompilerParams(vmem_limit_bytes=VMEM_LIMIT),
        cost_estimate=pl.CostEstimate(
            flops=2 * rows * width * chan, bytes_accessed=10 * rows * width, transcendentals=rows * chan
        ),
        name="enter",
    )(starts, x, gain, shift, wr, rate)


def back_scan_kernel(starts_n, scal, dmix_ref, rate_ref, scale_ref, local_ref):
    rate = rate_ref[...]
    grad = scale_ref[...] * dmix_ref[...]
    rows = grad.shape[0]
    row = lax.broadcasted_iota(jnp.int32, (rows, 1), 0)
    k = 1
    while k < rows:
        open_rows = row < rows - k
        for s in range(starts_n):
            open_rows = open_rows & ~((row < scal[s]) & (row >= scal[s] - k))
        factor = jnp.where(open_rows, jnp.exp(-float(k) * rate), 0.0)
        grad = grad + factor * pltpu.roll(grad, rows - k, 0)
        k *= 2
    local_ref[...] = grad


def back_scan_call(starts, dmix, rate, scale):
    rows, chan = dmix.shape
    return pl.pallas_call(
        functools.partial(back_scan_kernel, starts.shape[0]),
        out_shape=jax.ShapeDtypeStruct((rows, chan), F32),
        in_specs=[SCALARS] + [pl.BlockSpec(memory_space=pltpu.VMEM)] * 3,
        out_specs=pl.BlockSpec(memory_space=pltpu.VMEM),
        compiler_params=pltpu.CompilerParams(vmem_limit_bytes=VMEM_LIMIT),
        cost_estimate=pl.CostEstimate(flops=40 * rows * chan, bytes_accessed=8 * rows * chan, transcendentals=0),
        name="back_scan",
    )(starts, dmix, rate, scale)


def leave_kernel(
    starts_n,
    scal,
    dmix_ref,
    local_ref,
    arriving_ref,
    states_ref,
    state_in_ref,
    pre_ref,
    normed_ref,
    x_ref,
    gain_ref,
    wr_ref,
    dnorm_ref,
    up_ref,
    rate_ref,
    scale_ref,
    skip_ref,
    up_out_ref,
    low_ref,
    grad_ref,
    small_ref,
):
    rate = rate_ref[...]
    decay = jnp.exp(-rate)
    dmix = dmix_ref[...]
    rows, chan = dmix.shape
    row = lax.broadcasted_iota(jnp.int32, (rows, 1), 0)
    later = row >= 0
    first = row < 0
    for s in range(starts_n):
        later = later & ~((row < scal[s]) & (scal[s] < rows))
        first = first | (row == scal[s])
    left = (rows - 1 - row).astype(F32)
    running = jnp.where(later, jnp.exp(-left * rate), 0.0)
    grad = local_ref[...] + running * arriving_ref[...]
    reduced, slope = gelu_both(pre_ref[...])
    states = states_ref[...]
    before = jnp.where(row == 0, state_in_ref[...], pltpu.roll(states, 1, 0))
    before = jnp.where(first, 0.0, before)
    small_ref[...] = jnp.zeros_like(small_ref)
    small_ref[2:3, :chan] = -decay * jnp.sum(grad * (before - reduced), axis=0, keepdims=True)
    small_ref[3:4, :chan] = jnp.sum(dmix * states, axis=0, keepdims=True)
    small_ref[4:5, :chan] = jnp.sum(dmix * reduced, axis=0, keepdims=True)
    d_reduced = (1.0 - decay) * grad + skip_ref[...] * dmix
    d_pre = (d_reduced * slope).astype(BF)
    grad_ref[...] = dot_tn(d_pre, normed_ref[...])
    d_normed = dnorm_ref[...] + dot_nn(d_pre, wr_ref[...])
    x = x_ref[...].astype(F32)
    centred = x - jnp.mean(x, axis=-1, keepdims=True)
    spread = jnp.mean(centred * centred, axis=-1, keepdims=True)
    rs = lax.rsqrt(spread + 1e-05)
    xhat = centred * rs
    small_ref[0:1, :] = jnp.sum(d_normed * xhat, axis=0, keepdims=True)
    small_ref[1:2, :] = jnp.sum(d_normed, axis=0, keepdims=True)
    e = d_normed * gain_ref[...]
    mean_e = jnp.mean(e, axis=-1, keepdims=True)
    mean_ex = jnp.mean(e * xhat, axis=-1, keepdims=True)
    up = up_ref[...].astype(F32) + rs * (e - mean_e - xhat * mean_ex)
    up_out_ref[...] = up
    low_ref[...] = up.astype(BF)


def leave_call(starts, dmix, local, arriving, states, state_in, pre, normed, x, gain, wr, dnorm, up, rate, scale, skip):
    rows, width = x.shape
    chan = dmix.shape[1]
    return pl.pallas_call(
        functools.partial(leave_kernel, starts.shape[0]),
        out_shape=(
            jax.ShapeDtypeStruct((rows, width), F32),
            jax.ShapeDtypeStruct((rows, width), BF),
            jax.ShapeDtypeStruct((chan, width), F32),
            jax.ShapeDtypeStruct((8, width), F32),
        ),
        in_specs=[SCALARS] + [pl.BlockSpec(memory_space=pltpu.VMEM)] * 15,
        out_specs=(pl.BlockSpec(memory_space=pltpu.VMEM),) * 4,
        compiler_params=pltpu.CompilerParams(vmem_limit_bytes=VMEM_LIMIT),
        cost_estimate=pl.CostEstimate(
            flops=4 * rows * width * chan, bytes_accessed=24 * rows * width, transcendentals=rows * chan
        ),
        name="leave",
    )(starts, dmix, local, arriving, states, state_in, pre, normed, x, gain, wr, dnorm, up, rate, scale, skip)


def wide_kernel(names, mode, blocks, dims, *refs):
    r = dict(zip(names, refs))
    width, chan = dims
    step = pl.program_id(0)
    forward, backward = mode != "back", mode != "fore"
    weights = r["weights"]

    @pl.when(step == 0)
    def _():
        if forward:
            r["acc"][...] = r["base"][...].astype(F32)
        if backward:
            r["d_normed"][...] = r["d_normed_in"][...] if "d_normed_in" in r else jnp.zeros_like(r["d_normed"])
            r["d_mixed"][...] = r["d_mixed_in"][...] if "d_mixed_in" in r else jnp.zeros_like(r["d_mixed"])

    @pl.when(step < blocks)
    def _():
        weights[...] = r["own"][...]

    @pl.when(step >= blocks)
    def _():
        weights[...] = r["other"][...]

    normed, mixed = r["normed"][...], r["mixed"][...]
    if forward:
        pre = dot_nt(normed, weights[:, :width])
        expanded = dot_nt(mixed, weights[:, 2 * width :])
        if mode == "fore":
            r["pre"][...] = pre
            r["expanded"][...] = expanded
    else:
        pre, expanded = r["pre"][...], r["expanded"][...]
    if backward:
        gate, slope = gelu_both(pre)
    else:
        gate = gelu(pre)
    joined = (expanded * gate).astype(BF)
    if forward:
        r["acc"][...] += dot_nn(joined, weights[:, width : 2 * width])
    if backward:
        low = r["low"][...]
        d_joined = dot_nt(low, weights[:, width : 2 * width])
        d_expanded = (d_joined * gate).astype(BF)
        d_pre = (d_joined * expanded * slope).astype(BF)
        r["d_mixed"][...] += dot_nn(d_expanded, weights[:, 2 * width :])
        r["d_normed"][...] += dot_nn(d_pre, weights[:, :width])

        def store(out):
            out[:, :width] = dot_tn(d_pre, normed).astype(BF)
            out[:, width : 2 * width] = dot_tn(joined, low).astype(BF)
            out[:, 2 * width :] = dot_tn(d_expanded, mixed).astype(BF)

        grads = r["grads"]
        store(grads)

        @pl.when(step < blocks)
        def _():
            r["grad_own"][...] = grads[...]

        @pl.when(step >= blocks)
        def _():
            r["grad_other"][...] = grads[...]

    if "out" in r:

        @pl.when(step == 2 * blocks - 1)
        def _():
            r["out"][...] = r["acc"][...].astype(r["out"].dtype)


def wide_call(mode, own, other, normed, mixed, base=None, low=None, pre=None, expanded=None, sums=None, out_dtype=None):
    rows, width = normed.shape
    chan = mixed.shape[1]
    span = own.shape[0]
    block = span // 2 if span % 32 == 0 else span
    blocks = span // block
    lanes = own.shape[1]
    forward, backward = mode != "back", mode != "fore"
    ins, outs, scratch = [], [], []
    ins.append(("own", own, pl.BlockSpec((block, lanes), lambda i: (jnp.minimum(i, blocks - 1), 0))))
    ins.append(("other", other, pl.BlockSpec((block, lanes), lambda i: (jnp.maximum(i - blocks, 0), 0))))
    ins.append(("normed", normed, full_spec(normed.shape)))
    ins.append(("mixed", mixed, full_spec(mixed.shape)))
    saved = pl.BlockSpec((rows, block), lambda i: (0, i))
    saved_shape = jax.ShapeDtypeStruct((rows, 2 * span), F32)
    if forward:
        ins.append(("base", base, full_spec(base.shape)))
    if backward:
        ins.append(("low", low, full_spec(low.shape)))
        if sums is not None:
            ins.append(("d_normed_in", sums[0], full_spec(sums[0].shape)))
            ins.append(("d_mixed_in", sums[1], full_spec(sums[1].shape)))
    if mode == "back":
        ins.append(("pre", pre, saved))
        ins.append(("expanded", expanded, saved))
    if mode == "fore":
        outs.append(("pre", saved_shape, saved))
        outs.append(("expanded", saved_shape, saved))
    if forward:
        if out_dtype == F32:
            outs.append(("acc", jax.ShapeDtypeStruct((rows, width), F32), full_spec((rows, width))))
        else:
            outs.append(("out", jax.ShapeDtypeStruct((rows, width), out_dtype), full_spec((rows, width))))
            scratch.append(("acc", pltpu.VMEM((rows, width), F32)))
    if backward:
        outs.append(("d_normed", jax.ShapeDtypeStruct((rows, width), F32), full_spec((rows, width))))
        outs.append(("d_mixed", jax.ShapeDtypeStruct((rows, chan), F32), full_spec((rows, chan))))
        grad = jax.ShapeDtypeStruct((span, lanes), BF)
        outs.append(("grad_own", grad, pl.BlockSpec((block, lanes), lambda i: (jnp.minimum(i, blocks - 1), 0))))
        outs.append(("grad_other", grad, pl.BlockSpec((block, lanes), lambda i: (jnp.maximum(i - blocks, 0), 0))))
        scratch.append(("grads", pltpu.VMEM((block, lanes), BF)))
    scratch.append(("weights", pltpu.VMEM((block, lanes), BF)))
    names = [name for name, _, _ in ins + outs] + [name for name, _ in scratch]
    passes = (1 if forward else 0) + (2 if backward else 0)
    return pl.pallas_call(
        functools.partial(wide_kernel, names, mode, blocks, (width, chan)),
        grid=(2 * blocks,),
        out_shape=tuple(shape for _, shape, _ in outs),
        in_specs=[spec for _, _, spec in ins],
        out_specs=tuple(spec for _, _, spec in outs),
        scratch_shapes=[shape for _, shape in scratch],
        compiler_params=pltpu.CompilerParams(vmem_limit_bytes=VMEM_LIMIT),
        cost_estimate=pl.CostEstimate(
            flops=2 * passes * rows * 2 * span * lanes,
            bytes_accessed=8 * span * lanes,
            transcendentals=rows * 2 * span,
        ),
        name="wide_" + mode,
    )(*[array for _, array, _ in ins])


def seq_gather(lay, vector):
    held, k = vector, 1
    while k < lay.seq:
        pairs = [
            (d * lay.seq + s, d * lay.seq + (s ^ k)) for d in range(lay.dp) for s in range(lay.seq)
        ]
        held = cat(held, permute(held, pairs))
        k *= 2
    return held


def clear_between(starts, low, high):
    hit = (starts[None, :] >= low[:, None]) & (starts[None, :] < high[:, None])
    return ~jnp.any(hit, axis=1)


def carry_forward(lay, lasts, start_state, rate, starts, rows):
    me = lax.axis_index("seq")
    source = me ^ jnp.arange(lay.seq, dtype=jnp.int32)
    hops = me - 1 - source
    live = (hops >= 0) & clear_between(starts, (source + 1) * rows, jnp.full_like(source, me * rows))
    weight = jnp.where(live[:, None], jnp.exp(-(jnp.maximum(hops, 0) * rows).astype(F32)[:, None] * rate), 0.0)
    open_start = ~jnp.any(starts < me * rows)
    start_weight = jnp.where(open_start, jnp.exp(-(me * rows).astype(F32) * rate), 0.0)
    return jnp.sum(weight * lasts, axis=0, keepdims=True) + start_weight * start_state


def carry_backward(lay, firsts, rate, starts, rows):
    me = lax.axis_index("seq")
    source = me ^ jnp.arange(lay.seq, dtype=jnp.int32)
    hops = source - me - 1
    live = (hops >= 0) & clear_between(starts, jnp.full_like(source, (me + 1) * rows), source * rows)
    weight = jnp.where(live[:, None], jnp.exp(-(jnp.maximum(hops, 0) * rows).astype(F32)[:, None] * rate), 0.0)
    return jnp.sum(weight * firsts, axis=0, keepdims=True)


def local(
    lay,
    tokens,
    ln_gain,
    ln_shift,
    w_gate,
    w_reduce,
    decay_rate,
    state_scale,
    skip_scale,
    w_expand,
    w_out,
    prev_state,
    item_lengths,
    cotangent,
):
    rows, width = tokens.shape
    chan = w_expand.shape[1]
    small_rows = w_reduce.shape[2]
    ff_rows = w_gate.shape[2]
    job_rows = ff_rows // JOBS
    me_seq = lax.axis_index("seq")
    starts = jnp.cumsum(item_lengths[0])[:-1].astype(jnp.int32)
    near = starts - me_seq * rows
    pos = jnp.arange(rows, dtype=jnp.int32)

    def vectors(layer):
        return jnp.concatenate(
            [
                ln_gain[layer].reshape(small_rows, 2),
                ln_shift[layer].reshape(small_rows, 2),
                decay_rate[layer][:, None],
                state_scale[layer][:, None],
                skip_scale[layer][:, None],
                jnp.zeros((small_rows, PAD - SMALL), BF),
            ],
            axis=1,
        )

    head = cat(*[jnp.concatenate([w_reduce[i].T, vectors(i)], axis=1) for i in range(LAYERS)])
    head_own, head_other, tie = gather_job(lay, head)
    relative = cat(head_own, head_other).reshape(lay.count, LAYERS, small_rows, width + PAD)
    relative = jnp.swapaxes(relative, 0, 1).reshape(LAYERS, chan, width + PAD)
    nature = lay.natural_rows(small_rows)
    turn = (nature[None, :] == jnp.arange(chan, dtype=jnp.int32)[:, None])
    turn_low = turn.astype(BF)

    params = []
    for layer in range(LAYERS):
        whole = dot_nn(turn_low, relative[layer]).astype(BF)
        vec = whole[:, width : width + SMALL].astype(F32)
        params.append(
            dict(
                wr=whole[:, :width],
                gain=vec[:, 0:2].reshape(1, width),
                shift=vec[:, 2:4].reshape(1, width),
                rate=vec[:, 4].reshape(1, chan),
                scale=vec[:, 5].reshape(1, chan),
                skip=vec[:, 6].reshape(1, chan),
            )
        )

    weights = []
    for layer in range(LAYERS):
        bundle = jnp.concatenate([w_gate[layer].T, w_out[layer], w_expand[layer].T], axis=1)
        jobs = []
        for job in range(JOBS):
            shard = after(bundle[job * job_rows : (job + 1) * job_rows], tie)
            own, other, tie = gather_job(lay, shard)
            jobs.append((own, other))
        weights.append(jobs)

    def enter(layer, stream):
        p = params[layer]
        normed, pre_reduce, local_states = enter_call(near, stream, p["gain"], p["shift"], p["wr"], p["rate"])
        lasts = seq_gather(lay, local_states[rows - 1 :])
        state_in = carry_forward(lay, lasts, prev_state[layer], p["rate"], starts, rows)
        closed = jnp.any((near[None, :] >= 0) & (near[None, :] <= pos[:, None]), axis=1)[:, None]
        running = jnp.where(closed, 0.0, jnp.exp(-(pos + 1).astype(F32)[:, None] * p["rate"]))
        states = local_states + running * state_in
        mixed = (p["scale"] * states + p["skip"] * jax.nn.gelu(pre_reduce)).astype(BF)
        return dict(stream=stream, normed=normed, pre_reduce=pre_reduce, states=states, state_in=state_in, mixed=mixed)

    def leave(layer, kept, sums, upstream):
        p = params[layer]
        d_normed, d_mixed = sums
        back_local = back_scan_call(near, d_mixed, p["rate"], p["scale"])
        keep_first = jnp.where(jnp.any(near == 0), 0.0, 1.0)
        firsts = seq_gather(lay, keep_first * jnp.exp(-p["rate"]) * back_local[:1])
        arriving = carry_backward(lay, firsts, p["rate"], starts, rows)
        upstream, low, grad_reduce, small = leave_call(
            near,
            d_mixed,
            back_local,
            arriving,
            kept["states"],
            kept["state_in"],
            kept["pre_reduce"],
            kept["normed"],
            kept["stream"],
            p["gain"],
            p["wr"],
            d_normed,
            upstream,
            p["rate"],
            p["scale"],
            p["skip"],
        )
        vec = jnp.concatenate(
            [
                small[0].reshape(chan, 2),
                small[1].reshape(chan, 2),
                small[2:5, :chan].T,
                jnp.zeros((chan, PAD - SMALL), F32),
            ],
            axis=1,
        )
        bundle = jnp.concatenate([grad_reduce, vec], axis=1)
        moved = jnp.dot(turn.astype(F32).T, bundle, precision=lax.Precision.HIGHEST)
        half = chan // 2
        return upstream, low, scatter_job(lay, moved[:half], moved[half:])

    kept, stream = [], tokens
    saved = []
    for layer in range(LAYERS - 1):
        k = enter(layer, stream)
        acc, done = stream, []
        for own, other in weights[layer]:
            pre, expanded, acc = wide_call("fore", own, other, k["normed"], k["mixed"], base=acc, out_dtype=F32)
            done.append((pre, expanded))
        stream = acc
        kept.append(k)
        saved.append(done)

    top = LAYERS - 1
    k = enter(top, stream)
    kept.append(k)
    acc, sums = stream, None
    scattered = [[None] * JOBS for _ in range(LAYERS)]
    low = cotangent
    for job, (own, other) in enumerate(weights[top]):
        last = job == JOBS - 1
        acc, d_normed, d_mixed, grad_own, grad_other = wide_call(
            "both", own, other, k["normed"], k["mixed"], base=acc, low=low, sums=sums, out_dtype=BF if last else F32
        )
        sums = (d_normed, d_mixed)
        scattered[top][job] = scatter_job(lay, grad_own, grad_other)
    output = acc
    heads = [None] * LAYERS
    upstream, low, heads[top] = leave(top, k, sums, cotangent)

    for layer in reversed(range(top)):
        k, sums = kept[layer], None
        for job, (own, other) in enumerate(weights[layer]):
            pre, expanded = saved[layer][job]
            d_normed, d_mixed, grad_own, grad_other = wide_call(
                "back", own, other, k["normed"], k["mixed"], low=low, pre=pre, expanded=expanded, sums=sums
            )
            sums = (d_normed, d_mixed)
            scattered[layer][job] = scatter_job(lay, grad_own, grad_other)
        upstream, low, heads[layer] = leave(layer, k, sums, upstream)

    whole = [cat(*scattered[layer]) for layer in range(LAYERS)]
    vecs = [heads[layer][:, width : width + SMALL] for layer in range(LAYERS)]
    return (
        output,
        low,
        jnp.stack([v[:, 0:2].reshape(-1) for v in vecs]),
        jnp.stack([v[:, 2:4].reshape(-1) for v in vecs]),
        jnp.stack([g[:, :width].T for g in whole]),
        jnp.stack([h[:, :width].T for h in heads]),
        jnp.stack([v[:, 4] for v in vecs]),
        jnp.stack([v[:, 5] for v in vecs]),
        jnp.stack([v[:, 6] for v in vecs]),
        jnp.stack([g[:, 2 * width :].T for g in whole]),
        jnp.stack([g[:, width : 2 * width] for g in whole]),
    )


def solution(mesh):
    lay = Layout(mesh)
    both = ("dp", "seq")
    return jax.shard_map(
        functools.partial(local, lay),
        mesh=mesh,
        in_specs=(
            P(both, None),
            P(None, both),
            P(None, both),
            P(None, None, both),
            P(None, None, both),
            P(None, both),
            P(None, both),
            P(None, both),
            P(None, None, both),
            P(None, both, None),
            P(None, "dp", None),
            P("dp", None),
            P(both, None),
        ),
        out_specs=(
            P(both, None),
            P(both, None),
            P(None, both),
            P(None, both),
            P(None, None, both),
            P(None, None, both),
            P(None, both),
            P(None, both),
            P(None, both),
            P(None, None, both),
            P(None, both, None),
        ),
        check_vma=False,
    )
```

time: 2270 us -> 698 us (0.31)
  waiting for transfers between devices: 1040 us -> 310 us
  local copies, waits for them, and re-layouts: 569 us -> 64.3 us
  blocking collectives: 239 us -> 0 us
  other arithmetic: 219 us -> 38.7 us
  Pallas kernels: 0 us -> 160 us
  matrix products: 158 us -> 10.1 us
  starting transfers between devices: 1.11 us -> 102 us
    reduce_scatter x8 -> x0, waiting for transfers between devices: 1020 us -> none  [the longest x2 320 us: local(): lax.psum_scatter(grad_terms[8], ('dp', 'seq'), scatter_dimension=0, tiled...]
    slice x256 -> x40, local copies, waits for them, and re-layouts: 394 us -> 16 us  [the longest x18 5.11 us: scatter_job(): parts.append(permute(held[k * rows:(k + 1) * rows], pairs[k]))]
    ppermute x0 -> x78, waiting for transfers between devices: none -> 310 us  [permute(): return lax.ppermute(array, AXES, pairs)]
    pallas_call x0 -> x12, Pallas kernels: none -> 160 us  [the longest x6 113 us: wide_call(): pl.pallas_call(functools.partial(wide_kernel, names, mode, blocks, (width...]
    all_gather x6 -> x0, blocking collectives: 156 us -> none  [prefix(): gathered = jax.tree.map(lambda a: lax.all_gather(a, axis), part)]
    dot_general x24 -> x4, matrix products: 158 us -> 10.1 us  [the longest x2 8.36 us: leave(): moved = jnp.dot(turn.astype(F32).T, bundle, precision=lax.Precision.HIGHEST)]
    pad x128 -> x0, local copies, waits for them, and re-layouts: 126 us -> none  [the longest x64 75.6 us: layer_backward(): lax.associative_scan(combine_pair, (following, d_states), axis=0, reverse...]
    ppermute x0 -> x78, starting transfers between devices: none -> 102 us  [permute(): return lax.ppermute(array, AXES, pairs)]
  transfers between devices with their start and end apart: 16 -> 78, of which waited for: 9 -> 45; matrix products, arithmetic and copies ran while one was open for 21% -> 15% of each run, Pallas kernels for 0% -> 10%
where the time goes in v1:
time: 698 us; the launch traced here: 688 us
  waiting for transfers between devices  310 us (44%)
  Pallas kernels  160 us (23%)
  starting transfers between devices  102 us (15%)
  local copies, waits for them, and re-layouts  64.3 us (9%)
  other arithmetic  38.7 us (6%)
  matrix products  10.1 us (1%)
    ppermute x78, waiting for transfers between devices, permute(): return lax.ppermute(array, AXES, pairs)  310 us
    pallas_call x6, Pallas kernels, wide_call(): pl.pallas_call(functools.partial(wide_kernel, names, mode, blocks, (width...  113 us
    ppermute x78, starting transfers between devices, permute(): return lax.ppermute(array, AXES, pairs)  102 us
    pallas_call x2, Pallas kernels, leave_call(): pl.pallas_call(functools.partial(leave_kernel, starts.shape[0]), out_shap...  21.1 us
    unnamed x90, local copies, waits for them, and re-layouts  18.7 us
    convert_element_type x12, other arithmetic, add_parts(): return total.astype(dtype)  16.6 us
  transfers between devices with their start and end apart: 78, of which 45 were waited for; matrix products, arithmetic and copies ran while one was open for 15% of the time, Pallas kernels for 10%

profile of v1, /device:TPU:8, one launch (start us, length us, event | category | flops | bytes accessed | tf_op | source)
XLA Modules:
  0.0 688.5 jit_solution(8365763502518231846)
XLA Ops:
  34.1 9.3 %collective-permute-done.4 = bf16[48,2560]{1,0:T(8,128)(2,1)S(1)} collective-permute-done((bf16[48,2560]{1,0:T(8,128)(2,1)S(1)}, bf16[48,2560]{1,0:T(8,128)(2,1)S(1)}, u32[]{:S(2)}, u32[]{:S(2)}) %collective-permute-start.4) | collective-permute-done | bytes 245792 | tf_op jit(solution)/shard_map/ppermute | solution.py:81
  58.5 9.2 %collective-permute-done.7 = bf16[48,2560]{1,0:T(8,128)(2,1)S(1)} collective-permute-done((bf16[48,2560]{1,0:T(8,128)(2,1)S(1)}, bf16[48,2560]{1,0:T(8,128)(2,1)S(1)}, u32[]{:S(2)}, u32[]{:S(2)}) %collective-permute-start.7) | collective-permute-done | bytes 245792 | tf_op jit(solution)/shard_map/ppermute | solution.py:81
  83.8 7.5 %collective-permute-done.10 = bf16[48,2560]{1,0:T(8,128)(2,1)S(1)} collective-permute-done((bf16[48,2560]{1,0:T(8,128)(2,1)S(1)}, bf16[48,2560]{1,0:T(8,128)(2,1)S(1)}, u32[]{:S(2)}, u32[]{:S(2)}) %collective-permute-start.10) | collective-permute-done | bytes 245792 | tf_op jit(solution)/shard_map/ppermute | solution.py:81
  106.4 9.6 %collective-permute-done.13 = bf16[48,2560]{1,0:T(8,128)(2,1)S(1)} collective-permute-done((bf16[48,2560]{1,0:T(8,128)(2,1)S(1)}, bf16[48,2560]{1,0:T(8,128)(2,1)S(1)}, u32[]{:S(2)}, u32[]{:S(2)}) %collective-permute-start.13) | collective-permute-done | bytes 245792 | tf_op jit(solution)/shard_map/ppermute | solution.py:81
  130.2 13.7 %collective-permute-done.15 = bf16[192,2560]{1,0:T(8,128)(2,1)S(1)} collective-permute-done((bf16[192,2560]{1,0:T(8,128)(2,1)S(1)}, bf16[192,2560]{1,0:T(8,128)(2,1)S(1)}, u32[]{:S(2)}, u32[]{:S(2)}) %collective-permute-start.15) | collective-permute-done | bytes 983072 | tf_op jit(solution)/shard_map/ppermute | solution.py:81
  156.4 17.0 %collective-permute-done.19 = bf16[384,2560]{1,0:T(8,128)(2,1)S(1)} collective-permute-done((bf16[384,2560]{1,0:T(8,128)(2,1)S(1)}, bf16[384,2560]{1,0:T(8,128)(2,1)S(1)}, u32[]{:S(2)}, u32[]{:S(2)}) %collective-permute-start.19) | collective-permute-done | bytes 1966112 | tf_op jit(solution)/shard_map/ppermute | solution.py:81
  178.7 15.7 %collective-permute-done.34 = bf16[384,2560]{1,0:T(8,128)(2,1)S(1)} collective-permute-done((bf16[384,2560]{1,0:T(8,128)(2,1)S(1)}, bf16[384,2560]{1,0:T(8,128)(2,1)S(1)}, u32[]{:S(2)}, u32[]{:S(2)}) %collective-permute-start.34) | collective-permute-done | bytes 1966112 | tf_op jit(solution)/shard_map/ppermute | solution.py:81
  230.8 11.2 %wide_fore.2 = (f32[512,1536]{1,0:T(8,128)}, f32[512,1536]{1,0:T(8,128)}, f32[512,1024]{1,0:T(8,128)}) custom-call(bf16[768,2560]{1,0:T(8,128)(2,1)} %constant_dynamic-update-slice_fusion.65.refs_0_, bf16[768,2560]{1,0:T(8,128)(2,1)} %collective-permute-done.29.refs_1_, bf16[512,1024]{1,0:T(8,128)(2,1)} %get-tuple-element.56.refs_2_.normed_ref, ...), custom_call_target="tpu_custom_call" | custom-call | flops 4026531840 | bytes 15728640 | tf_op jit(solution)/shard_map/wide_fore/pallas_call | solution.py:419
  242.0 11.6 %wide_fore.3 = (f32[512,1536]{1,0:T(8,128)}, f32[512,1536]{1,0:T(8,128)}, f32[512,1024]{1,0:T(8,128)}) custom-call(bf16[768,2560]{1,0:T(8,128)(2,1)} %constant_dynamic-update-slice_fusion.33.refs_0_, bf16[768,2560]{1,0:T(8,128)(2,1)} %collective-permute-done.20.refs_1_, bf16[512,1024]{1,0:T(8,128)(2,1)} %get-tuple-element.56.refs_2_.normed_ref, ...), custom_call_target="tpu_custom_call" | custom-call | flops 4026531840 | bytes 15728640 | tf_op jit(solution)/shard_map/wide_fore/pallas_call | solution.py:419
  276.6 25.0 %wide_both.2 = (f32[512,1024]{1,0:T(8,128)}, f32[512,1024]{1,0:T(8,128)}, f32[512,512]{1,0:T(8,128)}, bf16[768,2560]{1,0:T(8,128)(2,1)}, bf16[768,2560]{1,0:T(8,128)(2,1)}) custom-call(bf16[768,2560]{1,0:T(8,128)(2,1)} %constant_dynamic-update-slice_fusion.76.refs_0_, bf16[768,2560]{1,0:T(8,128)(2,1)} %collective-permute-done.35.refs_1_, ...), custom_call_target="tpu_custom_call" | custom-call | flops 12079595520 | bytes 15728640 | tf_op jit(solution)/shard_map/wide_both/pallas_call | solution.py:419
  301.6 25.5 %wide_both.3 = (bf16[512,1024]{1,0:T(8,128)(2,1)}, f32[512,1024]{1,0:T(8,128)}, f32[512,512]{1,0:T(8,128)}, bf16[768,2560]{1,0:T(8,128)(2,1)}, bf16[768,2560]{1,0:T(8,128)(2,1)}) custom-call(bf16[768,2560]{1,0:T(8,128)(2,1)} %constant_dynamic-update-slice_fusion.22.refs_0_, bf16[768,2560]{1,0:T(8,128)(2,1)} %collective-permute-done.17.refs_1_, ...), custom_call_target="tpu_custom_call" | custom-call | flops 12079595520 | bytes 15728640 | tf_op jit(solution)/shard_map/wide_both/pallas_call | solution.py:419
  347.2 10.5 %leave.2 = (f32[512,1024]{1,0:T(8,128)}, bf16[512,1024]{1,0:T(8,128)(2,1)}, f32[512,1024]{1,0:T(8,128)}, f32[8,1024]{1,0:T(8,128)}) custom-call(s32[3]{0:T(128)} %copy-done.13, f32[512,512]{1,0:T(8,128)} %get-tuple-element.68.dmix_ref, f32[512,512]{1,0:T(8,128)} %back_scan.2.local_ref, f32[1,512]{1,0:T(1,128)} %bitcast.137, ...), custom_call_target="tpu_custom_call" | custom-call | flops 1073741824 | bytes 12582912 | tf_op jit(solution)/shard_map/leave/pallas_call | solution.py:287
  357.7 19.3 %wide_back.2 = (f32[512,1024]{1,0:T(8,128)}, f32[512,512]{1,0:T(8,128)}, bf16[768,2560]{1,0:T(8,128)(2,1)}, bf16[768,2560]{1,0:T(8,128)(2,1)}) custom-call(bf16[768,2560]{1,0:T(8,128)(2,1)} %constant_dynamic-update-slice_fusion.65.refs_0_, bf16[768,2560]{1,0:T(8,128)(2,1)} %collective-permute-done.29.refs_1_, ...), custom_call_target="tpu_custom_call" | custom-call | flops 8053063680 | bytes 15728640 | tf_op jit(solution)/shard_map/wide_back/pallas_call | solution.py:419
  377.0 20.6 %wide_back.3 = (f32[512,1024]{1,0:T(8,128)}, f32[512,512]{1,0:T(8,128)}, bf16[768,2560]{1,0:T(8,128)(2,1)}, bf16[768,2560]{1,0:T(8,128)(2,1)}) custom-call(bf16[768,2560]{1,0:T(8,128)(2,1)} %constant_dynamic-update-slice_fusion.33.refs_0_, bf16[768,2560]{1,0:T(8,128)(2,1)} %collective-permute-done.20.refs_1_, ...), custom_call_target="tpu_custom_call" | custom-call | flops 8053063680 | bytes 15728640 | tf_op jit(solution)/shard_map/wide_back/pallas_call | solution.py:419
  418.6 10.6 %leave.3 = (f32[512,1024]{1,0:T(8,128)}, bf16[512,1024]{1,0:T(8,128)(2,1)}, f32[512,1024]{1,0:T(8,128)}, f32[8,1024]{1,0:T(8,128)}) custom-call(s32[3]{0:T(128)} %copy-done.13, f32[512,512]{1,0:T(8,128)} %get-tuple-element.77.dmix_ref, f32[512,512]{1,0:T(8,128)} %back_scan.3.local_ref, f32[1,512]{1,0:T(1,128)} %bitcast.136, ...), custom_call_target="tpu_custom_call" | custom-call | flops 1073741824 | bytes 12582912 | tf_op jit(solution)/shard_map/leave/pallas_call | solution.py:287
  453.1 7.8 %collective-permute-done.43 = f32[128,1152]{1,0:T(8,128)S(1)} collective-permute-done((f32[128,1152]{1,0:T(8,128)S(1)}, f32[128,1152]{1,0:T(8,128)S(1)}, u32[]{:S(2)}, u32[]{:S(2)}) %collective-permute-start.43) | collective-permute-done | bytes 589856 | tf_op jit(solution)/shard_map/ppermute | solution.py:81
  510.4 8.0 %collective-permute-done.67 = bf16[384,2560]{1,0:T(8,128)(2,1)S(1)} collective-permute-done((bf16[384,2560]{1,0:T(8,128)(2,1)}, bf16[384,2560]{1,0:T(8,128)(2,1)S(1)}, u32[]{:S(2)}, u32[]{:S(2)}) %collective-permute-start.67) | collective-permute-done | bytes 1966112 | tf_op jit(solution)/shard_map/ppermute | solution.py:81
  520.7 29.3 %collective-permute-done.73 = bf16[384,2560]{1,0:T(8,128)(2,1)S(1)} collective-permute-done((bf16[384,2560]{1,0:T(8,128)(2,1)}, bf16[384,2560]{1,0:T(8,128)(2,1)S(1)}, u32[]{:S(2)}, u32[]{:S(2)}) %collective-permute-start.73) | collective-permute-done | bytes 1966112 | tf_op jit(solution)/shard_map/ppermute | solution.py:81
  552.3 29.3 %collective-permute-done.55 = bf16[384,2560]{1,0:T(8,128)(2,1)S(1)} collective-permute-done((bf16[384,2560]{1,0:T(8,128)(2,1)}, bf16[384,2560]{1,0:T(8,128)(2,1)S(1)}, u32[]{:S(2)}, u32[]{:S(2)}) %collective-permute-start.55) | collective-permute-done | bytes 1966112 | tf_op jit(solution)/shard_map/ppermute | solution.py:81
  585.7 26.6 %collective-permute-done.61 = bf16[384,2560]{1,0:T(8,128)(2,1)S(1)} collective-permute-done((bf16[384,2560]{1,0:T(8,128)(2,1)S(1)}, bf16[384,2560]{1,0:T(8,128)(2,1)S(1)}, u32[]{:S(2)}, u32[]{:S(2)}) %collective-permute-start.61) | collective-permute-done | bytes 1966112 | tf_op jit(solution)/shard_map/ppermute | solution.py:81
  615.0 13.6 %collective-permute-done.71 = bf16[48,2560]{1,0:T(8,128)(2,1)S(1)} collective-permute-done((bf16[48,2560]{1,0:T(8,128)(2,1)S(1)}, bf16[48,2560]{1,0:T(8,128)(2,1)S(1)}, u32[]{:S(2)}, u32[]{:S(2)}) %collective-permute-start.71) | collective-permute-done | bytes 245792 | tf_op jit(solution)/shard_map/ppermute | solution.py:81
  639.2 8.5 %collective-permute-done.76 = bf16[48,2560]{1,0:T(8,128)(2,1)S(1)} collective-permute-done((bf16[48,2560]{1,0:T(8,128)(2,1)S(1)}, bf16[48,2560]{1,0:T(8,128)(2,1)S(1)}, u32[]{:S(2)}, u32[]{:S(2)}) %collective-permute-start.76) | collective-permute-done | bytes 245792 | tf_op jit(solution)/shard_map/ppermute | solution.py:81
  651.5 11.4 %collective-permute-done.77 = bf16[48,2560]{1,0:T(8,128)(2,1)S(1)} collective-permute-done((bf16[48,2560]{1,0:T(8,128)(2,1)S(1)}, bf16[48,2560]{1,0:T(8,128)(2,1)S(1)}, u32[]{:S(2)}, u32[]{:S(2)}) %collective-permute-start.77) | collective-permute-done | bytes 245792 | tf_op jit(solution)/shard_map/ppermute | solution.py:81
  664.2 7.6 %collective-permute-done.58 = bf16[48,2560]{1,0:T(8,128)(2,1)S(1)} collective-permute-done((bf16[48,2560]{1,0:T(8,128)(2,1)S(1)}, bf16[48,2560]{1,0:T(8,128)(2,1)S(1)}, u32[]{:S(2)}, u32[]{:S(2)}) %collective-permute-start.58) | collective-permute-done | bytes 245792 | tf_op jit(solution)/shard_map/ppermute | solution.py:81
  (401 shorter events, 326.5 us)
Async XLA Ops:
  52.3 69.6 %collective-permute-start.27 = (bf16[192,2560]{1,0:T(8,128)(2,1)S(1)}, bf16[192,2560]{1,0:T(8,128)(2,1)S(1)}, u32[]{:S(2)}, u32[]{:S(2)}) collective-permute-start(bf16[192,2560]{1,0:T(8,128)(2,1)S(1)} %get-tuple-element.186), channel_id=1, source_target_pairs={{0,1},{2,3},{4,5},{6,7},{1,0},{3,2},{5,4},{7,6},{8,24},{10,26},{12... | collective-permute-start | bytes 2949128 | tf_op jit(solution)/shard_map/ppermute | solution.py:81
  54.7 45.9 %collective-permute-start.22 = (bf16[256,1152]{1,0:T(8,128)(2,1)S(1)}, bf16[256,1152]{1,0:T(8,128)(2,1)S(1)}, u32[]{:S(2)}, u32[]{:S(2)}) collective-permute-start(bf16[256,1152]{1,0:T(8,128)(2,1)S(1)} %get-tuple-element.167), channel_id=1, source_target_pairs={{0,16},{2,18},{4,20},{6,22},{1,17},{3,19},{5,21},{7,23},{8,9},{10,... | collective-permute-start | bytes 1769480 | tf_op jit(solution)/shard_map/ppermute | solution.py:81
  81.5 43.1 %collective-permute-start.18 = (bf16[192,2560]{1,0:T(8,128)(2,1)S(1)}, bf16[192,2560]{1,0:T(8,128)(2,1)S(1)}, u32[]{:S(2)}, u32[]{:S(2)}) collective-permute-start(bf16[192,2560]{1,0:T(8,128)(2,1)S(1)} %get-tuple-element.198), channel_id=1, source_target_pairs={{0,1},{2,3},{4,5},{6,7},{1,0},{3,2},{5,4},{7,6},{8,24},{10,26},{12... | collective-permute-start | bytes 2949128 | tf_op jit(solution)/shard_map/ppermute | solution.py:81
  116.0 30.9 %collective-permute-start.23 = (bf16[512,1152]{1,0:T(8,128)(2,1)S(1)}, bf16[512,1152]{1,0:T(8,128)(2,1)S(1)}, u32[]{:S(2)}, u32[]{:S(2)}) collective-permute-start(bf16[512,1152]{1,0:T(8,128)(2,1)S(1)} %get-tuple-element.149), channel_id=1, source_target_pairs={{0,8},{2,10},{4,12},{6,14},{1,9},{3,11},{5,13},{7,15},{8,0},{10,2}... | collective-permute-start | bytes 3538952 | tf_op jit(solution)/shard_map/ppermute | solution.py:81
  125.7 47.7 %collective-permute-start.19 = (bf16[384,2560]{1,0:T(8,128)(2,1)S(1)}, bf16[384,2560]{1,0:T(8,128)(2,1)S(1)}, u32[]{:S(2)}, u32[]{:S(2)}) collective-permute-start(bf16[384,2560]{1,0:T(8,128)(2,1)S(1)} %get-tuple-element.145), channel_id=1, source_target_pairs={{0,16},{2,18},{4,20},{6,22},{1,17},{3,19},{5,21},{7,23},{8,9},{10,... | collective-permute-start | bytes 5898248 | tf_op jit(solution)/shard_map/ppermute | solution.py:81
  128.7 65.7 %collective-permute-start.34 = (bf16[384,2560]{1,0:T(8,128)(2,1)S(1)}, bf16[384,2560]{1,0:T(8,128)(2,1)S(1)}, u32[]{:S(2)}, u32[]{:S(2)}) collective-permute-start(bf16[384,2560]{1,0:T(8,128)(2,1)S(1)} %get-tuple-element.141), channel_id=1, source_target_pairs={{0,16},{2,18},{4,20},{6,22},{1,17},{3,19},{5,21},{7,23},{8,9},{10,... | collective-permute-start | bytes 5898248 | tf_op jit(solution)/shard_map/ppermute | solution.py:81
  145.0 70.5 %collective-permute-start.16 = (bf16[384,2560]{1,0:T(8,128)(2,1)}, bf16[384,2560]{1,0:T(8,128)(2,1)}, u32[]{:S(2)}, u32[]{:S(2)}) collective-permute-start(bf16[384,2560]{1,0:T(8,128)(2,1)} %get-tuple-element.147), channel_id=1, source_target_pairs={{0,16},{2,18},{4,20},{6,22},{1,17},{3,19},{5,21},{7,23},{8,9},{10,... | collective-permute-start | bytes 5898248 | tf_op jit(solution)/shard_map/ppermute | solution.py:81
  153.6 77.2 %collective-permute-start.29 = (bf16[768,2560]{1,0:T(8,128)(2,1)}, bf16[768,2560]{1,0:T(8,128)(2,1)}, u32[]{:S(2)}, u32[]{:S(2)}) collective-permute-start(bf16[768,2560]{1,0:T(8,128)(2,1)} %constant_dynamic-update-slice_fusion.65.refs_0_), channel_id=1, source_target_pairs={{0,8},{2,10},{4,12},{6,14},{1,9},{3,11},{5,13},{7,15},{8,0},{10,2}... | collective-permute-start | bytes 11796488 | tf_op jit(solution)/shard_map/ppermute | solution.py:81
  174.7 67.3 %collective-permute-start.20 = (bf16[768,2560]{1,0:T(8,128)(2,1)}, bf16[768,2560]{1,0:T(8,128)(2,1)}, u32[]{:S(2)}, u32[]{:S(2)}) collective-permute-start(bf16[768,2560]{1,0:T(8,128)(2,1)} %constant_dynamic-update-slice_fusion.33.refs_0_), channel_id=1, source_target_pairs={{0,8},{2,10},{4,12},{6,14},{1,9},{3,11},{5,13},{7,15},{8,0},{10,2}... | collective-permute-start | bytes 11796488 | tf_op jit(solution)/shard_map/ppermute | solution.py:81
  195.8 80.8 %collective-permute-start.35 = (bf16[768,2560]{1,0:T(8,128)(2,1)}, bf16[768,2560]{1,0:T(8,128)(2,1)}, u32[]{:S(2)}, u32[]{:S(2)}) collective-permute-start(bf16[768,2560]{1,0:T(8,128)(2,1)} %constant_dynamic-update-slice_fusion.76.refs_0_), channel_id=1, source_target_pairs={{0,8},{2,10},{4,12},{6,14},{1,9},{3,11},{5,13},{7,15},{8,0},{10,2}... | collective-permute-start | bytes 11796488 | tf_op jit(solution)/shard_map/ppermute | solution.py:81
  218.6 83.0 %collective-permute-start.17 = (bf16[768,2560]{1,0:T(8,128)(2,1)}, bf16[768,2560]{1,0:T(8,128)(2,1)}, u32[]{:S(2)}, u32[]{:S(2)}) collective-permute-start(bf16[768,2560]{1,0:T(8,128)(2,1)} %constant_dynamic-update-slice_fusion.22.refs_0_), channel_id=1, source_target_pairs={{0,8},{2,10},{4,12},{6,14},{1,9},{3,11},{5,13},{7,15},{8,0},{10,2}... | collective-permute-start | bytes 11796488 | tf_op jit(solution)/shard_map/ppermute | solution.py:81
  443.8 43.1 %collective-permute-start.66 = (bf16[768,2560]{1,0:T(8,128)(2,1)}, bf16[768,2560]{1,0:T(8,128)(2,1)}, u32[]{:S(2)}, u32[]{:S(2)}) collective-permute-start(bf16[768,2560]{1,0:T(8,128)(2,1)} %get-tuple-element.90), channel_id=1, source_target_pairs={{0,8},{2,10},{4,12},{6,14},{1,9},{3,11},{5,13},{7,15},{8,0},{10,2}... | collective-permute-start | bytes 11796488 | tf_op jit(solution)/shard_map/ppermute | solution.py:81
  444.4 49.4 %collective-permute-start.72 = (bf16[768,2560]{1,0:T(8,128)(2,1)}, bf16[768,2560]{1,0:T(8,128)(2,1)}, u32[]{:S(2)}, u32[]{:S(2)}) collective-permute-start(bf16[768,2560]{1,0:T(8,128)(2,1)} %get-tuple-element.92), channel_id=1, source_target_pairs={{0,8},{2,10},{4,12},{6,14},{1,9},{3,11},{5,13},{7,15},{8,0},{10,2}... | collective-permute-start | bytes 11796488 | tf_op jit(solution)/shard_map/ppermute | solution.py:81
  498.7 51.3 %collective-permute-start.73 = (bf16[384,2560]{1,0:T(8,128)(2,1)}, bf16[384,2560]{1,0:T(8,128)(2,1)S(1)}, u32[]{:S(2)}, u32[]{:S(2)}) collective-permute-start(bf16[384,2560]{1,0:T(8,128)(2,1)} %slice.575), channel_id=1, source_target_pairs={{0,16},{2,18},{4,20},{6,22},{1,17},{3,19},{5,21},{7,23},{8,9},{10,... | collective-permute-start | bytes 5898248 | tf_op jit(solution)/shard_map/ppermute | solution.py:81
  504.6 76.9 %collective-permute-start.55 = (bf16[384,2560]{1,0:T(8,128)(2,1)}, bf16[384,2560]{1,0:T(8,128)(2,1)S(1)}, u32[]{:S(2)}, u32[]{:S(2)}) collective-permute-start(bf16[384,2560]{1,0:T(8,128)(2,1)} %slice.549), channel_id=1, source_target_pairs={{0,16},{2,18},{4,20},{6,22},{1,17},{3,19},{5,21},{7,23},{8,9},{10,... | collective-permute-start | bytes 5898248 | tf_op jit(solution)/shard_map/ppermute | solution.py:81
  509.3 103.1 %collective-permute-start.61 = (bf16[384,2560]{1,0:T(8,128)(2,1)S(1)}, bf16[384,2560]{1,0:T(8,128)(2,1)S(1)}, u32[]{:S(2)}, u32[]{:S(2)}) collective-permute-start(bf16[384,2560]{1,0:T(8,128)(2,1)S(1)} %slice.557), channel_id=1, source_target_pairs={{0,16},{2,18},{4,20},{6,22},{1,17},{3,19},{5,21},{7,23},{8,9},{10,... | collective-permute-start | bytes 5898248 | tf_op jit(solution)/shard_map/ppermute | solution.py:81
  518.9 64.9 %collective-permute-start.68 = (bf16[192,2560]{1,0:T(8,128)(2,1)S(1)}, bf16[192,2560]{1,0:T(8,128)(2,1)S(1)}, u32[]{:S(2)}, u32[]{:S(2)}) collective-permute-start(bf16[192,2560]{1,0:T(8,128)(2,1)S(1)} %slice.569), channel_id=1, source_target_pairs={{0,1},{2,3},{4,5},{6,7},{1,0},{3,2},{5,4},{7,6},{8,24},{10,26},{12... | collective-permute-start | bytes 2949128 | tf_op jit(solution)/shard_map/ppermute | solution.py:81
  550.5 78.2 %collective-permute-start.74 = (bf16[192,2560]{1,0:T(8,128)(2,1)S(1)}, bf16[192,2560]{1,0:T(8,128)(2,1)S(1)}, u32[]{:S(2)}, u32[]{:S(2)}) collective-permute-start(bf16[192,2560]{1,0:T(8,128)(2,1)S(1)} %slice.577), channel_id=1, source_target_pairs={{0,1},{2,3},{4,5},{6,7},{1,0},{3,2},{5,4},{7,6},{8,24},{10,26},{12... | collective-permute-start | bytes 2949128 | tf_op jit(solution)/shard_map/ppermute | solution.py:81
  582.1 50.5 %collective-permute-start.56 = (bf16[192,2560]{1,0:T(8,128)(2,1)S(1)}, bf16[192,2560]{1,0:T(8,128)(2,1)S(1)}, u32[]{:S(2)}, u32[]{:S(2)}) collective-permute-start(bf16[192,2560]{1,0:T(8,128)(2,1)S(1)} %slice.551), channel_id=1, source_target_pairs={{0,1},{2,3},{4,5},{6,7},{1,0},{3,2},{5,4},{7,6},{8,24},{10,26},{12... | collective-permute-start | bytes 2949128 | tf_op jit(solution)/shard_map/ppermute | solution.py:81
  584.6 30.5 %collective-permute-start.70 = (bf16[48,2560]{1,0:T(8,128)(2,1)S(1)}, bf16[48,2560]{1,0:T(8,128)(2,1)S(1)}, u32[]{:S(2)}, u32[]{:S(2)}) collective-permute-start(bf16[48,2560]{1,0:T(8,128)(2,1)S(1)} %get-tuple-element.140), channel_id=1, source_target_pairs={{0,4},{2,6},{4,0},{6,2},{1,5},{3,7},{5,1},{7,3},{8,12},{10,14},{12... | collective-permute-start | bytes 737288 | tf_op jit(solution)/shard_map/ppermute | solution.py:81
  631.7 31.1 %collective-permute-start.77 = (bf16[48,2560]{1,0:T(8,128)(2,1)S(1)}, bf16[48,2560]{1,0:T(8,128)(2,1)S(1)}, u32[]{:S(2)}, u32[]{:S(2)}) collective-permute-start(bf16[48,2560]{1,0:T(8,128)(2,1)S(1)} %get-tuple-element.136), channel_id=1, source_target_pairs={{0,6},{2,4},{4,2},{6,0},{1,7},{3,5},{5,3},{7,1},{8,14},{10,12},{12... | collective-permute-start | bytes 737288 | tf_op jit(solution)/shard_map/ppermute | solution.py:81
  634.0 37.9 %collective-permute-start.58 = (bf16[48,2560]{1,0:T(8,128)(2,1)S(1)}, bf16[48,2560]{1,0:T(8,128)(2,1)S(1)}, u32[]{:S(2)}, u32[]{:S(2)}) collective-permute-start(bf16[48,2560]{1,0:T(8,128)(2,1)S(1)} %get-tuple-element.134), channel_id=1, source_target_pairs={{0,4},{2,6},{4,0},{6,2},{1,5},{3,7},{5,1},{7,3},{8,12},{10,14},{12... | collective-permute-start | bytes 737288 | tf_op jit(solution)/shard_map/ppermute | solution.py:81
  638.0 40.7 %collective-permute-start.59 = (bf16[48,2560]{1,0:T(8,128)(2,1)S(1)}, bf16[48,2560]{1,0:T(8,128)(2,1)S(1)}, u32[]{:S(2)}, u32[]{:S(2)}) collective-permute-start(bf16[48,2560]{1,0:T(8,128)(2,1)S(1)} %get-tuple-element.133), channel_id=1, source_target_pairs={{0,6},{2,4},{4,2},{6,0},{1,7},{3,5},{5,3},{7,1},{8,14},{10,12},{12... | collective-permute-start | bytes 737288 | tf_op jit(solution)/shard_map/ppermute | solution.py:81
  647.7 31.1 %collective-permute-start.63 = (bf16[48,2560]{1,0:T(8,128)(2,1)S(1)}, bf16[48,2560]{1,0:T(8,128)(2,1)S(1)}, u32[]{:S(2)}, u32[]{:S(2)}) collective-permute-start(bf16[48,2560]{1,0:T(8,128)(2,1)S(1)} %get-tuple-element.129), channel_id=1, source_target_pairs={{0,2},{2,0},{4,6},{6,4},{1,3},{3,1},{5,7},{7,5},{8,10},{10,8},{12,... | collective-permute-start | bytes 737288 | tf_op jit(solution)/shard_map/ppermute | solution.py:81
  (88 other events, 1364.0 us)

commit v2 on v1

v2 whole, which is shorter than its diff:
```python
import functools
import itertools
import math

import jax
import jax.numpy as jnp
from jax import lax
from jax.experimental import pallas as pl
from jax.experimental.pallas import tpu as pltpu
from jax.sharding import PartitionSpec as P

LAYERS = 2
JOBS = 2
AXES = ("dp", "seq")
BF = jnp.bfloat16
F32 = jnp.float32
VMEM_LIMIT = 60 << 20
C0 = math.sqrt(2.0 / math.pi)
C1 = 0.044715
SMALL = 7
PAD = 128


class Layout:
    def __init__(self, mesh):
        self.dp, self.seq = mesh.shape["dp"], mesh.shape["seq"]
        self.x, self.c = self.dp // 2, 2
        self.s1 = 4
        self.s0 = self.seq // 4
        self.count = self.dp * self.seq
        self.alt_minor = self.s0 == self.x
        self.swap = self.s0 == self.x or self.s1 == self.x
        if self.alt_minor or not self.swap:
            self.alt, self.nq = self.s0, self.s1
        else:
            self.alt, self.nq = self.s1, self.s0
        self.n1, self.n2 = self.alt, self.x
        self.q = [self.pairs(self.move_q, k) for k in range(self.nq)]
        self.p1 = [self.pairs(self.move_1, k) for k in range(self.n1)]
        self.p2 = [self.pairs(self.move_2, k) for k in range(self.n2)]
        self.core = self.pairs(lambda x, c, a, q, k: (x, c ^ 1, a, q), 0)

    def place(self, x, c, a, q):
        s1, s0 = (q, a) if (self.alt_minor or not self.swap) else (a, q)
        return ((x * 2 + c) * self.s1 + s1) * self.s0 + s0

    def pairs(self, move, k):
        spots = itertools.product(range(self.x), range(2), range(self.alt), range(self.nq))
        return [(self.place(*spot), self.place(*move(*spot, k))) for spot in spots]

    def move_q(self, x, c, a, q, k):
        return (x, c, a, q ^ k)

    def move_1(self, x, c, a, q, k):
        return (x ^ k, c, a, q) if (self.swap and c == 1) else (x, c, a ^ k, q)

    def move_2(self, x, c, a, q, k):
        return (x, c, a ^ k, q) if (self.swap and c == 1) else (x ^ k, c, a, q)

    def natural_rows(self, rows):
        me_dp, me_seq = lax.axis_index("dp"), lax.axis_index("seq")
        mx, mc = me_dp // 2, me_dp % 2
        m1, m0 = me_seq // self.s0, me_seq % self.s0
        minor = self.alt_minor or not self.swap
        ma, mq = (m0, m1) if minor else (m1, m0)
        at = jnp.arange(self.count * rows, dtype=jnp.int32)
        row, at = at % rows, at // rows
        kq, at = at % self.nq, at // self.nq
        k1, at = at % self.n1, at // self.n1
        k2, half = at % self.n2, at // self.n2
        core = mc ^ half
        turned = (core == 1) if self.swap else (core > 1)
        kx = jnp.where(turned, k1, k2)
        ka = jnp.where(turned, k2, k1)
        x, a, q = mx ^ kx, ma ^ ka, mq ^ kq
        s1, s0 = (q, a) if minor else (a, q)
        return (((x * 2 + core) * self.s1 + s1) * self.s0 + s0) * rows + row


def permute(array, pairs):
    return lax.ppermute(array, AXES, pairs)


def cat(*arrays):
    return jnp.concatenate(arrays, axis=0)


def after(array, *others):
    return lax.optimization_barrier((array,) + others)[0]


def fence(*arrays):
    return lax.optimization_barrier(arrays)


def spread_lanes(block):
    third = block.shape[1] // 3
    return cat(*[block[:, i * third : (i + 1) * third] for i in range(3)])


def close_lanes(block, rows):
    parts = block.reshape(-1, 3, rows, block.shape[1])
    return jnp.concatenate([parts[:, i] for i in range(3)], axis=-1).reshape(-1, 3 * block.shape[1])


def stage(array, pairs):
    return cat(array, *[permute(array, pairs[k]) for k in range(1, len(pairs))])


def add_parts(parts, dtype):
    total = parts[0].astype(F32)
    for part in parts[1:]:
        total = total + part.astype(F32)
    return total.astype(dtype)


def fold(array, pairs, dtype=None):
    count = len(pairs)
    rows = array.shape[0] // count
    parts = [array[:rows]]
    for k in range(1, count):
        parts.append(permute(array[k * rows : (k + 1) * rows], pairs[k]))
    return add_parts(parts, dtype or array.dtype)


def dot_nn(a, b):
    return jnp.dot(a, b, preferred_element_type=F32)


def dot_nt(a, b):
    return lax.dot_general(a, b, (((1,), (1,)), ((), ())), preferred_element_type=F32)


def dot_tn(a, b):
    return lax.dot_general(a, b, (((0,), (0,)), ((), ())), preferred_element_type=F32)


def gelu(v):
    return 0.5 * v * (1.0 + jnp.tanh(C0 * (v + C1 * v * v * v)))


def gelu_both(v):
    square = v * v
    t = jnp.tanh(C0 * (v + C1 * v * square))
    half = 0.5 * (1.0 + t)
    slope = half + 0.5 * v * (1.0 - t * t) * (C0 * (1.0 + 3.0 * C1 * square))
    return v * half, slope


def full_spec(shape):
    return pl.BlockSpec(shape, lambda *_: (0,) * len(shape))


COST = pl.CostEstimate(flops=1000, bytes_accessed=1000, transcendentals=0)
SCALARS = pl.BlockSpec(memory_space=pltpu.SMEM)
VMEM = pl.BlockSpec(memory_space=pltpu.VMEM)


def one_hot(left, right):
    return jnp.where(left == right, 1.0, 0.0).astype(BF)


def column(count):
    return lax.broadcasted_iota(jnp.int32, (count, 1), 0)


def lane(count):
    return lax.broadcasted_iota(jnp.int32, (1, count), 1)


GAIN, SHIFT, RATE, SCALE, SKIP = range(5)


def params_kernel(lanes, dims, key_ref, own_hbm, other_hbm, wr_ref, rows_ref, own, other, sem):
    width, chan = dims
    span = own.shape[1] // LAYERS
    half = own.shape[0]
    pull_own = pltpu.make_async_copy(own_hbm.at[:, pl.ds(lanes, LAYERS * span)], own, sem.at[0])
    pull_other = pltpu.make_async_copy(other_hbm.at[:, pl.ds(lanes, LAYERS * span)], other, sem.at[1])
    pull_own.start()
    pull_other.start()
    pull_own.wait()
    pull_other.wait()
    rows_ref[...] = jnp.zeros_like(rows_ref)
    turns = []
    for g in range(3):
        key = key_ref[...] - g * chan
        turns.append((one_hot(key[:, :half], column(chan)), one_hot(key[:, half:], column(chan))))
    even = one_hot(2 * column(chan), lane(width))
    odd = one_hot(2 * column(chan) + 1, lane(width))
    same = one_hot(column(chan), lane(chan))
    for layer in range(LAYERS):
        at = layer * span
        for g, (turn_own, turn_other) in enumerate(turns):
            part = dot_nn(turn_own, own[:, at : at + span]) + dot_nn(turn_other, other[:, at : at + span])
            part = part.astype(BF)
            low, high = g * span, min((g + 1) * span, width)
            wr_ref[layer, :, low:high] = part[:, : high - low]
        vec = part[:, width - 2 * span :]
        evens, odds = dot_tn(vec, even), dot_tn(vec, odd)
        turned = dot_tn(vec, same)
        rows_ref[layer, GAIN : GAIN + 1, :] = evens[0:1] + odds[1:2]
        rows_ref[layer, SHIFT : SHIFT + 1, :] = evens[2:3] + odds[3:4]
        for name, k in ((RATE, 4), (SCALE, 5), (SKIP, 6)):
            rows_ref[layer, name : name + 1, :chan] = turned[k : k + 1]


def params_call(key, own, other, lanes, width, chan):
    half = own.shape[0]
    span = (own.shape[1] - lanes) // LAYERS
    return pl.pallas_call(
        functools.partial(params_kernel, lanes, (width, chan)),
        out_shape=(
            jax.ShapeDtypeStruct((LAYERS, chan, width), BF),
            jax.ShapeDtypeStruct((LAYERS, 8, width), F32),
        ),
        in_specs=[VMEM, pl.BlockSpec(memory_space=pl.ANY), pl.BlockSpec(memory_space=pl.ANY)],
        out_specs=(VMEM,) * 2,
        scratch_shapes=[
            pltpu.VMEM((half, LAYERS * span), BF),
            pltpu.VMEM((half, LAYERS * span), BF),
            pltpu.SemaphoreType.DMA((2,)),
        ],
        compiler_params=pltpu.CompilerParams(vmem_limit_bytes=VMEM_LIMIT),
        cost_estimate=COST,
        name="params",
    )(key, own, other)


def enter_kernel(starts_n, layer, scal, x_ref, rows_ref, wr_ref, normed_ref, pre_ref, local_ref, last_ref):
    x = x_ref[...].astype(F32)
    centred = x - jnp.mean(x, axis=-1, keepdims=True)
    spread = jnp.mean(centred * centred, axis=-1, keepdims=True)
    gain, shift = rows_ref[layer, GAIN : GAIN + 1, :], rows_ref[layer, SHIFT : SHIFT + 1, :]
    normed = (centred * lax.rsqrt(spread + 1e-05) * gain + shift).astype(BF)
    normed_ref[...] = normed
    pre = dot_nt(normed, wr_ref[layer])
    pre_ref[...] = pre
    rows, chan = pre.shape
    rate = rows_ref[layer, RATE : RATE + 1, :chan]
    state = (1.0 - jnp.exp(-rate)) * gelu(pre)
    row = column(rows)
    k = 1
    while k < rows:
        open_rows = row >= k
        for s in range(starts_n):
            open_rows = open_rows & ~((row >= scal[s]) & (row < scal[s] + k))
        factor = jnp.where(open_rows, jnp.exp(-float(k) * rate), 0.0)
        state = state + factor * pltpu.roll(state, k, 0)
        k *= 2
    local_ref[...] = state
    last_ref[...] = state[rows - 1 :]


def enter_call(layer, starts, x, rows_all, wr_all):
    rows, width = x.shape
    chan = wr_all.shape[1]
    return pl.pallas_call(
        functools.partial(enter_kernel, starts.shape[0], layer),
        out_shape=(
            jax.ShapeDtypeStruct((rows, width), BF),
            jax.ShapeDtypeStruct((rows, chan), F32),
            jax.ShapeDtypeStruct((rows, chan), F32),
            jax.ShapeDtypeStruct((1, chan), F32),
        ),
        in_specs=[SCALARS] + [VMEM] * 3,
        out_specs=(VMEM,) * 4,
        compiler_params=pltpu.CompilerParams(vmem_limit_bytes=VMEM_LIMIT),
        cost_estimate=COST,
        name="enter",
    )(starts, x, rows_all, wr_all)


def mix_kernel(starts_n, layer, scal, hops_ref, lasts_ref, start_ref, rows_ref, pre_ref, local_ref, states_ref, in_ref, mixed_ref):
    rows, chan = pre_ref.shape
    rate = rows_ref[layer, RATE : RATE + 1, :chan]
    hops = hops_ref[...]
    weight = jnp.where(hops >= 0.0, jnp.exp(-jnp.maximum(hops, 0.0) * rate), 0.0)
    many = lasts_ref.shape[0]
    entered = jnp.sum(weight[:many] * lasts_ref[...], axis=0, keepdims=True) + weight[many:] * start_ref[...]
    in_ref[...] = entered
    row = column(rows)
    open_rows = row >= 0
    for s in range(starts_n):
        open_rows = open_rows & ~((row >= scal[s]) & (scal[s] >= 0))
    running = jnp.where(open_rows, jnp.exp(-(row + 1).astype(F32) * rate), 0.0)
    states = local_ref[...] + running * entered
    states_ref[...] = states
    scale, skip = rows_ref[layer, SCALE : SCALE + 1, :chan], rows_ref[layer, SKIP : SKIP + 1, :chan]
    mixed_ref[...] = (scale * states + skip * gelu(pre_ref[...])).astype(BF)


def mix_call(layer, starts, hops, lasts, start_state, rows_all, pre, local_states):
    rows, chan = pre.shape
    return pl.pallas_call(
        functools.partial(mix_kernel, starts.shape[0], layer),
        out_shape=(
            jax.ShapeDtypeStruct((rows, chan), F32),
            jax.ShapeDtypeStruct((1, chan), F32),
            jax.ShapeDtypeStruct((rows, chan), BF),
        ),
        in_specs=[SCALARS] + [VMEM] * 6,
        out_specs=(VMEM,) * 3,
        compiler_params=pltpu.CompilerParams(vmem_limit_bytes=VMEM_LIMIT),
        cost_estimate=COST,
        name="mix",
    )(starts, hops, lasts, start_state, rows_all, pre, local_states)


def back_scan_kernel(starts_n, layer, scal, dmix_ref, rows_ref, local_ref, first_ref):
    rows, chan = dmix_ref.shape
    rate = rows_ref[layer, RATE : RATE + 1, :chan]
    grad = rows_ref[layer, SCALE : SCALE + 1, :chan] * dmix_ref[...]
    row = column(rows)
    k = 1
    while k < rows:
        open_rows = row < rows - k
        for s in range(starts_n):
            open_rows = open_rows & ~((row < scal[s]) & (row >= scal[s] - k))
        factor = jnp.where(open_rows, jnp.exp(-float(k) * rate), 0.0)
        grad = grad + factor * pltpu.roll(grad, rows - k, 0)
        k *= 2
    local_ref[...] = grad
    keep = 1.0
    for s in range(starts_n):
        keep = jnp.where(scal[s] == 0, 0.0, keep)
    first_ref[...] = keep * jnp.exp(-rate) * grad[:1]


def back_scan_call(layer, starts, dmix, rows_all):
    rows, chan = dmix.shape
    return pl.pallas_call(
        functools.partial(back_scan_kernel, starts.shape[0], layer),
        out_shape=(jax.ShapeDtypeStruct((rows, chan), F32), jax.ShapeDtypeStruct((1, chan), F32)),
        in_specs=[SCALARS] + [VMEM] * 2,
        out_specs=(VMEM,) * 2,
        compiler_params=pltpu.CompilerParams(vmem_limit_bytes=VMEM_LIMIT),
        cost_estimate=COST,
        name="back_scan",
    )(starts, dmix, rows_all)


def leave_kernel(
    starts_n,
    layer,
    scal,
    hops_ref,
    firsts_ref,
    key_ref,
    key_col_ref,
    dmix_ref,
    local_ref,
    states_ref,
    in_ref,
    pre_ref,
    normed_ref,
    x_ref,
    rows_ref,
    wr_ref,
    dnorm_ref,
    up_ref,
    up_out_ref,
    low_ref,
    own_ref,
    other_ref,
    small,
):
    rows, chan = dmix_ref.shape
    width = x_ref.shape[1]
    rate = rows_ref[layer, RATE : RATE + 1, :chan]
    decay = jnp.exp(-rate)
    hops = hops_ref[...]
    weight = jnp.where(hops >= 0.0, jnp.exp(-jnp.maximum(hops, 0.0) * rate), 0.0)
    arriving = jnp.sum(weight * firsts_ref[...], axis=0, keepdims=True)
    dmix = dmix_ref[...]
    row = column(rows)
    later = row >= 0
    first = row < 0
    for s in range(starts_n):
        later = later & ~((row < scal[s]) & (scal[s] < rows))
        first = first | (row == scal[s])
    running = jnp.where(later, jnp.exp(-(rows - 1 - row).astype(F32) * rate), 0.0)
    grad = local_ref[...] + running * arriving
    reduced, slope = gelu_both(pre_ref[...])
    states = states_ref[...]
    before = jnp.where(row == 0, in_ref[...], pltpu.roll(states, 1, 0))
    before = jnp.where(first, 0.0, before)
    small[...] = jnp.zeros_like(small)
    small[4:5, :chan] = -decay * jnp.sum(grad * (before - reduced), axis=0, keepdims=True)
    small[5:6, :chan] = jnp.sum(dmix * states, axis=0, keepdims=True)
    small[6:7, :chan] = jnp.sum(dmix * reduced, axis=0, keepdims=True)
    d_reduced = (1.0 - decay) * grad + rows_ref[layer, SKIP : SKIP + 1, :chan] * dmix
    d_pre = (d_reduced * slope).astype(BF)
    d_normed = dnorm_ref[...] + dot_nn(d_pre, wr_ref[layer])
    x = x_ref[...].astype(F32)
    centred = x - jnp.mean(x, axis=-1, keepdims=True)
    spread = jnp.mean(centred * centred, axis=-1, keepdims=True)
    rs = lax.rsqrt(spread + 1e-05)
    xhat = centred * rs
    small[0:1, :] = jnp.sum(d_normed * xhat, axis=0, keepdims=True)
    small[2:3, :] = jnp.sum(d_normed, axis=0, keepdims=True)
    e = d_normed * rows_ref[layer, GAIN : GAIN + 1, :]
    mean_e = jnp.mean(e, axis=-1, keepdims=True)
    mean_ex = jnp.mean(e * xhat, axis=-1, keepdims=True)
    up = up_ref[...].astype(F32) + rs * (e - mean_e - xhat * mean_ex)
    up_out_ref[...] = up
    low_ref[...] = up.astype(BF)
    key = key_ref[...]
    turned = dot_nn(d_pre, one_hot(column(chan), key)).astype(BF)
    grads = dot_tn(turned, normed_ref[...]).astype(BF)
    vecs = small[...].astype(BF)
    key_col = key_col_ref[...]
    pick = column(small.shape[0])
    tail = jnp.zeros((chan, PAD), F32)
    for source, at, spot in ((vecs, 2 * key_col, (0, 2)), (vecs, 2 * key_col + 1, (1, 3))):
        wide = dot_nt(one_hot(at, lane(width)), source)
        tail += dot_nn(wide.astype(BF), one_hot(jnp.where(pick == 0, spot[0], jnp.where(pick == 2, spot[1], -1)), lane(PAD)))
    thin = dot_nt(one_hot(key_col, lane(chan)), vecs[:, :chan])
    tail += dot_nn(thin.astype(BF), one_hot(jnp.where((pick >= 4) & (pick < 7), pick, -1), lane(PAD)))
    half = chan // 2
    own_ref[:, :width] = grads[:half]
    other_ref[:, :width] = grads[half:]
    own_ref[:, width:] = tail[:half].astype(BF)
    other_ref[:, width:] = tail[half:].astype(BF)


def leave_call(layer, starts, hops, firsts, key, dmix, local_grad, kept, rows_all, wr_all, dnorm, up):
    rows, width = kept["stream"].shape
    chan = dmix.shape[1]
    head = jax.ShapeDtypeStruct((chan // 2, width + PAD), BF)
    return pl.pallas_call(
        functools.partial(leave_kernel, starts.shape[0], layer),
        out_shape=(
            jax.ShapeDtypeStruct((rows, width), F32),
            jax.ShapeDtypeStruct((rows, width), BF),
            head,
            head,
        ),
        in_specs=[SCALARS] + [VMEM] * 15,
        out_specs=(VMEM,) * 4,
        scratch_shapes=[pltpu.VMEM((16, width), F32)],
        compiler_params=pltpu.CompilerParams(vmem_limit_bytes=VMEM_LIMIT),
        cost_estimate=COST,
        name="leave",
    )(
        starts,
        hops,
        firsts,
        key.reshape(1, chan),
        key.reshape(chan, 1),
        dmix,
        local_grad,
        kept["states"],
        kept["state_in"],
        kept["pre_reduce"],
        kept["normed"],
        kept["stream"],
        rows_all,
        wr_all,
        dnorm,
        up,
    )


def spread_block(head, count, rows, block):
    at = block * count + column(count)
    slot, group, row = at // (3 * rows), (at // rows) % 3, at % rows
    span = head.shape[1] // 3
    total = None
    for g in range(3):
        source = jnp.where(group == g, slot * rows + row, -1)
        part = dot_nn(one_hot(source, lane(head.shape[0])), head[:, g * span : (g + 1) * span])
        total = part if total is None else total + part
    return total.astype(BF)


def wide_kernel(names, mode, blocks, dims, head_rows, *refs):
    r = dict(zip(names, refs), head_rows=head_rows)
    width, chan = dims
    step = pl.program_id(0)
    forward, backward = mode != "back", mode != "fore"
    pair = "other" in r
    weights = r["weights"] if pair else r["own"]

    @pl.when(step == 0)
    def _():
        if forward:
            r["acc"][...] = r["base"][...].astype(F32)
        if backward:
            r["d_normed"][...] = r["d_normed_in"][...] if "d_normed_in" in r else jnp.zeros_like(r["d_normed"])
            r["d_mixed"][...] = r["d_mixed_in"][...] if "d_mixed_in" in r else jnp.zeros_like(r["d_mixed"])

    if pair:

        @pl.when(step < blocks)
        def _():
            weights[...] = r["own"][...]

        @pl.when(step >= blocks)
        def _():
            weights[...] = r["other"][...]

    normed, mixed = r["normed"][...], r["mixed"][...]
    if forward:
        pre = dot_nt(normed, weights[:, :width])
        expanded = dot_nt(mixed, weights[:, 2 * width :])
        if mode == "fore":
            r["pre"][...] = pre
            r["expanded"][...] = expanded
    else:
        pre, expanded = r["pre"][...], r["expanded"][...]
    if backward:
        gate, slope = gelu_both(pre)
    else:
        gate = gelu(pre)
    joined = (expanded * gate).astype(BF)
    if forward:
        r["acc"][...] += dot_nn(joined, weights[:, width : 2 * width])
    if backward:
        low = r["low"][...]
        d_joined = dot_nt(low, weights[:, width : 2 * width])
        d_expanded = (d_joined * gate).astype(BF)
        d_pre = (d_joined * expanded * slope).astype(BF)
        r["d_mixed"][...] += dot_nn(d_expanded, weights[:, 2 * width :])
        r["d_normed"][...] += dot_nn(d_pre, weights[:, :width])

        def store(out):
            out[:, :width] = dot_tn(d_pre, normed).astype(BF)
            out[:, width : 2 * width] = dot_tn(joined, low).astype(BF)
            out[:, 2 * width :] = dot_tn(d_expanded, mixed).astype(BF)

        if not pair:
            store(r["grad_own"])
        else:
            grads = r["grads"]
            store(grads)
            lanes = 2 * width + chan

            def put(out, head):
                out[:, :lanes] = grads[...]
                if head in r:
                    out[:, lanes:] = spread_block(r[head], out.shape[0], r["head_rows"], step % blocks)

            @pl.when(step < blocks)
            def _():
                put(r["grad_own"], "head_own")

            @pl.when(step >= blocks)
            def _():
                put(r["grad_other"], "head_other")

    if "out" in r:

        @pl.when(step == pl.num_programs(0) - 1)
        def _():
            r["out"][...] = r["acc"][...].astype(r["out"].dtype)


def wide_call(mode, own, other, normed, mixed, base=None, low=None, pre=None, expanded=None, sums=None, heads=None, head_rows=0, out_dtype=None):
    rows, width = normed.shape
    chan = mixed.shape[1]
    span = own.shape[0]
    pair = other is not None
    block = span // 2 if pair else span // 4
    blocks = span // block
    steps = blocks * (2 if pair else 1)
    lanes = 2 * width + chan
    forward, backward = mode != "back", mode != "fore"
    ins, outs, scratch = [], [], []

    def half_spec(which, count):
        if which == "own":
            return pl.BlockSpec((block, count), lambda i: (jnp.minimum(i, blocks - 1), 0))
        return pl.BlockSpec((block, count), lambda i: (jnp.maximum(i - blocks, 0), 0))

    ins.append(("own", own, half_spec("own", lanes)))
    more = 0
    if pair:
        ins.append(("other", other, half_spec("other", lanes)))
    if heads is not None:
        more = heads[0].shape[1] // 3
        ins.append(("head_own", heads[0], full_spec(heads[0].shape)))
        ins.append(("head_other", heads[1], full_spec(heads[1].shape)))
    ins.append(("normed", normed, full_spec(normed.shape)))
    ins.append(("mixed", mixed, full_spec(mixed.shape)))
    saved = pl.BlockSpec((rows, block), lambda i: (0, i))
    saved_shape = jax.ShapeDtypeStruct((rows, steps * block), F32)
    if forward:
        ins.append(("base", base, full_spec(base.shape)))
    if backward:
        ins.append(("low", low, full_spec(low.shape)))
        if sums is not None:
            ins.append(("d_normed_in", sums[0], full_spec(sums[0].shape)))
            ins.append(("d_mixed_in", sums[1], full_spec(sums[1].shape)))
    if mode == "back":
        ins.append(("pre", pre, saved))
        ins.append(("expanded", expanded, saved))
    if mode == "fore":
        outs.append(("pre", saved_shape, saved))
        outs.append(("expanded", saved_shape, saved))
    if forward:
        if out_dtype == F32:
            outs.append(("acc", jax.ShapeDtypeStruct((rows, width), F32), full_spec((rows, width))))
        else:
            outs.append(("out", jax.ShapeDtypeStruct((rows, width), out_dtype), full_spec((rows, width))))
            scratch.append(("acc", pltpu.VMEM((rows, width), F32)))
    if backward:
        outs.append(("d_normed", jax.ShapeDtypeStruct((rows, width), F32), full_spec((rows, width))))
        outs.append(("d_mixed", jax.ShapeDtypeStruct((rows, chan), F32), full_spec((rows, chan))))
        grad = jax.ShapeDtypeStruct((span, lanes + more), BF)
        outs.append(("grad_own", grad, half_spec("own", lanes + more)))
        if pair:
            outs.append(("grad_other", grad, half_spec("other", lanes + more)))
            scratch.append(("grads", pltpu.VMEM((block, lanes), BF)))
    if pair:
        scratch.append(("weights", pltpu.VMEM((block, lanes), BF)))
    names = [name for name, _, _ in ins + outs] + [name for name, _ in scratch]
    return pl.pallas_call(
        functools.partial(wide_kernel, names, mode, blocks, (width, chan), head_rows),
        grid=(steps,),
        out_shape=tuple(shape for _, shape, _ in outs),
        in_specs=[spec for _, _, spec in ins],
        out_specs=tuple(spec for _, _, spec in outs),
        scratch_shapes=[shape for _, shape in scratch],
        compiler_params=pltpu.CompilerParams(vmem_limit_bytes=VMEM_LIMIT),
        cost_estimate=COST,
        name="wide_" + mode,
    )(*[array for _, array, _ in ins])


def seq_gather(lay, vector):
    held, k = vector, 1
    while k < lay.seq:
        pairs = [
            (d * lay.seq + s, d * lay.seq + (s ^ k)) for d in range(lay.dp) for s in range(lay.seq)
        ]
        held = cat(held, permute(held, pairs))
        k *= 2
    return held


def hops_forward(lay, starts, rows):
    me = lax.axis_index("seq")
    source = jnp.concatenate([me ^ jnp.arange(lay.seq, dtype=jnp.int32), jnp.full((1,), -1, jnp.int32)])
    hops = me - 1 - source
    low, high = (source + 1) * rows, me * rows
    hit = jnp.any((starts[None, :] >= low[:, None]) & (starts[None, :] < high), axis=1)
    return jnp.where((hops >= 0) & ~hit, (hops * rows).astype(F32), -1.0)[:, None]


def hops_backward(lay, starts, rows):
    me = lax.axis_index("seq")
    source = me ^ jnp.arange(lay.seq, dtype=jnp.int32)
    hops = source - me - 1
    low, high = (me + 1) * rows, source * rows
    hit = jnp.any((starts[None, :] >= low) & (starts[None, :] < high[:, None]), axis=1)
    return jnp.where((hops >= 0) & ~hit, (hops * rows).astype(F32), -1.0)[:, None]


def local(
    lay,
    tokens,
    ln_gain,
    ln_shift,
    w_gate,
    w_reduce,
    decay_rate,
    state_scale,
    skip_scale,
    w_expand,
    w_out,
    prev_state,
    item_lengths,
    cotangent,
):
    rows, width = tokens.shape
    chan = w_expand.shape[1]
    small_rows = w_reduce.shape[2]
    ff_rows = w_gate.shape[2]
    job_rows = ff_rows // JOBS
    me_seq = lax.axis_index("seq")
    starts = jnp.cumsum(item_lengths[0])[:-1].astype(jnp.int32)
    near = starts - me_seq * rows
    hops_fore, hops_back = hops_forward(lay, starts, rows), hops_backward(lay, starts, rows)

    def vectors(layer):
        return jnp.concatenate(
            [
                ln_gain[layer].reshape(small_rows, 2),
                ln_shift[layer].reshape(small_rows, 2),
                decay_rate[layer][:, None],
                state_scale[layer][:, None],
                skip_scale[layer][:, None],
                jnp.zeros((small_rows, PAD - SMALL), BF),
            ],
            axis=1,
        )

    heads = [jnp.concatenate([w_reduce[i].T, vectors(i)], axis=1) for i in range(LAYERS)]
    bundles = [
        jnp.concatenate([w_gate[i].T, w_out[i], w_expand[i].T], axis=1).reshape(JOBS, job_rows, -1)
        for i in range(LAYERS)
    ]
    nature = lay.natural_rows(small_rows)
    lanes = bundles[0].shape[2]
    group = jnp.arange(3, dtype=jnp.int32)[None, :, None] * chan
    key = (nature.reshape(lay.count, 1, small_rows) + group).reshape(1, -1)

    def relative_order(gathered):
        order = lay.natural_rows(1)
        half = lay.count // 2
        return [
            gathered.at[at].get(mode="promise_in_bounds", unique_indices=True).reshape(half * job_rows, -1)
            for at in (order[:half], order[half:])
        ]

    first = jnp.concatenate([bundles[0][0]] + [spread_lanes(h) for h in heads], axis=1)
    third = bundles[0][1]
    gathered_a = lax.all_gather(bundles[1][0], AXES, axis=0)
    gathered_b = lax.all_gather(after(bundles[1][1], gathered_a), AXES, axis=0, tiled=True)

    line_a = stage(first, lay.q)
    line_a, third = fence(line_a, third)
    plane_a = stage(line_a, lay.p1)
    cut = max(1, (lay.nq * 2) // 3) + 1
    early = [permute(third, lay.q[k]) for k in range(1, cut)]
    plane_a, third, *early = fence(plane_a, third, *early)
    a_own = stage(plane_a, lay.p2)
    line_b = cat(third, *early, *[permute(third, lay.q[k]) for k in range(cut, lay.nq)])
    a_own, line_b = fence(a_own, line_b)
    a_other = permute(a_own, lay.core)
    plane_b = stage(line_b, lay.p1)
    a_own, a_other, plane_b, gathered_a = fence(a_own, a_other, plane_b, gathered_a)
    b_own = stage(plane_b, lay.p2)
    wr_all, rows_all = params_call(key, a_own, a_other, lanes, width, chan)

    def enter(layer, stream):
        normed, pre_reduce, local_states, last = enter_call(layer, near, stream, rows_all, wr_all)
        lasts = seq_gather(lay, last)
        states, state_in, mixed = mix_call(
            layer, near, hops_fore, lasts, prev_state[layer], rows_all, pre_reduce, local_states
        )
        return dict(stream=stream, normed=normed, pre_reduce=pre_reduce, states=states, state_in=state_in, mixed=mixed)

    def leave(layer, kept, sums, upstream):
        d_normed, d_mixed = sums
        back_local, first_row = back_scan_call(layer, near, d_mixed, rows_all)
        firsts = seq_gather(lay, first_row)
        upstream, low, *head = leave_call(
            layer, near, hops_back, firsts, nature, d_mixed, back_local, kept, rows_all, wr_all, d_normed, upstream
        )
        return upstream, low, head

    k0 = enter(0, tokens)
    top_a = relative_order(gathered_a)
    b_own, k0["mixed"], *top_a = fence(b_own, k0["mixed"], *top_a)
    b_other = permute(b_own, lay.core)
    pre_a, exp_a, acc = wide_call("fore", a_own, a_other, k0["normed"], k0["mixed"], base=tokens, out_dtype=F32)
    b_own, b_other, acc = fence(b_own, b_other, acc)
    pre_b, exp_b, acc = wide_call("fore", b_own, b_other, k0["normed"], k0["mixed"], base=acc, out_dtype=F32)

    k1 = enter(1, acc)
    acc, d_normed, d_mixed, a1_own, a1_other = wide_call(
        "both", *top_a, k1["normed"], k1["mixed"], base=k1["stream"], low=cotangent, out_dtype=F32
    )
    acc, d_normed, d_mixed, a1_own, a1_other = fence(acc, d_normed, d_mixed, a1_own, a1_other)
    a1 = add_parts([a1_own, permute(a1_other, lay.core)], BF)
    output, d_normed, d_mixed, b1 = wide_call(
        "both",
        gathered_b,
        None,
        k1["normed"],
        k1["mixed"],
        base=acc,
        low=cotangent,
        sums=(d_normed, d_mixed),
        out_dtype=BF,
    )
    a1, d_normed, d_mixed, b1 = fence(a1, d_normed, d_mixed, b1)
    b1_done = lax.psum_scatter(b1, AXES, scatter_dimension=0, tiled=True)

    a1 = fold(a1, lay.p2)
    upstream, low, head_1 = leave(1, k1, (d_normed, d_mixed), cotangent)
    a1, low, upstream, *head_1 = fence(a1, low, upstream, *head_1)

    a1 = fold(a1, lay.p1)
    d_normed, d_mixed, a0_own, a0_other = wide_call(
        "back",
        a_own,
        a_other,
        k0["normed"],
        k0["mixed"],
        low=low,
        pre=pre_a,
        expanded=exp_a,
        heads=head_1,
        head_rows=small_rows,
    )
    a1, d_normed, d_mixed, a0_own, a0_other = fence(a1, d_normed, d_mixed, a0_own, a0_other)

    a1_done = fold(a1, lay.q, F32)
    a0 = add_parts([a0_own, permute(a0_other, lay.core)], BF)
    d_normed, d_mixed, b0_own, b0_other = wide_call(
        "back",
        b_own,
        b_other,
        k0["normed"],
        k0["mixed"],
        low=low,
        pre=pre_b,
        expanded=exp_b,
        sums=(d_normed, d_mixed),
    )
    a1_done, a0, d_normed, d_mixed, b0_own, b0_other = fence(a1_done, a0, d_normed, d_mixed, b0_own, b0_other)

    b0 = add_parts([b0_own, permute(b0_other, lay.core)], BF)
    a0 = fold(a0, lay.p2)
    _, input_grad, (head_own, head_other) = leave(0, k0, (d_normed, d_mixed), upstream)
    a0, b0, head_own, head_other = fence(a0, b0, head_own, head_other)

    a0 = fold(a0, lay.p1)
    b0 = fold(b0, lay.p2)
    h0 = fold(add_parts([head_own, permute(head_other, lay.core)], BF), lay.p2)
    a0, b0, h0, b1_done = fence(a0, b0, h0, b1_done)

    a0_done = fold(a0, lay.q, F32)
    b0 = fold(b0, lay.p1)
    h0 = fold(h0, lay.p1)
    a0_done, b0, h0 = fence(a0_done, b0, h0)
    b0_done = fold(b0, lay.q, F32)
    h0_done = fold(h0, lay.q, F32)

    h1_done = close_lanes(a0_done[:, lanes:], small_rows)
    b1_done = b1_done.astype(F32)
    grads = [cat(a0_done[:, :lanes], b0_done), cat(a1_done, b1_done)]
    heads_done = [h0_done, h1_done]
    vecs = [h[:, width : width + SMALL] for h in heads_done]
    return (
        output,
        input_grad,
        jnp.stack([v[:, 0:2].reshape(-1) for v in vecs]),
        jnp.stack([v[:, 2:4].reshape(-1) for v in vecs]),
        jnp.stack([g[:, :width].T for g in grads]),
        jnp.stack([h[:, :width].T for h in heads_done]),
        jnp.stack([v[:, 4] for v in vecs]),
        jnp.stack([v[:, 5] for v in vecs]),
        jnp.stack([v[:, 6] for v in vecs]),
        jnp.stack([g[:, 2 * width :].T for g in grads]),
        jnp.stack([g[:, width : 2 * width] for g in grads]),
    )


def solution(mesh):
    lay = Layout(mesh)
    both = ("dp", "seq")
    return jax.shard_map(
        functools.partial(local, lay),
        mesh=mesh,
        in_specs=(
            P(both, None),
            P(None, both),
            P(None, both),
            P(None, None, both),
            P(None, None, both),
            P(None, both),
            P(None, both),
            P(None, both),
            P(None, None, both),
            P(None, both, None),
            P(None, "dp", None),
            P("dp", None),
            P(both, None),
        ),
        out_specs=(
            P(both, None),
            P(both, None),
            P(None, both),
            P(None, both),
            P(None, None, both),
            P(None, None, both),
            P(None, both),
            P(None, both),
            P(None, both),
            P(None, None, both),
            P(None, both, None),
        ),
        check_vma=False,
    )
```

time: 698 us -> 596 us (0.85)
  waiting for transfers between devices: 310 us -> 232 us
  local copies, waits for them, and re-layouts: 64.3 us -> 28.8 us
  Pallas kernels: 160 us -> 181 us
  starting transfers between devices: 102 us -> 84.3 us
  other arithmetic: 38.7 us -> 50.4 us
  between operations: 3.26 us -> 14.9 us
  matrix products: 10.1 us -> 0 us
    ppermute x78 -> x48, waiting for transfers between devices: 310 us -> 232 us  [permute(): return lax.ppermute(array, AXES, pairs)]
    pallas_call x6 -> x9, Pallas kernels: 46.7 us -> 66.8 us  [the longest x2 22.8 us: leave_call(): pl.pallas_call(functools.partial(leave_kernel, starts.shape[0], layer), o...]
    ppermute x78 -> x48, starting transfers between devices: 102 us -> 83.6 us  [permute(): return lax.ppermute(array, AXES, pairs)]
    concatenate x12 -> x1, local copies, waits for them, and re-layouts: 18.1 us -> 0.1 us  [hops_forward(): jnp.concatenate([me ^ jnp.arange(lay.seq, dtype=jnp.int32), jnp.full((1,)...]
    concatenate x10 -> x18, other arithmetic: 0.16 us -> 17.4 us  [cat(): return jnp.concatenate(arrays, axis=0)]
    unnamed x90 -> x50, local copies, waits for them, and re-layouts: 18.7 us -> 3.35 us
    gather x0 -> x2, local copies, waits for them, and re-layouts: none -> 12.1 us  [relative_order(): gathered.at[at].get(mode='promise_in_bounds', unique_indices=True)]
    dot_general x4 -> x0, matrix products: 10.1 us -> none  [the longest x2 8.36 us: leave(): moved = jnp.dot(turn.astype(F32).T, bundle, precision=lax.Precision.HIGHEST)]
  transfers between devices with their start and end apart: 78 -> 51, of which waited for: 45 -> 30; matrix products, arithmetic and copies ran while one was open for 15% -> 10% of each run, Pallas kernels for 10% -> 27%
where the time goes in v2:
time: 596 us; the launch traced here: 592 us
  waiting for transfers between devices  232 us (39%)
  Pallas kernels  181 us (30%)
  starting transfers between devices  84.3 us (14%)
  other arithmetic  50.4 us (8%)
  local copies, waits for them, and re-layouts  28.8 us (5%)
  between operations  14.9 us (2%)
    ppermute x48, waiting for transfers between devices, permute(): return lax.ppermute(array, AXES, pairs)  232 us
    pallas_call x6, Pallas kernels, wide_call(): pl.pallas_call(functools.partial(wide_kernel, names, mode, blocks, (width...  115 us
    ppermute x48, starting transfers between devices, permute(): return lax.ppermute(array, AXES, pairs)  83.6 us
    pallas_call x2, Pallas kernels, leave_call(): pl.pallas_call(functools.partial(leave_kernel, starts.shape[0], layer), o...  22.8 us
    convert_element_type x12, other arithmetic, add_parts(): return total.astype(dtype)  17.7 us
    concatenate x18, other arithmetic, cat(): return jnp.concatenate(arrays, axis=0)  17.4 us
    pallas_call x2, Pallas kernels, enter_call(): pl.pallas_call(functools.partial(enter_kernel, starts.shape[0], layer), o...  14.1 us
    gather x2, local copies, waits for them, and re-layouts, relative_order(): gathered.at[at].get(mode='promise_in_bounds', unique_indices=True)  12.1 us
  transfers between devices with their start and end apart: 51, of which 30 were waited for; matrix products, arithmetic and copies ran while one was open for 10% of the time, Pallas kernels for 27%

profile of v2, /device:TPU:8, one launch (start us, length us, event | category | flops | bytes accessed | tf_op | source)
XLA Modules:
  0.0 591.9 jit_solution(5219478873777492155)
XLA Ops:
  16.3 11.1 %collective-permute-done = bf16[48,3328]{1,0:T(8,128)(2,1)S(1)} collective-permute-done((bf16[48,3328]{1,0:T(8,128)(2,1)S(1)}, bf16[48,3328]{1,0:T(8,128)(2,1)S(1)}, u32[]{:S(2)}, u32[]{:S(2)}) %collective-permute-start) | collective-permute-done | bytes 319520 | tf_op jit(solution)/shard_map/ppermute | solution.py:81
  27.4 13.8 %collective-permute-done.1 = bf16[48,3328]{1,0:T(8,128)(2,1)S(1)} collective-permute-done((bf16[48,3328]{1,0:T(8,128)(2,1)S(1)}, bf16[48,3328]{1,0:T(8,128)(2,1)S(1)}, u32[]{:S(2)}, u32[]{:S(2)}) %collective-permute-start.1) | collective-permute-done | bytes 319520 | tf_op jit(solution)/shard_map/ppermute | solution.py:81
  41.2 7.9 %collective-permute-done.2 = bf16[48,3328]{1,0:T(8,128)(2,1)S(1)} collective-permute-done((bf16[48,3328]{1,0:T(8,128)(2,1)S(1)}, bf16[48,3328]{1,0:T(8,128)(2,1)S(1)}, u32[]{:S(2)}, u32[]{:S(2)}) %collective-permute-start.2) | collective-permute-done | bytes 319520 | tf_op jit(solution)/shard_map/ppermute | solution.py:81
  54.6 16.2 %collective-permute-done.3 = bf16[192,3328]{1,0:T(8,128)(2,1)S(1)} collective-permute-done((bf16[192,3328]{1,0:T(8,128)(2,1)S(1)}, bf16[192,3328]{1,0:T(8,128)(2,1)S(1)}, u32[]{:S(2)}, u32[]{:S(2)}) %collective-permute-start.3) | collective-permute-done | bytes 1277984 | tf_op jit(solution)/shard_map/ppermute | solution.py:81
  77.2 11.5 %collective-permute-done.7 = bf16[48,2560]{1,0:T(8,128)(2,1)S(1)} collective-permute-done((bf16[48,2560]{1,0:T(8,128)(2,1)S(1)}, bf16[48,2560]{1,0:T(8,128)(2,1)S(1)}, u32[]{:S(2)}, u32[]{:S(2)}) %collective-permute-start.7) | collective-permute-done | bytes 245792 | tf_op jit(solution)/shard_map/ppermute | solution.py:81
  88.7 31.4 %collective-permute-done.6 = bf16[384,3328]{1,0:T(8,128)(2,1)S(1)} collective-permute-done((bf16[384,3328]{1,0:T(8,128)(2,1)S(1)}, bf16[384,3328]{1,0:T(8,128)(2,1)S(1)}, u32[]{:S(2)}, u32[]{:S(2)}) %collective-permute-start.6) | collective-permute-done | bytes 2555936 | tf_op jit(solution)/shard_map/ppermute | solution.py:81
  126.4 12.3 %collective-permute-done.9 = bf16[192,2560]{1,0:T(8,128)(2,1)} collective-permute-done((bf16[192,2560]{1,0:T(8,128)(2,1)S(1)}, bf16[192,2560]{1,0:T(8,128)(2,1)}, u32[]{:S(2)}, u32[]{:S(2)}) %collective-permute-start.9) | collective-permute-done | bytes 983072 | tf_op jit(solution)/shard_map/ppermute | solution.py:81
  145.0 9.6 %params.1 = (bf16[2,512,1024]{2,1,0:T(8,128)(2,1)}, f32[2,8,1024]{2,1,0:T(8,128)}) custom-call(s32[1,1536]{1,0:T(1,128)} %add.494.key_ref, bf16[768,3328]{1,0:T(8,128)(2,1)} %pad_maximum_fusion.own_hbm.refs_0_, bf16[768,3328]{1,0:T(8,128)(2,1)} %collective-permute-done.8.other_hbm.refs_1_), custom_call_target="tpu_custom_call" | custom-call | flops 1000 | bytes 1000 | tf_op jit(solution)/shard_map/params/pallas_call | solution.py:211
  196.4 11.2 %wide_fore.2 = (f32[512,1536]{1,0:T(8,128)}, f32[512,1536]{1,0:T(8,128)}, f32[512,1024]{1,0:T(8,128)}) custom-call(bf16[768,3328]{1,0:T(8,128)(2,1)} %pad_maximum_fusion.own_hbm.refs_0_, bf16[768,3328]{1,0:T(8,128)(2,1)} %collective-permute-done.8.other_hbm.refs_1_, bf16[512,1024]{1,0:T(8,128)(2,1)} %get-tuple-element.132.refs_2_.refs_4_.normed_ref, ...), custom_call_target="tpu_custom_call" | custom-call | flops 1000 | bytes 1000 | tf_op jit(solution)/shard_map/wide_fore/pallas_call | solution.py:618
  207.6 11.6 %wide_fore.3 = (f32[512,1536]{1,0:T(8,128)}, f32[512,1536]{1,0:T(8,128)}, f32[512,1024]{1,0:T(8,128)}) custom-call(bf16[768,2560]{1,0:T(8,128)(2,1)} %copy-done, bf16[768,2560]{1,0:T(8,128)(2,1)} %collective-permute-done.14.refs_1_, bf16[512,1024]{1,0:T(8,128)(2,1)} %get-tuple-element.132.refs_2_.refs_4_.normed_ref, ...), custom_call_target="tpu_custom_call" | custom-call | flops 1000 | bytes 1000 | tf_op jit(solution)/shard_map/wide_fore/pallas_call | solution.py:618
  219.3 7.2 %enter.3 = (bf16[512,1024]{1,0:T(8,128)(2,1)}, f32[512,512]{1,0:T(8,128)}, f32[512,512]{1,0:T(8,128)}, f32[1,512]{1,0:T(1,128)}) custom-call(s32[3]{0:T(128)} %broadcast_subtract_fusion.scal, f32[512,1024]{1,0:T(8,128)} %get-tuple-element.138.x_ref.refs_4_, f32[2,8,1024]{2,1,0:T(8,128)} %get-tuple-element.124.rows_ref, ...), custom_call_target="tpu_custom_call" | custom-call | flops 1000 | bytes 1000 | tf_op jit(solution)/shard_map/enter/pallas_call | solution.py:258
  245.2 24.8 %wide_both.2 = (f32[512,1024]{1,0:T(8,128)}, f32[512,1024]{1,0:T(8,128)}, f32[512,512]{1,0:T(8,128)}, bf16[768,2560]{1,0:T(8,128)(2,1)}, bf16[768,2560]{1,0:T(8,128)(2,1)}) custom-call(bf16[768,2560]{1,0:T(8,128)(2,1)} %bitcast.105, bf16[768,2560]{1,0:T(8,128)(2,1)} %bitcast.106, bf16[512,1024]{1,0:T(8,128)(2,1)} %get-tuple-element.139.refs_2_.refs_1_.normed_ref, ...), custom_call_target="tpu_custom_call" | custom-call | flops 1000 | bytes 1000 | tf_op jit(solution)/shard_map/wide_both/pallas_call | solution.py:618
  282.1 23.5 %wide_both.3 = (bf16[512,1024]{1,0:T(8,128)(2,1)}, f32[512,1024]{1,0:T(8,128)}, f32[512,512]{1,0:T(8,128)}, bf16[1536,2560]{1,0:T(8,128)(2,1)}) custom-call(bf16[1536,2560]{1,0:T(8,128)(2,1)} %all-gather.4.cloned.1.call-done.refs_0_, bf16[512,1024]{1,0:T(8,128)(2,1)} %get-tuple-element.139.refs_2_.refs_1_.normed_ref, ...), custom_call_target="tpu_custom_call" | custom-call | flops 1000 | bytes 1000 | tf_op jit(solution)/shard_map/wide_both/pallas_call | solution.py:618
  331.2 11.4 %leave.2 = (f32[512,1024]{1,0:T(8,128)}, bf16[512,1024]{1,0:T(8,128)(2,1)}, bf16[256,1152]{1,0:T(8,128)(2,1)}, bf16[256,1152]{1,0:T(8,128)(2,1)}) custom-call(s32[3]{0:T(128)} %broadcast_subtract_fusion.scal, f32[8,1]{1,0:T(8,128)} %convert_select_fusion.1.hops_ref, f32[8,512]{1,0:T(8,128)} %pad_maximum_fusion.16.firsts_ref, s32[1,512]{1,0:T(1,128)} %fusion.52.key_ref, ...), custom_call_target="tpu_custom_call" | custom-call | flops 1000 | bytes 1000 | tf_op jit(solution)/shard_map/leave/pallas_call | solution.py:431
  347.8 23.0 %wide_back.2 = (f32[512,1024]{1,0:T(8,128)}, f32[512,512]{1,0:T(8,128)}, bf16[768,2944]{1,0:T(8,128)(2,1)}, bf16[768,2944]{1,0:T(8,128)(2,1)}) custom-call(bf16[768,3328]{1,0:T(8,128)(2,1)} %pad_maximum_fusion.own_hbm.refs_0_, bf16[768,3328]{1,0:T(8,128)(2,1)} %collective-permute-done.8.other_hbm.refs_1_, bf16[256,1152]{1,0:T(8,128)(2,1)} %get-tuple-element.167.refs_2_, ...), custom_call_target="tpu_custom_call" | custom-call | flops 1000 | bytes 1000 | tf_op jit(solution)/shard_map/wide_back/pallas_call | solution.py:618
  371.0 10.0 %collective-permute-start.27 = (bf16[768,2944]{1,0:T(8,128)(2,1)}, bf16[768,2944]{1,0:T(8,128)(2,1)}, u32[]{:S(2)}, u32[]{:S(2)}) collective-permute-start(bf16[768,2944]{1,0:T(8,128)(2,1)} %get-tuple-element.178), channel_id=1, source_target_pairs={{0,8},{2,10},{4,12},{6,14},{1,9},{3,11},{5,13},{7,15},{8,0},{10,2}... | collective-permute-start | bytes 13565960 | tf_op jit(solution)/shard_map/ppermute | solution.py:81
  384.6 20.5 %wide_back.3 = (f32[512,1024]{1,0:T(8,128)}, f32[512,512]{1,0:T(8,128)}, bf16[768,2560]{1,0:T(8,128)(2,1)}, bf16[768,2560]{1,0:T(8,128)(2,1)}) custom-call(bf16[768,2560]{1,0:T(8,128)(2,1)} %copy-done, bf16[768,2560]{1,0:T(8,128)(2,1)} %collective-permute-done.14.refs_1_, bf16[512,1024]{1,0:T(8,128)(2,1)} %get-tuple-element.132.refs_2_.refs_4_.normed_ref, ...), custom_call_target="tpu_custom_call" | custom-call | flops 1000 | bytes 1000 | tf_op jit(solution)/shard_map/wide_back/pallas_call | solution.py:618
  436.7 11.4 %leave.3 = (f32[512,1024]{1,0:T(8,128)}, bf16[512,1024]{1,0:T(8,128)(2,1)}, bf16[256,1152]{1,0:T(8,128)(2,1)}, bf16[256,1152]{1,0:T(8,128)(2,1)}) custom-call(s32[3]{0:T(128)} %broadcast_subtract_fusion.scal, f32[8,1]{1,0:T(8,128)} %convert_select_fusion.1.hops_ref, f32[8,512]{1,0:T(8,128)} %pad_maximum_fusion.17.firsts_ref, s32[1,512]{1,0:T(1,128)} %fusion.52.key_ref, ...), custom_call_target="tpu_custom_call" | custom-call | flops 1000 | bytes 1000 | tf_op jit(solution)/shard_map/leave/pallas_call | solution.py:431
  448.1 7.5 %collective-permute-done.31 = bf16[384,2944]{1,0:T(8,128)(2,1)} collective-permute-done((bf16[384,2944]{1,0:T(8,128)(2,1)}, bf16[384,2944]{1,0:T(8,128)(2,1)}, u32[]{:S(2)}, u32[]{:S(2)}) %collective-permute-start.31) | collective-permute-done | bytes 2261024 | tf_op jit(solution)/shard_map/ppermute | solution.py:81
  459.8 17.1 %collective-permute-start.35 = (bf16[256,1152]{1,0:T(8,128)(2,1)S(1)}, bf16[256,1152]{1,0:T(8,128)(2,1)S(1)}, u32[]{:S(2)}, u32[]{:S(2)}) collective-permute-start(bf16[256,1152]{1,0:T(8,128)(2,1)S(1)} %copy-done.23), channel_id=1, source_target_pairs={{0,8},{2,10},{4,12},{6,14},{1,9},{3,11},{5,13},{7,15},{8,0},{10,2}... | collective-permute-start | bytes 1769480 | tf_op jit(solution)/shard_map/ppermute | solution.py:81
  482.0 37.4 %collective-permute-done.36 = bf16[128,1152]{1,0:T(8,128)(2,1)S(1)} collective-permute-done((bf16[128,1152]{1,0:T(8,128)(2,1)S(1)}, bf16[128,1152]{1,0:T(8,128)(2,1)S(1)}, u32[]{:S(2)}, u32[]{:S(2)}) %collective-permute-start.36) | collective-permute-done | bytes 294944 | tf_op jit(solution)/shard_map/ppermute | solution.py:81
  527.8 8.1 %collective-permute-done.37 = bf16[48,2944]{1,0:T(8,128)(2,1)S(1)} collective-permute-done((bf16[48,2944]{1,0:T(8,128)(2,1)S(1)}, bf16[48,2944]{1,0:T(8,128)(2,1)S(1)}, u32[]{:S(2)}, u32[]{:S(2)}) %collective-permute-start.37) | collective-permute-done | bytes 282656 | tf_op jit(solution)/shard_map/ppermute | solution.py:81
  537.5 12.9 %collective-permute-done.39 = bf16[48,2944]{1,0:T(8,128)(2,1)S(1)} collective-permute-done((bf16[48,2944]{1,0:T(8,128)(2,1)S(1)}, bf16[48,2944]{1,0:T(8,128)(2,1)S(1)}, u32[]{:S(2)}, u32[]{:S(2)}) %collective-permute-start.39) | collective-permute-done | bytes 282656 | tf_op jit(solution)/shard_map/ppermute | solution.py:81
  568.2 7.2 %collective-permute-done.46 = bf16[48,2560]{1,0:T(8,128)(2,1)} collective-permute-done((bf16[48,2560]{1,0:T(8,128)(2,1)S(1)}, bf16[48,2560]{1,0:T(8,128)(2,1)}, u32[]{:S(2)}, u32[]{:S(2)}) %collective-permute-start.46) | collective-permute-done | bytes 245792 | tf_op jit(solution)/shard_map/ppermute | solution.py:81
  (277 shorter events, 218.5 us)
Async XLA Ops:
  7.2 115.5 %all-gather.6.cloned.1.call-start = ((), (), s32[]{:S(2)}) async-start(), calls=%async_computation.3 | async-start | bytes 8110080 | tf_op jit(solution)/shard_map/all_gather | solution.py:719
  11.3 270.8 %all-gather.4.cloned.1.call-start = ((), (), s32[]{:S(2)}) async-start(), calls=%async_computation.1 | async-start | bytes 8110080 | tf_op jit(solution)/shard_map/all_gather | solution.py:720
  12.8 28.4 %collective-permute-start.1 = (bf16[48,3328]{1,0:T(8,128)(2,1)S(1)}, bf16[48,3328]{1,0:T(8,128)(2,1)S(1)}, u32[]{:S(2)}, u32[]{:S(2)}) collective-permute-start(bf16[48,3328]{1,0:T(8,128)(2,1)S(1)} %maximum_maximum_fusion), channel_id=1, source_target_pairs={{0,4},{2,6},{4,0},{6,2},{1,5},{3,7},{5,1},{7,3},{8,12},{10,14},{12... | collective-permute-start | bytes 958472 | tf_op jit(solution)/shard_map/ppermute | solution.py:81
  15.8 33.3 %collective-permute-start.2 = (bf16[48,3328]{1,0:T(8,128)(2,1)S(1)}, bf16[48,3328]{1,0:T(8,128)(2,1)S(1)}, u32[]{:S(2)}, u32[]{:S(2)}) collective-permute-start(bf16[48,3328]{1,0:T(8,128)(2,1)S(1)} %maximum_maximum_fusion), channel_id=1, source_target_pairs={{0,6},{2,4},{4,2},{6,0},{1,7},{3,5},{5,3},{7,1},{8,14},{10,12},{12... | collective-permute-start | bytes 958472 | tf_op jit(solution)/shard_map/ppermute | solution.py:81
  50.0 20.8 %collective-permute-start.3 = (bf16[192,3328]{1,0:T(8,128)(2,1)S(1)}, bf16[192,3328]{1,0:T(8,128)(2,1)S(1)}, u32[]{:S(2)}, u32[]{:S(2)}) collective-permute-start(bf16[192,3328]{1,0:T(8,128)(2,1)S(1)} %pad_maximum_fusion.4), channel_id=1, source_target_pairs={{0,1},{2,3},{4,5},{6,7},{1,0},{3,2},{5,4},{7,6},{8,24},{10,26},{12... | collective-permute-start | bytes 3833864 | tf_op jit(solution)/shard_map/ppermute | solution.py:81
  51.6 22.7 %collective-permute-start.5 = (bf16[48,2560]{1,0:T(8,128)(2,1)S(1)}, bf16[48,2560]{1,0:T(8,128)(2,1)S(1)}, u32[]{:S(2)}, u32[]{:S(2)}) collective-permute-start(bf16[48,2560]{1,0:T(8,128)(2,1)S(1)} %get-tuple-element.116), channel_id=1, source_target_pairs={{0,4},{2,6},{4,0},{6,2},{1,5},{3,7},{5,1},{7,3},{8,12},{10,14},{12... | collective-permute-start | bytes 737288 | tf_op jit(solution)/shard_map/ppermute | solution.py:81
  74.3 45.8 %collective-permute-start.6 = (bf16[384,3328]{1,0:T(8,128)(2,1)S(1)}, bf16[384,3328]{1,0:T(8,128)(2,1)S(1)}, u32[]{:S(2)}, u32[]{:S(2)}) collective-permute-start(bf16[384,3328]{1,0:T(8,128)(2,1)S(1)} %pad_maximum_fusion.2), channel_id=1, source_target_pairs={{0,16},{2,18},{4,20},{6,22},{1,17},{3,19},{5,21},{7,23},{8,9},{10,... | collective-permute-start | bytes 7667720 | tf_op jit(solution)/shard_map/ppermute | solution.py:81
  122.7 397.5 %reduce-scatter.2.cloned.1.call-start = ((), (), s32[]{:S(2)}) async-start(), calls=%async_computation.2 | async-start | bytes 8110080 | tf_op jit(solution)/shard_map/reduce_scatter | solution.py:780
  140.1 50.9 %collective-permute-start.10 = (bf16[384,2560]{1,0:T(8,128)(2,1)S(1)}, bf16[384,2560]{1,0:T(8,128)(2,1)}, u32[]{:S(2)}, u32[]{:S(2)}) collective-permute-start(bf16[384,2560]{1,0:T(8,128)(2,1)S(1)} %pad_maximum_fusion.3), channel_id=1, source_target_pairs={{0,16},{2,18},{4,20},{6,22},{1,17},{3,19},{5,21},{7,23},{8,9},{10,... | collective-permute-start | bytes 5898248 | tf_op jit(solution)/shard_map/ppermute | solution.py:81
  308.5 34.1 %collective-permute-start.19 = (bf16[384,2560]{1,0:T(8,128)(2,1)}, bf16[384,2560]{1,0:T(8,128)(2,1)}, u32[]{:S(2)}, u32[]{:S(2)}) collective-permute-start(bf16[384,2560]{1,0:T(8,128)(2,1)} %slice.321), channel_id=1, source_target_pairs={{0,16},{2,18},{4,20},{6,22},{1,17},{3,19},{5,21},{7,23},{8,9},{10,... | collective-permute-start | bytes 5898248 | tf_op jit(solution)/shard_map/ppermute | solution.py:81
  346.0 24.8 %collective-permute-start.23 = (bf16[192,2560]{1,0:T(8,128)(2,1)S(1)}, bf16[192,2560]{1,0:T(8,128)(2,1)S(1)}, u32[]{:S(2)}, u32[]{:S(2)}) collective-permute-start(bf16[192,2560]{1,0:T(8,128)(2,1)S(1)} %slice.323), channel_id=1, source_target_pairs={{0,1},{2,3},{4,5},{6,7},{1,0},{3,2},{5,4},{7,6},{8,24},{10,26},{12... | collective-permute-start | bytes 2949128 | tf_op jit(solution)/shard_map/ppermute | solution.py:81
  371.0 35.9 %collective-permute-start.27 = (bf16[768,2944]{1,0:T(8,128)(2,1)}, bf16[768,2944]{1,0:T(8,128)(2,1)}, u32[]{:S(2)}, u32[]{:S(2)}) collective-permute-start(bf16[768,2944]{1,0:T(8,128)(2,1)} %get-tuple-element.178), channel_id=1, source_target_pairs={{0,8},{2,10},{4,12},{6,14},{1,9},{3,11},{5,13},{7,15},{8,0},{10,2}... | collective-permute-start | bytes 13565960 | tf_op jit(solution)/shard_map/ppermute | solution.py:81
  381.0 24.1 %collective-permute-start.24 = (bf16[48,2560]{1,0:T(8,128)(2,1)S(1)}, bf16[48,2560]{1,0:T(8,128)(2,1)S(1)}, u32[]{:S(2)}, u32[]{:S(2)}) collective-permute-start(bf16[48,2560]{1,0:T(8,128)(2,1)S(1)} %get-tuple-element.233), channel_id=1, source_target_pairs={{0,2},{2,0},{4,6},{6,4},{1,3},{3,1},{5,7},{7,5},{8,10},{10,8},{12,... | collective-permute-start | bytes 737288 | tf_op jit(solution)/shard_map/ppermute | solution.py:81
  381.6 23.6 %collective-permute-start.25 = (bf16[48,2560]{1,0:T(8,128)(2,1)S(1)}, bf16[48,2560]{1,0:T(8,128)(2,1)S(1)}, u32[]{:S(2)}, u32[]{:S(2)}) collective-permute-start(bf16[48,2560]{1,0:T(8,128)(2,1)S(1)} %get-tuple-element.235), channel_id=1, source_target_pairs={{0,4},{2,6},{4,0},{6,2},{1,5},{3,7},{5,1},{7,3},{8,12},{10,14},{12... | collective-permute-start | bytes 737288 | tf_op jit(solution)/shard_map/ppermute | solution.py:81
  381.8 24.2 %collective-permute-start.26 = (bf16[48,2560]{1,0:T(8,128)(2,1)S(1)}, bf16[48,2560]{1,0:T(8,128)(2,1)S(1)}, u32[]{:S(2)}, u32[]{:S(2)}) collective-permute-start(bf16[48,2560]{1,0:T(8,128)(2,1)S(1)} %get-tuple-element.234), channel_id=1, source_target_pairs={{0,6},{2,4},{4,2},{6,0},{1,7},{3,5},{5,3},{7,1},{8,14},{10,12},{12... | collective-permute-start | bytes 737288 | tf_op jit(solution)/shard_map/ppermute | solution.py:81
  412.0 46.4 %collective-permute-start.32 = (bf16[768,2560]{1,0:T(8,128)(2,1)}, bf16[768,2560]{1,0:T(8,128)(2,1)S(1)}, u32[]{:S(2)}, u32[]{:S(2)}) collective-permute-start(bf16[768,2560]{1,0:T(8,128)(2,1)} %get-tuple-element.197), channel_id=1, source_target_pairs={{0,8},{2,10},{4,12},{6,14},{1,9},{3,11},{5,13},{7,15},{8,0},{10,2}... | collective-permute-start | bytes 11796488 | tf_op jit(solution)/shard_map/ppermute | solution.py:81
  415.6 40.0 %collective-permute-start.31 = (bf16[384,2944]{1,0:T(8,128)(2,1)}, bf16[384,2944]{1,0:T(8,128)(2,1)}, u32[]{:S(2)}, u32[]{:S(2)}) collective-permute-start(bf16[384,2944]{1,0:T(8,128)(2,1)} %slice.329), channel_id=1, source_target_pairs={{0,16},{2,18},{4,20},{6,22},{1,17},{3,19},{5,21},{7,23},{8,9},{10,... | collective-permute-start | bytes 6782984 | tf_op jit(solution)/shard_map/ppermute | solution.py:81
  459.8 19.9 %collective-permute-start.35 = (bf16[256,1152]{1,0:T(8,128)(2,1)S(1)}, bf16[256,1152]{1,0:T(8,128)(2,1)S(1)}, u32[]{:S(2)}, u32[]{:S(2)}) collective-permute-start(bf16[256,1152]{1,0:T(8,128)(2,1)S(1)} %copy-done.23), channel_id=1, source_target_pairs={{0,8},{2,10},{4,12},{6,14},{1,9},{3,11},{5,13},{7,15},{8,0},{10,2}... | collective-permute-start | bytes 1769480 | tf_op jit(solution)/shard_map/ppermute | solution.py:81
  477.0 42.8 %collective-permute-start.34 = (bf16[384,2560]{1,0:T(8,128)(2,1)S(1)}, bf16[384,2560]{1,0:T(8,128)(2,1)S(1)}, u32[]{:S(2)}, u32[]{:S(2)}) collective-permute-start(bf16[384,2560]{1,0:T(8,128)(2,1)S(1)} %slice.333), channel_id=1, source_target_pairs={{0,16},{2,18},{4,20},{6,22},{1,17},{3,19},{5,21},{7,23},{8,9},{10,... | collective-permute-start | bytes 5898248 | tf_op jit(solution)/shard_map/ppermute | solution.py:81
  477.1 42.3 %collective-permute-start.33 = (bf16[192,2944]{1,0:T(8,128)(2,1)S(1)}, bf16[192,2944]{1,0:T(8,128)(2,1)S(1)}, u32[]{:S(2)}, u32[]{:S(2)}) collective-permute-start(bf16[192,2944]{1,0:T(8,128)(2,1)S(1)} %slice.331), channel_id=1, source_target_pairs={{0,1},{2,3},{4,5},{6,7},{1,0},{3,2},{5,4},{7,6},{8,24},{10,26},{12... | collective-permute-start | bytes 3391496 | tf_op jit(solution)/shard_map/ppermute | solution.py:81
  479.9 39.5 %collective-permute-start.36 = (bf16[128,1152]{1,0:T(8,128)(2,1)S(1)}, bf16[128,1152]{1,0:T(8,128)(2,1)S(1)}, u32[]{:S(2)}, u32[]{:S(2)}) collective-permute-start(bf16[128,1152]{1,0:T(8,128)(2,1)S(1)} %slice.390), channel_id=1, source_target_pairs={{0,16},{2,18},{4,20},{6,22},{1,17},{3,19},{5,21},{7,23},{8,9},{10,... | collective-permute-start | bytes 884744 | tf_op jit(solution)/shard_map/ppermute | solution.py:81
  521.9 28.7 %collective-permute-start.40 = (bf16[192,2560]{1,0:T(8,128)(2,1)S(1)}, bf16[192,2560]{1,0:T(8,128)(2,1)S(1)}, u32[]{:S(2)}, u32[]{:S(2)}) collective-permute-start(bf16[192,2560]{1,0:T(8,128)(2,1)S(1)} %slice.341), channel_id=1, source_target_pairs={{0,1},{2,3},{4,5},{6,7},{1,0},{3,2},{5,4},{7,6},{8,24},{10,26},{12... | collective-permute-start | bytes 2949128 | tf_op jit(solution)/shard_map/ppermute | solution.py:81
  525.6 24.8 %collective-permute-start.39 = (bf16[48,2944]{1,0:T(8,128)(2,1)S(1)}, bf16[48,2944]{1,0:T(8,128)(2,1)S(1)}, u32[]{:S(2)}, u32[]{:S(2)}) collective-permute-start(bf16[48,2944]{1,0:T(8,128)(2,1)S(1)} %get-tuple-element.224), channel_id=1, source_target_pairs={{0,6},{2,4},{4,2},{6,0},{1,7},{3,5},{5,3},{7,1},{8,14},{10,12},{12... | collective-permute-start | bytes 847880 | tf_op jit(solution)/shard_map/ppermute | solution.py:81
  558.7 22.5 %collective-permute-start.47 = (bf16[48,2560]{1,0:T(8,128)(2,1)S(1)}, bf16[48,2560]{1,0:T(8,128)(2,1)}, u32[]{:S(2)}, u32[]{:S(2)}) collective-permute-start(bf16[48,2560]{1,0:T(8,128)(2,1)S(1)} %get-tuple-element.231), channel_id=1, source_target_pairs={{0,6},{2,4},{4,2},{6,0},{1,7},{3,5},{5,3},{7,1},{8,14},{10,12},{12... | collective-permute-start | bytes 737288 | tf_op jit(solution)/shard_map/ppermute | solution.py:81
  (52 other events, 499.9 us)
Sparse Core Ops, SparseCore 0:
  11.6 107.9 all-gather.5
  123.0 82.4 all-gather.3
  381.1 138.1 reduce-scatter.1

commit v3 on v2

--- a/solution.py
+++ b/solution.py
@@ -14,7 +14,7 @@
 AXES = ("dp", "seq")
 BF = jnp.bfloat16
 F32 = jnp.float32
-VMEM_LIMIT = 60 << 20
+VMEM_LIMIT = 30 << 20
 C0 = math.sqrt(2.0 / math.pi)
 C1 = 0.044715
 SMALL = 7
@@ -93,11 +93,6 @@
     return lax.optimization_barrier(arrays)
 
 
-def spread_lanes(block):
-    third = block.shape[1] // 3
-    return cat(*[block[:, i * third : (i + 1) * third] for i in range(3)])
-
-
 def close_lanes(block, rows):
     parts = block.reshape(-1, 3, rows, block.shape[1])
     return jnp.concatenate([parts[:, i] for i in range(3)], axis=-1).reshape(-1, 3 * block.shape[1])
@@ -148,7 +143,7 @@
 
 
 def full_spec(shape):
-    return pl.BlockSpec(shape, lambda *_: (0,) * len(shape))
+    return pl.BlockSpec(memory_space=pltpu.VMEM)
 
 
 COST = pl.CostEstimate(flops=1000, bytes_accessed=1000, transcendentals=0)
@@ -171,32 +166,20 @@
 GAIN, SHIFT, RATE, SCALE, SKIP = range(5)
 
 
-def params_kernel(lanes, dims, key_ref, own_hbm, other_hbm, wr_ref, rows_ref, own, other, sem):
-    width, chan = dims
-    span = own.shape[1] // LAYERS
-    half = own.shape[0]
-    pull_own = pltpu.make_async_copy(own_hbm.at[:, pl.ds(lanes, LAYERS * span)], own, sem.at[0])
-    pull_other = pltpu.make_async_copy(other_hbm.at[:, pl.ds(lanes, LAYERS * span)], other, sem.at[1])
-    pull_own.start()
-    pull_other.start()
-    pull_own.wait()
-    pull_other.wait()
+def params_kernel(key_ref, own_ref, other_ref, wr_ref, rows_ref):
+    chan, width = wr_ref.shape[1:]
+    half = own_ref.shape[0]
     rows_ref[...] = jnp.zeros_like(rows_ref)
-    turns = []
-    for g in range(3):
-        key = key_ref[...] - g * chan
-        turns.append((one_hot(key[:, :half], column(chan)), one_hot(key[:, half:], column(chan))))
     even = one_hot(2 * column(chan), lane(width))
     odd = one_hot(2 * column(chan) + 1, lane(width))
     same = one_hot(column(chan), lane(chan))
     for layer in range(LAYERS):
-        at = layer * span
-        for g, (turn_own, turn_other) in enumerate(turns):
-            part = dot_nn(turn_own, own[:, at : at + span]) + dot_nn(turn_other, other[:, at : at + span])
-            part = part.astype(BF)
-            low, high = g * span, min((g + 1) * span, width)
-            wr_ref[layer, :, low:high] = part[:, : high - low]
-        vec = part[:, width - 2 * span :]
+        key = key_ref[...] - layer * chan
+        whole = dot_nn(one_hot(key[:, :half], column(chan)), own_ref[...])
+        whole += dot_nn(one_hot(key[:, half:], column(chan)), other_ref[...])
+        whole = whole.astype(BF)
+        wr_ref[layer] = whole[:, :width]
+        vec = whole[:, width:]
         evens, odds = dot_tn(vec, even), dot_tn(vec, odd)
         turned = dot_tn(vec, same)
         rows_ref[layer, GAIN : GAIN + 1, :] = evens[0:1] + odds[1:2]
@@ -205,22 +188,15 @@
             rows_ref[layer, name : name + 1, :chan] = turned[k : k + 1]
 
 
-def params_call(key, own, other, lanes, width, chan):
-    half = own.shape[0]
-    span = (own.shape[1] - lanes) // LAYERS
+def params_call(key, own, other, width, chan):
     return pl.pallas_call(
-        functools.partial(params_kernel, lanes, (width, chan)),
+        params_kernel,
         out_shape=(
             jax.ShapeDtypeStruct((LAYERS, chan, width), BF),
             jax.ShapeDtypeStruct((LAYERS, 8, width), F32),
         ),
-        in_specs=[VMEM, pl.BlockSpec(memory_space=pl.ANY), pl.BlockSpec(memory_space=pl.ANY)],
+        in_specs=[VMEM] * 3,
         out_specs=(VMEM,) * 2,
-        scratch_shapes=[
-            pltpu.VMEM((half, LAYERS * span), BF),
-            pltpu.VMEM((half, LAYERS * span), BF),
-            pltpu.SemaphoreType.DMA((2,)),
-        ],
         compiler_params=pltpu.CompilerParams(vmem_limit_bytes=VMEM_LIMIT),
         cost_estimate=COST,
         name="params",
@@ -474,13 +450,20 @@
     return total.astype(BF)
 
 
-def wide_kernel(names, mode, blocks, dims, head_rows, *refs):
-    r = dict(zip(names, refs), head_rows=head_rows)
+def wide_kernel(names, mode, blocks, dims, groups, *refs):
+    r = dict(zip(names, (groups,) + refs))
     width, chan = dims
     step = pl.program_id(0)
     forward, backward = mode != "back", mode != "fore"
     pair = "other" in r
     weights = r["weights"] if pair else r["own"]
+
+    def part(low, high):
+        if len(weights.shape) == 4:
+            return weights[:, 0, :, low:high].reshape(-1, high - low)
+        return weights[:, low:high]
+
+    w_gate, w_out, w_expand = [functools.partial(part, *at) for at in ((0, width), (width, 2 * width), (2 * width, 2 * width + chan))]
 
     @pl.when(step == 0)
     def _():
@@ -502,8 +485,8 @@
 
     normed, mixed = r["normed"][...], r["mixed"][...]
     if forward:
-        pre = dot_nt(normed, weights[:, :width])
-        expanded = dot_nt(mixed, weights[:, 2 * width :])
+        pre = dot_nt(normed, w_gate())
+        expanded = dot_nt(mixed, w_expand())
         if mode == "fore":
             r["pre"][...] = pre
             r["expanded"][...] = expanded
@@ -515,39 +498,25 @@
         gate = gelu(pre)
     joined = (expanded * gate).astype(BF)
     if forward:
-        r["acc"][...] += dot_nn(joined, weights[:, width : 2 * width])
+        r["acc"][...] += dot_nn(joined, w_out())
     if backward:
         low = r["low"][...]
-        d_joined = dot_nt(low, weights[:, width : 2 * width])
+        d_joined = dot_nt(low, w_out())
         d_expanded = (d_joined * gate).astype(BF)
         d_pre = (d_joined * expanded * slope).astype(BF)
-        r["d_mixed"][...] += dot_nn(d_expanded, weights[:, 2 * width :])
-        r["d_normed"][...] += dot_nn(d_pre, weights[:, :width])
-
-        def store(out):
-            out[:, :width] = dot_tn(d_pre, normed).astype(BF)
-            out[:, width : 2 * width] = dot_tn(joined, low).astype(BF)
-            out[:, 2 * width :] = dot_tn(d_expanded, mixed).astype(BF)
-
-        if not pair:
-            store(r["grad_own"])
-        else:
-            grads = r["grads"]
-            store(grads)
-            lanes = 2 * width + chan
-
-            def put(out, head):
-                out[:, :lanes] = grads[...]
-                if head in r:
-                    out[:, lanes:] = spread_block(r[head], out.shape[0], r["head_rows"], step % blocks)
-
-            @pl.when(step < blocks)
-            def _():
-                put(r["grad_own"], "head_own")
-
-            @pl.when(step >= blocks)
-            def _():
-                put(r["grad_other"], "head_other")
+        r["d_mixed"][...] += dot_nn(d_expanded, w_expand())
+        r["d_normed"][...] += dot_nn(d_pre, w_gate())
+
+        def keep(out):
+            out[0], out[1], out[2] = d_pre, joined, d_expanded
+
+        @pl.when(step < blocks)
+        def _():
+            keep(r["acts_first"])
+
+        @pl.when(step >= blocks)
+        def _():
+            keep(r["acts_last"])
 
     if "out" in r:
 
@@ -556,35 +525,30 @@
             r["out"][...] = r["acc"][...].astype(r["out"].dtype)
 
 
-def wide_call(mode, own, other, normed, mixed, base=None, low=None, pre=None, expanded=None, sums=None, heads=None, head_rows=0, out_dtype=None):
+def wide_call(mode, own, other, normed, mixed, base=None, low=None, saved=None, sums=None, out_dtype=F32, job=0, groups=None):
     rows, width = normed.shape
     chan = mixed.shape[1]
-    span = own.shape[0]
-    pair = other is not None
-    block = span // 2 if pair else span // 4
-    blocks = span // block
-    steps = blocks * (2 if pair else 1)
+    pair = groups is None
+    if pair:
+        groups = jnp.zeros((1,), jnp.int32)
+        blocks, block = 2, own.shape[0] // 2
+    else:
+        blocks = groups.shape[0] // 2
+        block = own.shape[0] * own.shape[2] // groups.shape[0]
     lanes = 2 * width + chan
     forward, backward = mode != "back", mode != "fore"
     ins, outs, scratch = [], [], []
-
-    def half_spec(which, count):
-        if which == "own":
-            return pl.BlockSpec((block, count), lambda i: (jnp.minimum(i, blocks - 1), 0))
-        return pl.BlockSpec((block, count), lambda i: (jnp.maximum(i - blocks, 0), 0))
-
-    ins.append(("own", own, half_spec("own", lanes)))
-    more = 0
+    early = lambda i, _: (jnp.minimum(i, blocks - 1), 0)
+    late = lambda i, _: (jnp.maximum(i - blocks, 0), 0)
     if pair:
-        ins.append(("other", other, half_spec("other", lanes)))
-    if heads is not None:
-        more = heads[0].shape[1] // 3
-        ins.append(("head_own", heads[0], full_spec(heads[0].shape)))
-        ins.append(("head_other", heads[1], full_spec(heads[1].shape)))
+        ins.append(("own", own, pl.BlockSpec((block, lanes), early)))
+        ins.append(("other", other, pl.BlockSpec((block, lanes), late)))
+    else:
+        deep = (block // own.shape[2], 1, own.shape[2], lanes)
+        ins.append(("own", own, pl.BlockSpec(deep, lambda i, at: (at[i], job, 0, 0))))
     ins.append(("normed", normed, full_spec(normed.shape)))
     ins.append(("mixed", mixed, full_spec(mixed.shape)))
-    saved = pl.BlockSpec((rows, block), lambda i: (0, i))
-    saved_shape = jax.ShapeDtypeStruct((rows, steps * block), F32)
+    side = pl.BlockSpec((rows, block), lambda i, _: (0, i))
     if forward:
         ins.append(("base", base, full_spec(base.shape)))
     if backward:
@@ -593,11 +557,11 @@
             ins.append(("d_normed_in", sums[0], full_spec(sums[0].shape)))
             ins.append(("d_mixed_in", sums[1], full_spec(sums[1].shape)))
     if mode == "back":
-        ins.append(("pre", pre, saved))
-        ins.append(("expanded", expanded, saved))
+        ins.append(("pre", saved[0], side))
+        ins.append(("expanded", saved[1], side))
     if mode == "fore":
-        outs.append(("pre", saved_shape, saved))
-        outs.append(("expanded", saved_shape, saved))
+        for name in ("pre", "expanded"):
+            outs.append((name, jax.ShapeDtypeStruct((rows, 2 * blocks * block), F32), side))
     if forward:
         if out_dtype == F32:
             outs.append(("acc", jax.ShapeDtypeStruct((rows, width), F32), full_spec((rows, width))))
@@ -607,25 +571,78 @@
     if backward:
         outs.append(("d_normed", jax.ShapeDtypeStruct((rows, width), F32), full_spec((rows, width))))
         outs.append(("d_mixed", jax.ShapeDtypeStruct((rows, chan), F32), full_spec((rows, chan))))
-        grad = jax.ShapeDtypeStruct((span, lanes + more), BF)
-        outs.append(("grad_own", grad, half_spec("own", lanes + more)))
-        if pair:
-            outs.append(("grad_other", grad, half_spec("other", lanes + more)))
-            scratch.append(("grads", pltpu.VMEM((block, lanes), BF)))
+        acts = jax.ShapeDtypeStruct((3, rows, blocks * block), BF)
+        for name, at in (("acts_first", early), ("acts_last", late)):
+            outs.append((name, acts, pl.BlockSpec((3, rows, block), lambda i, _, at=at: (0, 0, at(i, _)[0]))))
     if pair:
         scratch.append(("weights", pltpu.VMEM((block, lanes), BF)))
-    names = [name for name, _, _ in ins + outs] + [name for name, _ in scratch]
+    names = ["groups"] + [name for name, _, _ in ins + outs] + [name for name, _ in scratch]
     return pl.pallas_call(
-        functools.partial(wide_kernel, names, mode, blocks, (width, chan), head_rows),
-        grid=(steps,),
+        functools.partial(wide_kernel, names, mode, blocks, (width, chan)),
+        grid_spec=pltpu.PrefetchScalarGridSpec(
+            num_scalar_prefetch=1,
+            grid=(2 * blocks,),
+            in_specs=[spec for _, _, spec in ins],
+            out_specs=tuple(spec for _, _, spec in outs),
+            scratch_shapes=[shape for _, shape in scratch],
+        ),
         out_shape=tuple(shape for _, shape, _ in outs),
-        in_specs=[spec for _, _, spec in ins],
-        out_specs=tuple(spec for _, _, spec in outs),
-        scratch_shapes=[shape for _, shape in scratch],
         compiler_params=pltpu.CompilerParams(vmem_limit_bytes=VMEM_LIMIT),
         cost_estimate=COST,
         name="wide_" + mode,
-    )(*[array for _, array, _ in ins])
+    )(groups, *[array for _, array, _ in ins])
+
+
+def grads_kernel(names, head_rows, sub, places, *refs):
+    r = dict(zip(names, refs))
+    step = pl.program_id(0)
+    out = r["grads"] if sub else r["out"]
+    at = 0
+    for k, name in enumerate(("normed", "low", "mixed")):
+        span = r[name].shape[1]
+        total = dot_tn(r["acts"][k], r[name][...]) + dot_tn(r["peer_acts"][k], r["peer_" + name][...])
+        out[:, at : at + span] = total.astype(BF)
+        at += span
+    if "head" in r:
+        head = (r["head"][...].astype(F32) + r["peer_head"][...].astype(F32)).astype(BF)
+        out[:, at:] = spread_block(head, out.shape[0], head_rows, step)
+    if sub:
+        count = out.shape[0] // sub
+        for j in range(count):
+            to = pl.multiple_of(places[step * count + j] * sub, 16)
+            r["out"][pl.ds(to, sub), :] = out[j * sub : (j + 1) * sub, :]
+
+
+def grads_call(acts, peer_acts, inputs, peer_inputs, places=None, sub=0, heads=None, head_rows=0):
+    rows, span = acts.shape[1:]
+    steps = 2
+    block = span // steps
+    ins = []
+    for prefix, array, sides in (("", acts, inputs), ("peer_", peer_acts, peer_inputs)):
+        ins.append((prefix + "acts", array, pl.BlockSpec((3, rows, block), lambda i, _: (0, 0, i))))
+        for name, side in zip(("normed", "low", "mixed"), sides):
+            ins.append((prefix + name, side, full_spec(side.shape)))
+    lanes = sum(side.shape[1] for side in inputs)
+    if heads is not None:
+        ins.append(("head", heads[0], full_spec(heads[0].shape)))
+        ins.append(("peer_head", heads[1], full_spec(heads[1].shape)))
+        lanes += heads[0].shape[1] // 3
+    out_spec = full_spec((span, lanes)) if sub else pl.BlockSpec((block, lanes), lambda i, _: (i, 0))
+    names = [name for name, _, _ in ins] + ["out"] + (["grads"] if sub else [])
+    return pl.pallas_call(
+        functools.partial(grads_kernel, names, head_rows, sub),
+        grid_spec=pltpu.PrefetchScalarGridSpec(
+            num_scalar_prefetch=1,
+            grid=(steps,),
+            in_specs=[spec for _, _, spec in ins],
+            out_specs=out_spec,
+            scratch_shapes=[pltpu.VMEM((block, lanes), BF)] if sub else [],
+        ),
+        out_shape=jax.ShapeDtypeStruct((span, lanes), BF),
+        compiler_params=pltpu.CompilerParams(vmem_limit_bytes=VMEM_LIMIT),
+        cost_estimate=COST,
+        name="grads",
+    )(jnp.zeros((1,), jnp.int32) if places is None else places, *[array for _, array, _ in ins])
 
 
 def seq_gather(lay, vector):
@@ -696,142 +713,164 @@
             axis=1,
         )
 
-    heads = [jnp.concatenate([w_reduce[i].T, vectors(i)], axis=1) for i in range(LAYERS)]
-    bundles = [
-        jnp.concatenate([w_gate[i].T, w_out[i], w_expand[i].T], axis=1).reshape(JOBS, job_rows, -1)
-        for i in range(LAYERS)
+    head = cat(*[jnp.concatenate([w_reduce[i].T, vectors(i)], axis=1) for i in range(LAYERS)])
+    bundles = [jnp.concatenate([w_gate[i].T, w_out[i], w_expand[i].T], axis=1) for i in range(LAYERS)]
+    shard_a, shard_b, shard_c, shard_d = [
+        bundle[job * job_rows : (job + 1) * job_rows] for bundle in bundles for job in range(JOBS)
     ]
     nature = lay.natural_rows(small_rows)
-    lanes = bundles[0].shape[2]
-    group = jnp.arange(3, dtype=jnp.int32)[None, :, None] * chan
+    lanes = bundles[0].shape[1]
+    group = jnp.arange(LAYERS, dtype=jnp.int32)[None, :, None] * chan
     key = (nature.reshape(lay.count, 1, small_rows) + group).reshape(1, -1)
 
-    def relative_order(gathered):
-        order = lay.natural_rows(1)
-        half = lay.count // 2
-        return [
-            gathered.at[at].get(mode="promise_in_bounds", unique_indices=True).reshape(half * job_rows, -1)
-            for at in (order[:half], order[half:])
-        ]
-
-    first = jnp.concatenate([bundles[0][0]] + [spread_lanes(h) for h in heads], axis=1)
-    third = bundles[0][1]
-    gathered_a = lax.all_gather(bundles[1][0], AXES, axis=0)
-    gathered_b = lax.all_gather(after(bundles[1][1], gathered_a), AXES, axis=0, tiled=True)
-
-    line_a = stage(first, lay.q)
-    line_a, third = fence(line_a, third)
+    steps = [list(range(1, lay.nq))[i::3] for i in range(3)]
+
+    def pulls(shard, *which):
+        return {k: permute(shard, lay.q[k]) for i in which for k in steps[i]}
+
+    def line_of(shard, pulled):
+        return cat(shard, *[pulled[k] for k in range(1, lay.nq)])
+
+    def swap(*arrays):
+        return [permute(array, lay.core) for array in arrays]
+
+    line_h = stage(head, lay.q)
+    line_h, shard_a = fence(line_h, shard_a)
+    plane_h = stage(line_h, lay.p1)
+    pulled = pulls(shard_a, 0)
+    plane_h, shard_a, pulled = fence(plane_h, shard_a, pulled)
+    head_own = stage(plane_h, lay.p2)
+    pulled |= pulls(shard_a, 1)
+    head_own, shard_a, pulled = fence(head_own, shard_a, pulled)
+    head_other = permute(head_own, lay.core)
+    pulled |= pulls(shard_a, 2)
+    head_own, head_other, line_a, shard_b = fence(head_own, head_other, line_of(shard_a, pulled), shard_b)
+
     plane_a = stage(line_a, lay.p1)
-    cut = max(1, (lay.nq * 2) // 3) + 1
-    early = [permute(third, lay.q[k]) for k in range(1, cut)]
-    plane_a, third, *early = fence(plane_a, third, *early)
-    a_own = stage(plane_a, lay.p2)
-    line_b = cat(third, *early, *[permute(third, lay.q[k]) for k in range(cut, lay.nq)])
-    a_own, line_b = fence(a_own, line_b)
-    a_other = permute(a_own, lay.core)
-    plane_b = stage(line_b, lay.p1)
-    a_own, a_other, plane_b, gathered_a = fence(a_own, a_other, plane_b, gathered_a)
-    b_own = stage(plane_b, lay.p2)
-    wr_all, rows_all = params_call(key, a_own, a_other, lanes, width, chan)
-
-    def enter(layer, stream):
-        normed, pre_reduce, local_states, last = enter_call(layer, near, stream, rows_all, wr_all)
-        lasts = seq_gather(lay, last)
+    pulled = pulls(shard_b, 0)
+    wr_all, rows_all = params_call(key, head_own, head_other, width, chan)
+    entered = enter_call(0, near, tokens, rows_all, wr_all)
+    lasts = seq_gather(lay, entered[3])
+    plane_a, shard_b, pulled, entered, lasts = fence(plane_a, shard_b, pulled, entered, lasts)
+
+    def enter(layer, stream, entered, lasts):
+        normed, pre_reduce, local_states, _ = entered
         states, state_in, mixed = mix_call(
             layer, near, hops_fore, lasts, prev_state[layer], rows_all, pre_reduce, local_states
         )
         return dict(stream=stream, normed=normed, pre_reduce=pre_reduce, states=states, state_in=state_in, mixed=mixed)
 
-    def leave(layer, kept, sums, upstream):
-        d_normed, d_mixed = sums
-        back_local, first_row = back_scan_call(layer, near, d_mixed, rows_all)
-        firsts = seq_gather(lay, first_row)
+    def turn_back(layer, sums):
+        back_local, first_row = back_scan_call(layer, near, sums[1], rows_all)
+        return back_local, seq_gather(lay, first_row)
+
+    def leave(layer, kept, sums, reached, upstream):
         upstream, low, *head = leave_call(
-            layer, near, hops_back, firsts, nature, d_mixed, back_local, kept, rows_all, wr_all, d_normed, upstream
+            layer, near, hops_back, reached[1], nature, sums[1], reached[0], kept, rows_all, wr_all, sums[0], upstream
         )
         return upstream, low, head
 
-    k0 = enter(0, tokens)
-    top_a = relative_order(gathered_a)
-    b_own, k0["mixed"], *top_a = fence(b_own, k0["mixed"], *top_a)
-    b_other = permute(b_own, lay.core)
-    pre_a, exp_a, acc = wide_call("fore", a_own, a_other, k0["normed"], k0["mixed"], base=tokens, out_dtype=F32)
-    b_own, b_other, acc = fence(b_own, b_other, acc)
-    pre_b, exp_b, acc = wide_call("fore", b_own, b_other, k0["normed"], k0["mixed"], base=acc, out_dtype=F32)
-
-    k1 = enter(1, acc)
-    acc, d_normed, d_mixed, a1_own, a1_other = wide_call(
-        "both", *top_a, k1["normed"], k1["mixed"], base=k1["stream"], low=cotangent, out_dtype=F32
+    def both(own, other, base, sums, out_dtype=F32):
+        out, d_normed, d_mixed, mine, peers = wide_call(
+            "both",
+            own,
+            other,
+            k1["normed"],
+            k1["mixed"],
+            base=base,
+            low=cotangent,
+            sums=sums,
+            out_dtype=out_dtype,
+        )
+        return out, [d_normed, d_mixed], mine, peers
+
+    def back(own, other, saved, sums):
+        d_normed, d_mixed, mine, peers = wide_call(
+            "back", own, other, k0["normed"], k0["mixed"], low=low, saved=saved, sums=sums
+        )
+        return [d_normed, d_mixed], mine, peers
+
+    k0 = enter(0, tokens, entered, lasts)
+    a_own = stage(plane_a, lay.p2)
+    pulled |= pulls(shard_b, 1, 2)
+    a_own, line_b, k0, shard_c = fence(a_own, line_of(shard_b, pulled), k0, shard_c)
+    (a_other,) = swap(a_own)
+    plane_b = stage(line_b, lay.p1)
+    pulled = pulls(shard_c, 0)
+    a_own, a_other, plane_b, shard_c, pulled = fence(a_own, a_other, plane_b, shard_c, pulled)
+    b_own = stage(plane_b, lay.p2)
+    pulled |= pulls(shard_c, 1, 2)
+    *save_a, acc = wide_call("fore", a_own, a_other, k0["normed"], k0["mixed"], base=tokens)
+    b_own, line_c, acc, shard_d = fence(b_own, line_of(shard_c, pulled), acc, shard_d)
+    (b_other,) = swap(b_own)
+    plane_c = stage(line_c, lay.p1)
+    pulled = pulls(shard_d, 0)
+    b_own, b_other, plane_c, shard_d, pulled = fence(b_own, b_other, plane_c, shard_d, pulled)
+    c_own = stage(plane_c, lay.p2)
+    pulled |= pulls(shard_d, 1, 2)
+    *save_b, acc = wide_call("fore", b_own, b_other, k0["normed"], k0["mixed"], base=acc)
+    entered = enter_call(1, near, acc, rows_all, wr_all)
+    c_own, line_d, acc, entered = fence(c_own, line_of(shard_d, pulled), acc, entered)
+    (c_other,) = swap(c_own)
+    plane_d = stage(line_d, lay.p1)
+    k1 = enter(1, acc, entered, seq_gather(lay, entered[3]))
+    c_own, c_other, plane_d, k1 = fence(c_own, c_other, plane_d, k1)
+
+    d_own = stage(plane_d, lay.p2)
+    ins_1 = (k1["normed"], cotangent, k1["mixed"])
+    peer_1 = swap(*ins_1)
+    acc, sums, a1_own, a1_peer = both(c_own, c_other, acc, None)
+    d_own, acc, sums, a1_own, a1_peer, peer_1 = fence(d_own, acc, sums, a1_own, a1_peer, peer_1)
+    (a1_peer,) = swap(a1_peer)
+    (d_other,) = swap(d_own)
+    a1 = grads_call(a1_own, a1_peer, ins_1, peer_1)
+    d_own, d_other, a1 = fence(d_own, d_other, a1)
+    a1 = fold(a1, lay.p2)
+    output, sums, b1_own, b1_peer = both(d_own, d_other, acc, sums, BF)
+    a1, sums, b1_own, b1_peer = fence(a1, sums, b1_own, b1_peer)
+
+    (b1_peer,) = swap(b1_peer)
+    reached = turn_back(1, sums)
+    b1 = grads_call(b1_own, b1_peer, ins_1, peer_1)
+    a1, b1, sums, reached = fence(a1, b1, sums, reached)
+    upstream, low, head_1 = leave(1, k1, sums, reached, cotangent)
+
+    b1 = fold(b1, lay.p2)
+    a1_done = fold(fold(a1, lay.p1), lay.q, F32)
+    peer_0 = swap(k0["normed"], low, k0["mixed"])
+    (head_peer,) = swap(head_1[1])
+    sums, a0_own, a0_peer = back(a_own, a_other, save_a, None)
+    sums, a0_sent = fence(sums, a0_peer)
+    (a0_peer,) = swap(a0_sent)
+    sums, b0_own, b0_peer = back(b_own, b_other, save_b, sums)
+    a1_done, b1, peer_0, head_peer, a0_own, a0_peer, sums, b0_own, b0_peer = fence(
+        a1_done, b1, peer_0, head_peer, a0_own, a0_peer, sums, b0_own, b0_peer
     )
-    acc, d_normed, d_mixed, a1_own, a1_other = fence(acc, d_normed, d_mixed, a1_own, a1_other)
-    a1 = add_parts([a1_own, permute(a1_other, lay.core)], BF)
-    output, d_normed, d_mixed, b1 = wide_call(
-        "both",
-        gathered_b,
-        None,
-        k1["normed"],
-        k1["mixed"],
-        base=acc,
-        low=cotangent,
-        sums=(d_normed, d_mixed),
-        out_dtype=BF,
-    )
-    a1, d_normed, d_mixed, b1 = fence(a1, d_normed, d_mixed, b1)
-    b1_done = lax.psum_scatter(b1, AXES, scatter_dimension=0, tiled=True)
-
-    a1 = fold(a1, lay.p2)
-    upstream, low, head_1 = leave(1, k1, (d_normed, d_mixed), cotangent)
-    a1, low, upstream, *head_1 = fence(a1, low, upstream, *head_1)
-
-    a1 = fold(a1, lay.p1)
-    d_normed, d_mixed, a0_own, a0_other = wide_call(
-        "back",
-        a_own,
-        a_other,
-        k0["normed"],
-        k0["mixed"],
-        low=low,
-        pre=pre_a,
-        expanded=exp_a,
-        heads=head_1,
-        head_rows=small_rows,
-    )
-    a1, d_normed, d_mixed, a0_own, a0_other = fence(a1, d_normed, d_mixed, a0_own, a0_other)
-
-    a1_done = fold(a1, lay.q, F32)
-    a0 = add_parts([a0_own, permute(a0_other, lay.core)], BF)
-    d_normed, d_mixed, b0_own, b0_other = wide_call(
-        "back",
-        b_own,
-        b_other,
-        k0["normed"],
-        k0["mixed"],
-        low=low,
-        pre=pre_b,
-        expanded=exp_b,
-        sums=(d_normed, d_mixed),
-    )
-    a1_done, a0, d_normed, d_mixed, b0_own, b0_other = fence(a1_done, a0, d_normed, d_mixed, b0_own, b0_other)
-
-    b0 = add_parts([b0_own, permute(b0_other, lay.core)], BF)
+    ins_0 = (k0["normed"], low, k0["mixed"])
+    b1 = fold(b1, lay.p1)
+    (b0_peer,) = swap(b0_peer)
+    a0 = grads_call(a0_own, a0_peer, ins_0, peer_0, heads=(head_1[0], head_peer), head_rows=small_rows)
+    b1, a0, sums, b0_own, b0_peer = fence(b1, a0, sums, b0_own, b0_peer)
+
     a0 = fold(a0, lay.p2)
-    _, input_grad, (head_own, head_other) = leave(0, k0, (d_normed, d_mixed), upstream)
-    a0, b0, head_own, head_other = fence(a0, b0, head_own, head_other)
-
+    b1_done = fold(b1, lay.q, F32)
+    b0 = grads_call(b0_own, b0_peer, ins_0, peer_0)
+    sums[1] = after(sums[1], b0)
+    reached = turn_back(0, sums)
+    a0, b0, b1_done, sums, reached = fence(a0, b0, b1_done, sums, reached)
     a0 = fold(a0, lay.p1)
+    _, input_grad, (head_own, head_other) = leave(0, k0, sums, reached, upstream)
+    a0, head_own, head_other = fence(a0, head_own, head_other)
+    a0_done = fold(a0, lay.q, F32)
     b0 = fold(b0, lay.p2)
-    h0 = fold(add_parts([head_own, permute(head_other, lay.core)], BF), lay.p2)
-    a0, b0, h0, b1_done = fence(a0, b0, h0, b1_done)
-
-    a0_done = fold(a0, lay.q, F32)
-    b0 = fold(b0, lay.p1)
-    h0 = fold(h0, lay.p1)
+    h0 = add_parts([head_own, *swap(head_other)], BF)
     a0_done, b0, h0 = fence(a0_done, b0, h0)
+    b0, h0 = fold(b0, lay.p1), fold(h0, lay.p2)
+    b0, h0 = fence(b0, h0)
     b0_done = fold(b0, lay.q, F32)
-    h0_done = fold(h0, lay.q, F32)
+    h0_done = fold(fold(h0, lay.p1), lay.q, F32)
 
     h1_done = close_lanes(a0_done[:, lanes:], small_rows)
-    b1_done = b1_done.astype(F32)
     grads = [cat(a0_done[:, :lanes], b0_done), cat(a1_done, b1_done)]
     heads_done = [h0_done, h1_done]
     vecs = [h[:, width : width + SMALL] for h in heads_done]

time: 596 us -> 549 us (0.921)
  Pallas kernels: 181 us -> 143 us
  local copies, waits for them, and re-layouts: 28.8 us -> 63.7 us
  other arithmetic: 50.4 us -> 25.7 us
  between operations: 14.9 us -> 2.31 us
  starting transfers between devices: 84.3 us -> 75.5 us
    unnamed x50 -> x187, local copies, waits for them, and re-layouts: 3.35 us -> 49 us
    pallas_call x6, Pallas kernels: 115 us -> 77.9 us  [wide_call(): pl.pallas_call(functools.partial(wide_kernel, names, mode, blocks, (width...]
    pallas_call x1 -> x5, Pallas kernels: 9.55 us -> 29.3 us  [the longest x4 24.7 us: grads_call(): pl.pallas_call(functools.partial(grads_kernel, names, head_rows, sub), gr...]
    gather x2 -> x0, local copies, waits for them, and re-layouts: 12.1 us -> none  [relative_order(): gathered.at[at].get(mode='promise_in_bounds', unique_indices=True)]
    pallas_call x2, Pallas kernels: 22.8 us -> 12.9 us  [leave_call(): pl.pallas_call(functools.partial(leave_kernel, starts.shape[0], layer), o...]
    concatenate x18 -> x27, other arithmetic: 17.4 us -> 7.62 us  [cat(): return jnp.concatenate(arrays, axis=0)]
    convert_element_type x12 -> x11, other arithmetic: 17.7 us -> 8.13 us  [add_parts(): return total.astype(dtype)]
    ppermute x48 -> x79, starting transfers between devices: 83.6 us -> 75.5 us  [permute(): return lax.ppermute(array, AXES, pairs)]
  transfers between devices with their start and end apart: 51 -> 79, of which waited for: 30 -> 43; matrix products, arithmetic and copies ran while one was open for 10% -> 4% of each run, Pallas kernels for 27% -> 25%
where the time goes in v3:
time: 549 us; the launch traced here: 542 us
  waiting for transfers between devices  232 us (42%)
  Pallas kernels  143 us (26%)
  starting transfers between devices  75.5 us (14%)
  local copies, waits for them, and re-layouts  63.7 us (12%)
  other arithmetic  25.7 us (5%)
    ppermute x79, waiting for transfers between devices, permute(): return lax.ppermute(array, AXES, pairs)  232 us
    pallas_call x6, Pallas kernels, wide_call(): pl.pallas_call(functools.partial(wide_kernel, names, mode, blocks, (width...  77.9 us
    ppermute x79, starting transfers between devices, permute(): return lax.ppermute(array, AXES, pairs)  75.5 us
    unnamed x187, local copies, waits for them, and re-layouts  49 us
    pallas_call x4, Pallas kernels, grads_call(): pl.pallas_call(functools.partial(grads_kernel, names, head_rows, sub), gr...  24.7 us
    pallas_call x2, Pallas kernels, leave_call(): pl.pallas_call(functools.partial(leave_kernel, starts.shape[0], layer), o...  12.9 us
  transfers between devices with their start and end apart: 79, of which 43 were waited for; matrix products, arithmetic and copies ran while one was open for 4% of the time, Pallas kernels for 25%

profile of v3, /device:TPU:8, one launch (start us, length us, event | category | flops | bytes accessed | tf_op | source)
XLA Modules:
  0.0 542.1 jit_solution(15459995185163910685)
XLA Ops:
  26.7 6.7 %collective-permute-done.5 = bf16[256,1152]{1,0:T(8,128)(2,1)S(1)} collective-permute-done((bf16[256,1152]{1,0:T(8,128)(2,1)S(1)}, bf16[256,1152]{1,0:T(8,128)(2,1)S(1)}, u32[]{:S(2)}, u32[]{:S(2)}) %collective-permute-start.5) | collective-permute-done | bytes 589856 | tf_op jit(solution)/shard_map/ppermute | solution.py:81
  36.2 12.3 %collective-permute-done.8 = bf16[48,2560]{1,0:T(8,128)(2,1)S(1)} collective-permute-done((bf16[48,2560]{1,0:T(8,128)(2,1)S(1)}, bf16[48,2560]{1,0:T(8,128)(2,1)S(1)}, u32[]{:S(2)}, u32[]{:S(2)}) %collective-permute-start.8) | collective-permute-done | bytes 245792 | tf_op jit(solution)/shard_map/ppermute | solution.py:81
  92.4 7.1 %collective-permute-done.16 = bf16[48,2560]{1,0:T(8,128)(2,1)} collective-permute-done((bf16[48,2560]{1,0:T(8,128)(2,1)S(1)}, bf16[48,2560]{1,0:T(8,128)(2,1)}, u32[]{:S(2)}, u32[]{:S(2)}) %collective-permute-start.16) | collective-permute-done | bytes 245792 | tf_op jit(solution)/shard_map/ppermute | solution.py:81
  108.1 11.2 %collective-permute-done.18 = bf16[192,2560]{1,0:T(8,128)(2,1)S(1)} collective-permute-done((bf16[192,2560]{1,0:T(8,128)(2,1)S(1)}, bf16[192,2560]{1,0:T(8,128)(2,1)S(1)}, u32[]{:S(2)}, u32[]{:S(2)}) %collective-permute-start.18) | collective-permute-done | bytes 983072 | tf_op jit(solution)/shard_map/ppermute | solution.py:81
  123.3 7.3 %wide_fore.2 = (f32[512,1536]{1,0:T(8,128)S(1)}, f32[512,1536]{1,0:T(8,128)S(1)}, f32[512,1024]{1,0:T(8,128)S(1)}) custom-call(s32[1]{0:T(128)} %constant.172.clone.1.groups.places, bf16[768,2560]{1,0:T(8,128)(2,1)S(1)} %pad_maximum_fusion.refs_0_, bf16[768,2560]{1,0:T(8,128)(2,1)S(1)} %collective-permute-done.17.refs_1_, ...), custom_call_target="tpu_custom_call" | custom-call | flops 1000 | bytes 1000 | tf_op jit(solution)/shard_map/wide_fore/pallas_call | solution.py:580
  137.6 6.7 %collective-permute-done.22 = bf16[48,2560]{1,0:T(8,128)(2,1)S(1)} collective-permute-done((bf16[48,2560]{1,0:T(8,128)(2,1)S(1)}, bf16[48,2560]{1,0:T(8,128)(2,1)S(1)}, u32[]{:S(2)}, u32[]{:S(2)}) %collective-permute-start.22) | collective-permute-done | bytes 245792 | tf_op jit(solution)/shard_map/ppermute | solution.py:81
  147.4 11.5 %collective-permute-done.24 = bf16[192,2560]{1,0:T(8,128)(2,1)S(1)} collective-permute-done((bf16[192,2560]{1,0:T(8,128)(2,1)S(1)}, bf16[192,2560]{1,0:T(8,128)(2,1)S(1)}, u32[]{:S(2)}, u32[]{:S(2)}) %collective-permute-start.24) | collective-permute-done | bytes 983072 | tf_op jit(solution)/shard_map/ppermute | solution.py:81
  162.7 7.3 %wide_fore.3 = (f32[512,1536]{1,0:T(8,128)S(1)}, f32[512,1536]{1,0:T(8,128)S(1)}, f32[512,1024]{1,0:T(8,128)S(1)}) custom-call(s32[1]{0:T(128)} %constant.172.clone.1.groups.places, bf16[768,2560]{1,0:T(8,128)(2,1)S(1)} %pad_maximum_fusion.1.refs_0_, bf16[768,2560]{1,0:T(8,128)(2,1)S(1)} %collective-permute-done.23.refs_1_, ...), custom_call_target="tpu_custom_call" | custom-call | flops 1000 | bytes 1000 | tf_op jit(solution)/shard_map/wide_fore/pallas_call | solution.py:580
  177.8 6.2 %collective-permute-done.28 = bf16[48,2560]{1,0:T(8,128)(2,1)S(1)} collective-permute-done((bf16[48,2560]{1,0:T(8,128)(2,1)S(1)}, bf16[48,2560]{1,0:T(8,128)(2,1)S(1)}, u32[]{:S(2)}, u32[]{:S(2)}) %collective-permute-start.28) | collective-permute-done | bytes 245792 | tf_op jit(solution)/shard_map/ppermute | solution.py:81
  186.6 12.1 %collective-permute-done.31 = f32[1,512]{1,0:T(1,128)S(1)} collective-permute-done((f32[1,512]{1,0:T(1,128)S(1)}, f32[1,512]{1,0:T(1,128)S(1)}, u32[]{:S(2)}, u32[]{:S(2)}) %collective-permute-start.31) | collective-permute-done | bytes 2080 | tf_op jit(solution)/shard_map/ppermute | solution.py:81
  211.7 25.9 %wide_both.2 = (f32[512,1024]{1,0:T(8,128)S(1)}, f32[512,1024]{1,0:T(8,128)S(1)}, f32[512,512]{1,0:T(8,128)S(1)}, bf16[3,512,768]{2,1,0:T(8,128)(2,1)S(1)}, bf16[3,512,768]{2,1,0:T(8,128)(2,1)S(1)}) custom-call(s32[1]{0:T(128)} %constant.172.clone.1.groups.places, bf16[768,2560]{1,0:T(8,128)(2,1)S(1)} %pad_maximum_fusion.2.refs_0_, ...), custom_call_target="tpu_custom_call" | custom-call | flops 1000 | bytes 1000 | tf_op jit(solution)/shard_map/wide_both/pallas_call | solution.py:580
  241.6 9.7 %collective-permute-done.39.refs_4_ = bf16[3,512,768]{2,1,0:T(8,128)(2,1)S(1)} collective-permute-done((bf16[3,512,768]{2,1,0:T(8,128)(2,1)S(1)}, bf16[3,512,768]{2,1,0:T(8,128)(2,1)S(1)}, u32[]{:S(2)}, u32[]{:S(2)}) %collective-permute-start.39) | collective-permute-done | bytes 2359328 | tf_op jit(solution)/shard_map/ppermute | solution.py:81
  266.6 15.1 %wide_both.3 = (bf16[512,1024]{1,0:T(8,128)(2,1)}, f32[512,1024]{1,0:T(8,128)S(1)}, f32[512,512]{1,0:T(8,128)S(1)}, bf16[3,512,768]{2,1,0:T(8,128)(2,1)S(1)}, bf16[3,512,768]{2,1,0:T(8,128)(2,1)S(1)}) custom-call(s32[1]{0:T(128)} %constant.172.clone.1.groups.places, bf16[768,2560]{1,0:T(8,128)(2,1)S(1)} %pad_maximum_fusion.3.refs_0_, ...), custom_call_target="tpu_custom_call" | custom-call | flops 1000 | bytes 1000 | tf_op jit(solution)/shard_map/wide_both/pallas_call | solution.py:580
  281.7 6.5 %collective-permute-done.40 = bf16[384,2560]{1,0:T(8,128)(2,1)} collective-permute-done((bf16[384,2560]{1,0:T(8,128)(2,1)}, bf16[384,2560]{1,0:T(8,128)(2,1)}, u32[]{:S(2)}, u32[]{:S(2)}) %collective-permute-start.40) | collective-permute-done | bytes 1966112 | tf_op jit(solution)/shard_map/ppermute | solution.py:81
  306.7 6.4 %grads.5 = bf16[768,2560]{1,0:T(8,128)(2,1)S(1)} custom-call(s32[1]{0:T(128)} %constant.172.clone.1.groups.places, bf16[3,512,768]{2,1,0:T(8,128)(2,1)S(1)} %get-tuple-element.273.refs_0_, bf16[512,1024]{1,0:T(8,128)(2,1)S(1)} %get-tuple-element.248.refs_2_.refs_1_.normed_ref, bf16[512,1024]{1,0:T(8,128)(2,1)S(1)} %copy-done.4, ...), custom_call_target="tpu_custom_call" | custom-call | flops 1000 | bytes 1000 | tf_op jit(solution)/shard_map/grads/pallas_call | solution.py:632
  342.8 10.2 %wide_back.2 = (f32[512,1024]{1,0:T(8,128)S(1)}, f32[512,512]{1,0:T(8,128)S(1)}, bf16[3,512,768]{2,1,0:T(8,128)(2,1)S(1)}, bf16[3,512,768]{2,1,0:T(8,128)(2,1)}) custom-call(s32[1]{0:T(128)} %constant.172.clone.1.groups.places, bf16[768,2560]{1,0:T(8,128)(2,1)S(1)} %copy-done.1, bf16[768,2560]{1,0:T(8,128)(2,1)S(1)} %copy-done.13, ...), custom_call_target="tpu_custom_call" | custom-call | flops 1000 | bytes 1000 | tf_op jit(solution)/shard_map/wide_back/pallas_call | solution.py:580
  366.5 12.0 %wide_back.3 = (f32[512,1024]{1,0:T(8,128)S(1)}, f32[512,512]{1,0:T(8,128)S(1)}, bf16[3,512,768]{2,1,0:T(8,128)(2,1)S(1)}, bf16[3,512,768]{2,1,0:T(8,128)(2,1)}) custom-call(s32[1]{0:T(128)} %constant.172.clone.1.groups.places, bf16[768,2560]{1,0:T(8,128)(2,1)S(1)} %copy-done.3, bf16[768,2560]{1,0:T(8,128)(2,1)} %copy-done.14, ...), custom_call_target="tpu_custom_call" | custom-call | flops 1000 | bytes 1000 | tf_op jit(solution)/shard_map/wide_back/pallas_call | solution.py:580
  388.8 7.1 %grads.6 = bf16[768,2944]{1,0:T(8,128)(2,1)S(1)} custom-call(s32[1]{0:T(128)} %constant.172.clone.1.groups.places, bf16[3,512,768]{2,1,0:T(8,128)(2,1)S(1)} %copy-done.48, bf16[512,1024]{1,0:T(8,128)(2,1)S(1)} %get-tuple-element.218.refs_2_.refs_1_.normed_ref, bf16[512,1024]{1,0:T(8,128)(2,1)S(1)} %get-tuple-element.289.refs_4_.refs_2_, ...), custom_call_target="tpu_custom_call" | custom-call | flops 1000 | bytes 1000 | tf_op jit(solution)/shard_map/grads/pallas_call | solution.py:632
  418.8 13.2 %collective-permute-done.62 = f32[2,512]{1,0:T(2,128)S(1)} collective-permute-done((f32[2,512]{1,0:T(2,128)S(1)}, f32[2,512]{1,0:T(2,128)S(1)}, u32[]{:S(2)}, u32[]{:S(2)}) %collective-permute-start.62) | collective-permute-done | bytes 4128 | tf_op jit(solution)/shard_map/ppermute | solution.py:81
  442.8 6.8 %leave.3 = (f32[512,1024]{1,0:T(8,128)}, bf16[512,1024]{1,0:T(8,128)(2,1)}, bf16[256,1152]{1,0:T(8,128)(2,1)S(1)}, bf16[256,1152]{1,0:T(8,128)(2,1)S(1)}) custom-call(s32[3]{0:T(128)S(1)} %broadcast_subtract_fusion.scal, f32[8,1]{1,0:T(8,128)S(1)} %convert_select_fusion.1.hops_ref, f32[8,512]{1,0:T(8,128)S(1)} %pad_maximum_fusion.25.firsts_ref, ...), custom_call_target="tpu_custom_call" | custom-call | flops 1000 | bytes 1000 | tf_op jit(solution)/shard_map/leave/pallas_call | solution.py:407
  449.7 17.7 %collective-permute-done.64 = bf16[192,2944]{1,0:T(8,128)(2,1)S(1)} collective-permute-done((bf16[192,2944]{1,0:T(8,128)(2,1)S(1)}, bf16[192,2944]{1,0:T(8,128)(2,1)S(1)}, u32[]{:S(2)}, u32[]{:S(2)}) %collective-permute-start.64) | collective-permute-done | bytes 1130528 | tf_op jit(solution)/shard_map/ppermute | solution.py:81
  476.3 6.9 %collective-permute-done.66 = bf16[48,2944]{1,0:T(8,128)(2,1)S(1)} collective-permute-done((bf16[48,2944]{1,0:T(8,128)(2,1)S(1)}, bf16[48,2944]{1,0:T(8,128)(2,1)S(1)}, u32[]{:S(2)}, u32[]{:S(2)}) %collective-permute-start.66) | collective-permute-done | bytes 282656 | tf_op jit(solution)/shard_map/ppermute | solution.py:81
  492.1 7.5 %collective-permute-done.71 = bf16[128,1152]{1,0:T(8,128)(2,1)S(1)} collective-permute-done((bf16[128,1152]{1,0:T(8,128)(2,1)S(1)}, bf16[128,1152]{1,0:T(8,128)(2,1)S(1)}, u32[]{:S(2)}, u32[]{:S(2)}) %collective-permute-start.71) | collective-permute-done | bytes 294944 | tf_op jit(solution)/shard_map/ppermute | solution.py:81
  523.9 9.2 %collective-permute-done.77 = bf16[48,2560]{1,0:T(8,128)(2,1)} collective-permute-done((bf16[48,2560]{1,0:T(8,128)(2,1)}, bf16[48,2560]{1,0:T(8,128)(2,1)}, u32[]{:S(2)}, u32[]{:S(2)}) %collective-permute-start.77) | collective-permute-done | bytes 245792 | tf_op jit(solution)/shard_map/ppermute | solution.py:81
  (475 shorter events, 297.2 us)
Async XLA Ops:
  50.7 24.0 %collective-permute-start.9 = (bf16[192,2560]{1,0:T(8,128)(2,1)S(1)}, bf16[192,2560]{1,0:T(8,128)(2,1)S(1)}, u32[]{:S(2)}, u32[]{:S(2)}) collective-permute-start(bf16[192,2560]{1,0:T(8,128)(2,1)S(1)} %pad_maximum_fusion.9), channel_id=1, source_target_pairs={{0,1},{2,3},{4,5},{6,7},{1,0},{3,2},{5,4},{7,6},{8,24},{10,26},{12... | collective-permute-start | bytes 2949128 | tf_op jit(solution)/shard_map/ppermute | solution.py:81
  77.6 24.9 %collective-permute-start.14 = (bf16[384,2560]{1,0:T(8,128)(2,1)}, bf16[384,2560]{1,0:T(8,128)(2,1)}, u32[]{:S(2)}, u32[]{:S(2)}) collective-permute-start(bf16[384,2560]{1,0:T(8,128)(2,1)} %pad_maximum_fusion.4), channel_id=1, source_target_pairs={{0,16},{2,18},{4,20},{6,22},{1,17},{3,19},{5,21},{7,23},{8,9},{10,... | collective-permute-start | bytes 5898248 | tf_op jit(solution)/shard_map/ppermute | solution.py:81
  119.4 25.0 %collective-permute-start.20 = (bf16[384,2560]{1,0:T(8,128)(2,1)S(1)}, bf16[384,2560]{1,0:T(8,128)(2,1)S(1)}, u32[]{:S(2)}, u32[]{:S(2)}) collective-permute-start(bf16[384,2560]{1,0:T(8,128)(2,1)S(1)} %pad_maximum_fusion.5), channel_id=1, source_target_pairs={{0,16},{2,18},{4,20},{6,22},{1,17},{3,19},{5,21},{7,23},{8,9},{10,... | collective-permute-start | bytes 5898248 | tf_op jit(solution)/shard_map/ppermute | solution.py:81
  121.7 22.6 %collective-permute-start.22 = (bf16[48,2560]{1,0:T(8,128)(2,1)S(1)}, bf16[48,2560]{1,0:T(8,128)(2,1)S(1)}, u32[]{:S(2)}, u32[]{:S(2)}) collective-permute-start(bf16[48,2560]{1,0:T(8,128)(2,1)S(1)} %copy-done.85), channel_id=1, source_target_pairs={{0,6},{2,4},{4,2},{6,0},{1,7},{3,5},{5,3},{7,1},{8,14},{10,12},{12... | collective-permute-start | bytes 737288 | tf_op jit(solution)/shard_map/ppermute | solution.py:81
  159.1 25.1 %collective-permute-start.26 = (bf16[384,2560]{1,0:T(8,128)(2,1)S(1)}, bf16[384,2560]{1,0:T(8,128)(2,1)S(1)}, u32[]{:S(2)}, u32[]{:S(2)}) collective-permute-start(bf16[384,2560]{1,0:T(8,128)(2,1)S(1)} %pad_maximum_fusion.6), channel_id=1, source_target_pairs={{0,16},{2,18},{4,20},{6,22},{1,17},{3,19},{5,21},{7,23},{8,9},{10,... | collective-permute-start | bytes 5898248 | tf_op jit(solution)/shard_map/ppermute | solution.py:81
  161.1 23.0 %collective-permute-start.28 = (bf16[48,2560]{1,0:T(8,128)(2,1)S(1)}, bf16[48,2560]{1,0:T(8,128)(2,1)S(1)}, u32[]{:S(2)}, u32[]{:S(2)}) collective-permute-start(bf16[48,2560]{1,0:T(8,128)(2,1)S(1)} %copy-done.84), channel_id=1, source_target_pairs={{0,6},{2,4},{4,2},{6,0},{1,7},{3,5},{5,3},{7,1},{8,14},{10,12},{12... | collective-permute-start | bytes 737288 | tf_op jit(solution)/shard_map/ppermute | solution.py:81
  184.4 26.0 %collective-permute-start.29 = (bf16[768,2560]{1,0:T(8,128)(2,1)S(1)}, bf16[768,2560]{1,0:T(8,128)(2,1)S(1)}, u32[]{:S(2)}, u32[]{:S(2)}) collective-permute-start(bf16[768,2560]{1,0:T(8,128)(2,1)S(1)} %pad_maximum_fusion.2.refs_0_), channel_id=1, source_target_pairs={{0,8},{2,10},{4,12},{6,14},{1,9},{3,11},{5,13},{7,15},{8,0},{10,2}... | collective-permute-start | bytes 11796488 | tf_op jit(solution)/shard_map/ppermute | solution.py:81
  184.5 24.9 %collective-permute-start.30 = (bf16[192,2560]{1,0:T(8,128)(2,1)S(1)}, bf16[192,2560]{1,0:T(8,128)(2,1)S(1)}, u32[]{:S(2)}, u32[]{:S(2)}) collective-permute-start(bf16[192,2560]{1,0:T(8,128)(2,1)S(1)} %pad_maximum_fusion.12), channel_id=1, source_target_pairs={{0,1},{2,3},{4,5},{6,7},{1,0},{3,2},{5,4},{7,6},{8,24},{10,26},{12... | collective-permute-start | bytes 2949128 | tf_op jit(solution)/shard_map/ppermute | solution.py:81
  210.4 27.3 %collective-permute-start.34 = (bf16[384,2560]{1,0:T(8,128)(2,1)S(1)}, bf16[384,2560]{1,0:T(8,128)(2,1)S(1)}, u32[]{:S(2)}, u32[]{:S(2)}) collective-permute-start(bf16[384,2560]{1,0:T(8,128)(2,1)S(1)} %pad_maximum_fusion.7), channel_id=1, source_target_pairs={{0,16},{2,18},{4,20},{6,22},{1,17},{3,19},{5,21},{7,23},{8,9},{10,... | collective-permute-start | bytes 5898248 | tf_op jit(solution)/shard_map/ppermute | solution.py:81
  211.2 28.8 %collective-permute-start.36 = (bf16[512,1024]{1,0:T(8,128)(2,1)S(1)}, bf16[512,1024]{1,0:T(8,128)(2,1)S(1)}, u32[]{:S(2)}, u32[]{:S(2)}) collective-permute-start(bf16[512,1024]{1,0:T(8,128)(2,1)S(1)} %copy-done.4), channel_id=1, source_target_pairs={{0,8},{2,10},{4,12},{6,14},{1,9},{3,11},{5,13},{7,15},{8,0},{10,2}... | collective-permute-start | bytes 3145736 | tf_op jit(solution)/shard_map/ppermute | solution.py:81
  211.2 29.8 %collective-permute-start.35 = (bf16[512,1024]{1,0:T(8,128)(2,1)S(1)}, bf16[512,1024]{1,0:T(8,128)(2,1)}, u32[]{:S(2)}, u32[]{:S(2)}) collective-permute-start(bf16[512,1024]{1,0:T(8,128)(2,1)S(1)} %get-tuple-element.248.refs_2_.refs_1_.normed_ref), channel_id=1, source_target_pairs={{0,8},{2,10},{4,12},{6,14},{1,9},{3,11},{5,13},{7,15},{8,0},{10,2}... | collective-permute-start | bytes 3145736 | tf_op jit(solution)/shard_map/ppermute | solution.py:81
  211.7 29.3 %collective-permute-start.37 = (bf16[512,512]{1,0:T(8,128)(2,1)S(1)}, bf16[512,512]{1,0:T(8,128)(2,1)S(1)}, u32[]{:S(2)}, u32[]{:S(2)}) collective-permute-start(bf16[512,512]{1,0:T(8,128)(2,1)S(1)} %get-tuple-element.249.refs_3_), channel_id=1, source_target_pairs={{0,8},{2,10},{4,12},{6,14},{1,9},{3,11},{5,13},{7,15},{8,0},{10,2}... | collective-permute-start | bytes 1572872 | tf_op jit(solution)/shard_map/ppermute | solution.py:81
  263.3 24.9 %collective-permute-start.40 = (bf16[384,2560]{1,0:T(8,128)(2,1)}, bf16[384,2560]{1,0:T(8,128)(2,1)}, u32[]{:S(2)}, u32[]{:S(2)}) collective-permute-start(bf16[384,2560]{1,0:T(8,128)(2,1)} %slice.306), channel_id=1, source_target_pairs={{0,16},{2,18},{4,20},{6,22},{1,17},{3,19},{5,21},{7,23},{8,9},{10,... | collective-permute-start | bytes 5898248 | tf_op jit(solution)/shard_map/ppermute | solution.py:81
  316.1 41.5 %collective-permute-start.45 = (bf16[192,2560]{1,0:T(8,128)(2,1)}, bf16[192,2560]{1,0:T(8,128)(2,1)}, u32[]{:S(2)}, u32[]{:S(2)}) collective-permute-start(bf16[192,2560]{1,0:T(8,128)(2,1)} %slice.308), channel_id=1, source_target_pairs={{0,1},{2,3},{4,5},{6,7},{1,0},{3,2},{5,4},{7,6},{8,24},{10,26},{12... | collective-permute-start | bytes 2949128 | tf_op jit(solution)/shard_map/ppermute | solution.py:81
  354.3 33.2 %collective-permute-start.54 = (bf16[3,512,768]{2,1,0:T(8,128)(2,1)}, bf16[3,512,768]{2,1,0:T(8,128)(2,1)}, u32[]{:S(2)}, u32[]{:S(2)}) collective-permute-start(bf16[3,512,768]{2,1,0:T(8,128)(2,1)} %get-tuple-element.297), channel_id=1, source_target_pairs={{0,8},{2,10},{4,12},{6,14},{1,9},{3,11},{5,13},{7,15},{8,0},{10,2}... | collective-permute-start | bytes 7077896 | tf_op jit(solution)/shard_map/ppermute | solution.py:81
  356.5 27.6 %collective-permute-start.49 = (bf16[384,2560]{1,0:T(8,128)(2,1)}, bf16[384,2560]{1,0:T(8,128)(2,1)}, u32[]{:S(2)}, u32[]{:S(2)}) collective-permute-start(bf16[384,2560]{1,0:T(8,128)(2,1)} %slice.314), channel_id=1, source_target_pairs={{0,16},{2,18},{4,20},{6,22},{1,17},{3,19},{5,21},{7,23},{8,9},{10,... | collective-permute-start | bytes 5898248 | tf_op jit(solution)/shard_map/ppermute | solution.py:81
  361.4 22.5 %collective-permute-start.48 = (bf16[48,2560]{1,0:T(8,128)(2,1)S(1)}, bf16[48,2560]{1,0:T(8,128)(2,1)S(1)}, u32[]{:S(2)}, u32[]{:S(2)}) collective-permute-start(bf16[48,2560]{1,0:T(8,128)(2,1)S(1)} %get-tuple-element.375), channel_id=1, source_target_pairs={{0,6},{2,4},{4,2},{6,0},{1,7},{3,5},{5,3},{7,1},{8,14},{10,12},{12... | collective-permute-start | bytes 737288 | tf_op jit(solution)/shard_map/ppermute | solution.py:81
  402.3 36.5 %collective-permute-start.57 = (bf16[384,2944]{1,0:T(8,128)(2,1)S(1)}, bf16[384,2944]{1,0:T(8,128)(2,1)S(1)}, u32[]{:S(2)}, u32[]{:S(2)}) collective-permute-start(bf16[384,2944]{1,0:T(8,128)(2,1)S(1)} %slice.318), channel_id=1, source_target_pairs={{0,16},{2,18},{4,20},{6,22},{1,17},{3,19},{5,21},{7,23},{8,9},{10,... | collective-permute-start | bytes 6782984 | tf_op jit(solution)/shard_map/ppermute | solution.py:81
  414.2 22.6 %collective-permute-start.58 = (bf16[48,2560]{1,0:T(8,128)(2,1)S(1)}, bf16[48,2560]{1,0:T(8,128)(2,1)S(1)}, u32[]{:S(2)}, u32[]{:S(2)}) collective-permute-start(bf16[48,2560]{1,0:T(8,128)(2,1)S(1)} %get-tuple-element.371), channel_id=1, source_target_pairs={{0,2},{2,0},{4,6},{6,4},{1,3},{3,1},{5,7},{7,5},{8,10},{10,8},{12,... | collective-permute-start | bytes 737288 | tf_op jit(solution)/shard_map/ppermute | solution.py:81
  414.3 22.5 %collective-permute-start.59 = (bf16[48,2560]{1,0:T(8,128)(2,1)S(1)}, bf16[48,2560]{1,0:T(8,128)(2,1)S(1)}, u32[]{:S(2)}, u32[]{:S(2)}) collective-permute-start(bf16[48,2560]{1,0:T(8,128)(2,1)S(1)} %get-tuple-element.373), channel_id=1, source_target_pairs={{0,4},{2,6},{4,0},{6,2},{1,5},{3,7},{5,1},{7,3},{8,12},{10,14},{12... | collective-permute-start | bytes 737288 | tf_op jit(solution)/shard_map/ppermute | solution.py:81
  416.2 22.5 %collective-permute-start.60 = (bf16[48,2560]{1,0:T(8,128)(2,1)S(1)}, bf16[48,2560]{1,0:T(8,128)(2,1)S(1)}, u32[]{:S(2)}, u32[]{:S(2)}) collective-permute-start(bf16[48,2560]{1,0:T(8,128)(2,1)S(1)} %get-tuple-element.372), channel_id=1, source_target_pairs={{0,6},{2,4},{4,2},{6,0},{1,7},{3,5},{5,3},{7,1},{8,14},{10,12},{12... | collective-permute-start | bytes 737288 | tf_op jit(solution)/shard_map/ppermute | solution.py:81
  439.5 27.9 %collective-permute-start.64 = (bf16[192,2944]{1,0:T(8,128)(2,1)S(1)}, bf16[192,2944]{1,0:T(8,128)(2,1)S(1)}, u32[]{:S(2)}, u32[]{:S(2)}) collective-permute-start(bf16[192,2944]{1,0:T(8,128)(2,1)S(1)} %slice.324), channel_id=1, source_target_pairs={{0,1},{2,3},{4,5},{6,7},{1,0},{3,2},{5,4},{7,6},{8,24},{10,26},{12... | collective-permute-start | bytes 3391496 | tf_op jit(solution)/shard_map/ppermute | solution.py:81
  440.7 48.1 %collective-permute-start.68 = (bf16[384,2560]{1,0:T(8,128)(2,1)S(1)}, bf16[384,2560]{1,0:T(8,128)(2,1)S(1)}, u32[]{:S(2)}, u32[]{:S(2)}) collective-permute-start(bf16[384,2560]{1,0:T(8,128)(2,1)S(1)} %slice.330), channel_id=1, source_target_pairs={{0,16},{2,18},{4,20},{6,22},{1,17},{3,19},{5,21},{7,23},{8,9},{10,... | collective-permute-start | bytes 5898248 | tf_op jit(solution)/shard_map/ppermute | solution.py:81
  516.6 21.3 %collective-permute-start.78 = (bf16[48,2560]{1,0:T(8,128)(2,1)S(1)}, bf16[48,2560]{1,0:T(8,128)(2,1)}, u32[]{:S(2)}, u32[]{:S(2)}) collective-permute-start(bf16[48,2560]{1,0:T(8,128)(2,1)S(1)} %get-tuple-element.369), channel_id=1, source_target_pairs={{0,6},{2,4},{4,2},{6,0},{1,7},{3,5},{5,3},{7,1},{8,14},{10,12},{12... | collective-permute-start | bytes 737288 | tf_op jit(solution)/shard_map/ppermute | solution.py:81
  (146 other events, 1504.1 us)

commit v4 on v3

--- a/solution.py
+++ b/solution.py
@@ -14,7 +14,7 @@
 AXES = ("dp", "seq")
 BF = jnp.bfloat16
 F32 = jnp.float32
-VMEM_LIMIT = 30 << 20
+VMEM_LIMIT = 24 << 20
 C0 = math.sqrt(2.0 / math.pi)
 C1 = 0.044715
 SMALL = 7
@@ -645,13 +645,15 @@
     )(jnp.zeros((1,), jnp.int32) if places is None else places, *[array for _, array, _ in ins])
 
 
-def seq_gather(lay, vector):
-    held, k = vector, 1
+def seq_step(lay, held, k):
+    pairs = [(d * lay.seq + s, d * lay.seq + (s ^ k)) for d in range(lay.dp) for s in range(lay.seq)]
+    return cat(held, permute(held, pairs))
+
+
+def seq_rest(lay, held):
+    k = 2
     while k < lay.seq:
-        pairs = [
-            (d * lay.seq + s, d * lay.seq + (s ^ k)) for d in range(lay.dp) for s in range(lay.seq)
-        ]
-        held = cat(held, permute(held, pairs))
+        held = seq_step(lay, held, k)
         k *= 2
     return held
 
@@ -750,8 +752,8 @@
     pulled = pulls(shard_b, 0)
     wr_all, rows_all = params_call(key, head_own, head_other, width, chan)
     entered = enter_call(0, near, tokens, rows_all, wr_all)
-    lasts = seq_gather(lay, entered[3])
-    plane_a, shard_b, pulled, entered, lasts = fence(plane_a, shard_b, pulled, entered, lasts)
+    held = seq_step(lay, entered[3], 1)
+    plane_a, shard_b, pulled, entered, held = fence(plane_a, shard_b, pulled, entered, held)
 
     def enter(layer, stream, entered, lasts):
         normed, pre_reduce, local_states, _ = entered
@@ -759,10 +761,6 @@
             layer, near, hops_fore, lasts, prev_state[layer], rows_all, pre_reduce, local_states
         )
         return dict(stream=stream, normed=normed, pre_reduce=pre_reduce, states=states, state_in=state_in, mixed=mixed)
-
-    def turn_back(layer, sums):
-        back_local, first_row = back_scan_call(layer, near, sums[1], rows_all)
-        return back_local, seq_gather(lay, first_row)
 
     def leave(layer, kept, sums, reached, upstream):
         upstream, low, *head = leave_call(
@@ -790,7 +788,7 @@
         )
         return [d_normed, d_mixed], mine, peers
 
-    k0 = enter(0, tokens, entered, lasts)
+    k0 = enter(0, tokens, entered, seq_rest(lay, held))
     a_own = stage(plane_a, lay.p2)
     pulled |= pulls(shard_b, 1, 2)
     a_own, line_b, k0, shard_c = fence(a_own, line_of(shard_b, pulled), k0, shard_c)
@@ -812,8 +810,9 @@
     entered = enter_call(1, near, acc, rows_all, wr_all)
     c_own, line_d, acc, entered = fence(c_own, line_of(shard_d, pulled), acc, entered)
     (c_other,) = swap(c_own)
-    plane_d = stage(line_d, lay.p1)
-    k1 = enter(1, acc, entered, seq_gather(lay, entered[3]))
+    held = seq_step(lay, entered[3], 1)
+    plane_d = stage(after(line_d, held), lay.p1)
+    k1 = enter(1, acc, entered, seq_rest(lay, held))
     c_own, c_other, plane_d, k1 = fence(c_own, c_other, plane_d, k1)
 
     d_own = stage(plane_d, lay.p2)
@@ -830,13 +829,16 @@
     a1, sums, b1_own, b1_peer = fence(a1, sums, b1_own, b1_peer)
 
     (b1_peer,) = swap(b1_peer)
-    reached = turn_back(1, sums)
+    back_local, first_row = back_scan_call(1, near, sums[1], rows_all)
+    held = seq_step(lay, first_row, 1)
+    a1 = fold(after(a1, held), lay.p1)
     b1 = grads_call(b1_own, b1_peer, ins_1, peer_1)
-    a1, b1, sums, reached = fence(a1, b1, sums, reached)
+    reached = back_local, seq_rest(lay, after(held, b1))
     upstream, low, head_1 = leave(1, k1, sums, reached, cotangent)
+    a1, b1, upstream, low, head_1 = fence(a1, b1, upstream, low, head_1)
 
     b1 = fold(b1, lay.p2)
-    a1_done = fold(fold(a1, lay.p1), lay.q, F32)
+    a1_done = fold(a1, lay.q, F32)
     peer_0 = swap(k0["normed"], low, k0["mixed"])
     (head_peer,) = swap(head_1[1])
     sums, a0_own, a0_peer = back(a_own, a_other, save_a, None)
@@ -850,25 +852,34 @@
     b1 = fold(b1, lay.p1)
     (b0_peer,) = swap(b0_peer)
     a0 = grads_call(a0_own, a0_peer, ins_0, peer_0, heads=(head_1[0], head_peer), head_rows=small_rows)
-    b1, a0, sums, b0_own, b0_peer = fence(b1, a0, sums, b0_own, b0_peer)
-
-    a0 = fold(a0, lay.p2)
-    b1_done = fold(b1, lay.q, F32)
+    back_local, first_row = back_scan_call(0, near, sums[1], rows_all)
+    b1, a0, sums, b0_own, b0_peer, back_local, first_row = fence(
+        b1, a0, sums, b0_own, b0_peer, back_local, first_row
+    )
+
+    held = seq_step(lay, first_row, 1)
+    a0 = fold(after(a0, held), lay.p2)
     b0 = grads_call(b0_own, b0_peer, ins_0, peer_0)
-    sums[1] = after(sums[1], b0)
-    reached = turn_back(0, sums)
-    a0, b0, b1_done, sums, reached = fence(a0, b0, b1_done, sums, reached)
+    _, input_grad, (head_own, head_other) = leave(0, k0, sums, (back_local, seq_rest(lay, held)), upstream)
+    a0, b0, b1, head_own, head_other = fence(a0, b0, b1, head_own, head_other)
+
     a0 = fold(a0, lay.p1)
-    _, input_grad, (head_own, head_other) = leave(0, k0, sums, reached, upstream)
-    a0, head_own, head_other = fence(a0, head_own, head_other)
+    size = b1.shape[0] // lay.nq
+    cut = (2 * lay.nq + 2) // 3
+    b1_parts = [b1[k * size : (k + 1) * size] for k in range(lay.nq)]
+    b1_parts[1:cut] = [permute(b1_parts[k], lay.q[k]) for k in range(1, cut)]
+    h0 = add_parts([head_own, *swap(head_other)], BF)
+    a0, b0, b1_parts, h0 = fence(a0, b0, b1_parts, h0)
+
     a0_done = fold(a0, lay.q, F32)
-    b0 = fold(b0, lay.p2)
-    h0 = add_parts([head_own, *swap(head_other)], BF)
-    a0_done, b0, h0 = fence(a0_done, b0, h0)
-    b0, h0 = fold(b0, lay.p1), fold(h0, lay.p2)
-    b0, h0 = fence(b0, h0)
-    b0_done = fold(b0, lay.q, F32)
-    h0_done = fold(fold(h0, lay.p1), lay.q, F32)
+    b0, h0 = fold(b0, lay.p2), fold(h0, lay.p2)
+    a0_done, b0, b1_parts, h0 = fence(a0_done, b0, b1_parts, h0)
+
+    b1_parts[cut:] = [permute(b1_parts[k], lay.q[k]) for k in range(cut, lay.nq)]
+    b1_done = add_parts(b1_parts, F32)
+    b0, h0 = fold(b0, lay.p1), fold(h0, lay.p1)
+    b1_done, b0, h0 = fence(b1_done, b0, h0)
+    b0_done, h0_done = fold(b0, lay.q, F32), fold(h0, lay.q, F32)
 
     h1_done = close_lanes(a0_done[:, lanes:], small_rows)
     grads = [cat(a0_done[:, :lanes], b0_done), cat(a1_done, b1_done)]

time: 549 us -> 514 us (0.936)
  waiting for transfers between devices: 232 us -> 208 us
  Pallas kernels: 143 us -> 129 us
  local copies, waits for them, and re-layouts: 63.7 us -> 50.1 us
  starting transfers between devices: 75.5 us -> 85.6 us
    ppermute x79, waiting for transfers between devices: 232 us -> 208 us  [permute(): return lax.ppermute(array, AXES, pairs)]
    unnamed x187 -> x171, local copies, waits for them, and re-layouts: 49 us -> 35.5 us
    pallas_call x6, Pallas kernels: 77.9 us -> 65.9 us  [wide_call(): pl.pallas_call(functools.partial(wide_kernel, names, mode, blocks, (width...]
    ppermute x79, starting transfers between devices: 75.5 us -> 85.6 us  [permute(): return lax.ppermute(array, AXES, pairs)]
  transfers between devices with their start and end apart: 79 -> 79, of which waited for: 43 -> 43; matrix products, arithmetic and copies ran while one was open for 4% -> 5% of each run, Pallas kernels for 25% -> 24%
where the time goes in v4:
time: 514 us; the launch traced here: 504 us
  waiting for transfers between devices  208 us (40%)
  Pallas kernels  129 us (25%)
  starting transfers between devices  85.6 us (17%)
  local copies, waits for them, and re-layouts  50.1 us (10%)
  other arithmetic  28.5 us (6%)
    ppermute x79, waiting for transfers between devices, permute(): return lax.ppermute(array, AXES, pairs)  208 us
    ppermute x79, starting transfers between devices, permute(): return lax.ppermute(array, AXES, pairs)  85.6 us
    pallas_call x6, Pallas kernels, wide_call(): pl.pallas_call(functools.partial(wide_kernel, names, mode, blocks, (width...  65.9 us
    unnamed x171, local copies, waits for them, and re-layouts  35.5 us
    pallas_call x4, Pallas kernels, grads_call(): pl.pallas_call(functools.partial(grads_kernel, names, head_rows, sub), gr...  22.8 us
    pallas_call x2, Pallas kernels, leave_call(): pl.pallas_call(functools.partial(leave_kernel, starts.shape[0], layer), o...  12.8 us
  transfers between devices with their start and end apart: 79, of which 43 were waited for; matrix products, arithmetic and copies ran while one was open for 5% of the time, Pallas kernels for 24%

profile of v4, /device:TPU:8, one launch (start us, length us, event | category | flops | bytes accessed | tf_op | source)
XLA Modules:
  0.0 503.9 jit_solution(18400376244266189555)
XLA Ops:
  26.7 6.7 %collective-permute-done.5 = bf16[256,1152]{1,0:T(8,128)(2,1)S(1)} collective-permute-done((bf16[256,1152]{1,0:T(8,128)(2,1)S(1)}, bf16[256,1152]{1,0:T(8,128)(2,1)S(1)}, u32[]{:S(2)}, u32[]{:S(2)}) %collective-permute-start.5) | collective-permute-done | bytes 589856 | tf_op jit(solution)/shard_map/ppermute | solution.py:81
  36.2 12.3 %collective-permute-done.8 = bf16[48,2560]{1,0:T(8,128)(2,1)S(1)} collective-permute-done((bf16[48,2560]{1,0:T(8,128)(2,1)S(1)}, bf16[48,2560]{1,0:T(8,128)(2,1)S(1)}, u32[]{:S(2)}, u32[]{:S(2)}) %collective-permute-start.8) | collective-permute-done | bytes 245792 | tf_op jit(solution)/shard_map/ppermute | solution.py:81
  80.1 16.3 %collective-permute-done.16 = f32[4,512]{1,0:T(4,128)S(1)} collective-permute-done((f32[4,512]{1,0:T(4,128)S(1)}, f32[4,512]{1,0:T(4,128)S(1)}, u32[]{:S(2)}, u32[]{:S(2)}) %collective-permute-start.16) | collective-permute-done | bytes 8224 | tf_op jit(solution)/shard_map/ppermute | solution.py:81
  107.8 11.3 %collective-permute-done.18 = bf16[192,2560]{1,0:T(8,128)(2,1)S(1)} collective-permute-done((bf16[192,2560]{1,0:T(8,128)(2,1)S(1)}, bf16[192,2560]{1,0:T(8,128)(2,1)S(1)}, u32[]{:S(2)}, u32[]{:S(2)}) %collective-permute-start.18) | collective-permute-done | bytes 983072 | tf_op jit(solution)/shard_map/ppermute | solution.py:81
  126.2 7.3 %wide_fore.2 = (f32[512,1536]{1,0:T(8,128)S(1)}, f32[512,1536]{1,0:T(8,128)S(1)}, f32[512,1024]{1,0:T(8,128)S(1)}) custom-call(s32[1]{0:T(128)} %constant.172.clone.1.groups.places, bf16[768,2560]{1,0:T(8,128)(2,1)S(1)} %pad_maximum_fusion.refs_0_, bf16[768,2560]{1,0:T(8,128)(2,1)S(1)} %collective-permute-done.17.refs_1_, ...), custom_call_target="tpu_custom_call" | custom-call | flops 1000 | bytes 1000 | tf_op jit(solution)/shard_map/wide_fore/pallas_call | solution.py:580
  138.1 6.2 %collective-permute-done.22 = bf16[48,2560]{1,0:T(8,128)(2,1)S(1)} collective-permute-done((bf16[48,2560]{1,0:T(8,128)(2,1)S(1)}, bf16[48,2560]{1,0:T(8,128)(2,1)S(1)}, u32[]{:S(2)}, u32[]{:S(2)}) %collective-permute-start.22) | collective-permute-done | bytes 245792 | tf_op jit(solution)/shard_map/ppermute | solution.py:81
  148.0 10.9 %collective-permute-done.24 = bf16[192,2560]{1,0:T(8,128)(2,1)S(1)} collective-permute-done((bf16[192,2560]{1,0:T(8,128)(2,1)S(1)}, bf16[192,2560]{1,0:T(8,128)(2,1)S(1)}, u32[]{:S(2)}, u32[]{:S(2)}) %collective-permute-start.24) | collective-permute-done | bytes 983072 | tf_op jit(solution)/shard_map/ppermute | solution.py:81
  165.6 7.3 %wide_fore.3 = (f32[512,1536]{1,0:T(8,128)S(1)}, f32[512,1536]{1,0:T(8,128)S(1)}, f32[512,1024]{1,0:T(8,128)S(1)}) custom-call(s32[1]{0:T(128)} %constant.172.clone.1.groups.places, bf16[768,2560]{1,0:T(8,128)(2,1)S(1)} %pad_maximum_fusion.1.refs_0_, bf16[768,2560]{1,0:T(8,128)(2,1)S(1)} %collective-permute-done.23.refs_1_, ...), custom_call_target="tpu_custom_call" | custom-call | flops 1000 | bytes 1000 | tf_op jit(solution)/shard_map/wide_fore/pallas_call | solution.py:580
  205.3 14.5 %wide_both.2 = (f32[512,1024]{1,0:T(8,128)S(1)}, f32[512,1024]{1,0:T(8,128)S(1)}, f32[512,512]{1,0:T(8,128)S(1)}, bf16[3,512,768]{2,1,0:T(8,128)(2,1)S(1)}, bf16[3,512,768]{2,1,0:T(8,128)(2,1)S(1)}) custom-call(s32[1]{0:T(128)} %constant.172.clone.1.groups.places, bf16[768,2560]{1,0:T(8,128)(2,1)S(1)} %pad_maximum_fusion.2.refs_0_, ...), custom_call_target="tpu_custom_call" | custom-call | flops 1000 | bytes 1000 | tf_op jit(solution)/shard_map/wide_both/pallas_call | solution.py:580
  221.1 6.7 %collective-permute-done.34 = bf16[384,2560]{1,0:T(8,128)(2,1)} collective-permute-done((bf16[384,2560]{1,0:T(8,128)(2,1)S(1)}, bf16[384,2560]{1,0:T(8,128)(2,1)}, u32[]{:S(2)}, u32[]{:S(2)}) %collective-permute-start.34) | collective-permute-done | bytes 1966112 | tf_op jit(solution)/shard_map/ppermute | solution.py:81
  230.3 9.5 %collective-permute-done.39.refs_4_ = bf16[3,512,768]{2,1,0:T(8,128)(2,1)S(1)} collective-permute-done((bf16[3,512,768]{2,1,0:T(8,128)(2,1)}, bf16[3,512,768]{2,1,0:T(8,128)(2,1)S(1)}, u32[]{:S(2)}, u32[]{:S(2)}) %collective-permute-start.39) | collective-permute-done | bytes 2359328 | tf_op jit(solution)/shard_map/ppermute | solution.py:81
  246.7 15.9 %wide_both.3 = (bf16[512,1024]{1,0:T(8,128)(2,1)}, f32[512,1024]{1,0:T(8,128)S(1)}, f32[512,512]{1,0:T(8,128)S(1)}, bf16[3,512,768]{2,1,0:T(8,128)(2,1)S(1)}, bf16[3,512,768]{2,1,0:T(8,128)(2,1)}) custom-call(s32[1]{0:T(128)} %constant.172.clone.1.groups.places, bf16[768,2560]{1,0:T(8,128)(2,1)S(1)} %pad_maximum_fusion.3.refs_0_, ...), custom_call_target="tpu_custom_call" | custom-call | flops 1000 | bytes 1000 | tf_op jit(solution)/shard_map/wide_both/pallas_call | solution.py:580
  262.7 7.0 %collective-permute-done.40 = bf16[384,2560]{1,0:T(8,128)(2,1)S(1)} collective-permute-done((bf16[384,2560]{1,0:T(8,128)(2,1)S(1)}, bf16[384,2560]{1,0:T(8,128)(2,1)S(1)}, u32[]{:S(2)}, u32[]{:S(2)}) %collective-permute-start.40) | collective-permute-done | bytes 1966112 | tf_op jit(solution)/shard_map/ppermute | solution.py:81
  290.3 6.3 %grads.5 = bf16[768,2560]{1,0:T(8,128)(2,1)S(1)} custom-call(s32[1]{0:T(128)} %constant.172.clone.1.groups.places, bf16[3,512,768]{2,1,0:T(8,128)(2,1)S(1)} %copy-done.50, bf16[512,1024]{1,0:T(8,128)(2,1)S(1)} %copy-done.8, bf16[512,1024]{1,0:T(8,128)(2,1)S(1)} %copy-done.5, bf16[512,512]{1,0:T(8,128)(2,1)S(1)} %copy-done.23, ...), custom_call_target="tpu_custom_call" | custom-call | flops 1000 | bytes 1000 | tf_op jit(solution)/shard_map/grads/pallas_call | solution.py:632
  317.2 10.3 %wide_back.2 = (f32[512,1024]{1,0:T(8,128)S(1)}, f32[512,512]{1,0:T(8,128)S(1)}, bf16[3,512,768]{2,1,0:T(8,128)(2,1)S(1)}, bf16[3,512,768]{2,1,0:T(8,128)(2,1)}) custom-call(s32[1]{0:T(128)} %constant.172.clone.1.groups.places, bf16[768,2560]{1,0:T(8,128)(2,1)S(1)} %copy-done.1, bf16[768,2560]{1,0:T(8,128)(2,1)S(1)} %copy-done.14, ...), custom_call_target="tpu_custom_call" | custom-call | flops 1000 | bytes 1000 | tf_op jit(solution)/shard_map/wide_back/pallas_call | solution.py:580
  334.4 10.6 %wide_back.3 = (f32[512,1024]{1,0:T(8,128)S(1)}, f32[512,512]{1,0:T(8,128)S(1)}, bf16[3,512,768]{2,1,0:T(8,128)(2,1)S(1)}, bf16[3,512,768]{2,1,0:T(8,128)(2,1)}) custom-call(s32[1]{0:T(128)} %constant.172.clone.1.groups.places, bf16[768,2560]{1,0:T(8,128)(2,1)S(1)} %copy-done.3, bf16[768,2560]{1,0:T(8,128)(2,1)S(1)} %copy-done.16, ...), custom_call_target="tpu_custom_call" | custom-call | flops 1000 | bytes 1000 | tf_op jit(solution)/shard_map/wide_back/pallas_call | solution.py:580
  367.4 6.2 %grads.6 = bf16[768,2944]{1,0:T(8,128)(2,1)S(1)} custom-call(s32[1]{0:T(128)} %constant.172.clone.1.groups.places, bf16[3,512,768]{2,1,0:T(8,128)(2,1)S(1)} %copy-done.46, bf16[512,1024]{1,0:T(8,128)(2,1)S(1)} %get-tuple-element.230.refs_2_.refs_1_.normed_ref, bf16[512,1024]{1,0:T(8,128)(2,1)S(1)} %get-tuple-element.304.refs_4_.refs_2_, ...), custom_call_target="tpu_custom_call" | custom-call | flops 1000 | bytes 1000 | tf_op jit(solution)/shard_map/grads/pallas_call | solution.py:632
  389.5 6.8 %leave.3 = (f32[512,1024]{1,0:T(8,128)}, bf16[512,1024]{1,0:T(8,128)(2,1)}, bf16[256,1152]{1,0:T(8,128)(2,1)S(1)}, bf16[256,1152]{1,0:T(8,128)(2,1)S(1)}) custom-call(s32[3]{0:T(128)S(1)} %broadcast_subtract_fusion.scal, f32[8,1]{1,0:T(8,128)S(1)} %convert_select_fusion.1.hops_ref, f32[8,512]{1,0:T(8,128)S(1)} %pad_maximum_fusion.25.firsts_ref, ...), custom_call_target="tpu_custom_call" | custom-call | flops 1000 | bytes 1000 | tf_op jit(solution)/shard_map/leave/pallas_call | solution.py:407
  396.2 9.5 %collective-permute-done.60 = bf16[384,2944]{1,0:T(8,128)(2,1)S(1)} collective-permute-done((bf16[384,2944]{1,0:T(8,128)(2,1)S(1)}, bf16[384,2944]{1,0:T(8,128)(2,1)S(1)}, u32[]{:S(2)}, u32[]{:S(2)}) %collective-permute-start.60) | collective-permute-done | bytes 2261024 | tf_op jit(solution)/shard_map/ppermute | solution.py:81
  411.0 11.1 %collective-permute-done.61 = bf16[192,2944]{1,0:T(8,128)(2,1)S(1)} collective-permute-done((bf16[192,2944]{1,0:T(8,128)(2,1)S(1)}, bf16[192,2944]{1,0:T(8,128)(2,1)S(1)}, u32[]{:S(2)}, u32[]{:S(2)}) %collective-permute-start.61) | collective-permute-done | bytes 1130528 | tf_op jit(solution)/shard_map/ppermute | solution.py:81
  429.4 8.0 %collective-permute-done.65 = bf16[48,2944]{1,0:T(8,128)(2,1)S(1)} collective-permute-done((bf16[48,2944]{1,0:T(8,128)(2,1)S(1)}, bf16[48,2944]{1,0:T(8,128)(2,1)S(1)}, u32[]{:S(2)}, u32[]{:S(2)}) %collective-permute-start.65) | collective-permute-done | bytes 282656 | tf_op jit(solution)/shard_map/ppermute | solution.py:81
  437.4 9.2 %collective-permute-done.66 = bf16[48,2944]{1,0:T(8,128)(2,1)S(1)} collective-permute-done((bf16[48,2944]{1,0:T(8,128)(2,1)S(1)}, bf16[48,2944]{1,0:T(8,128)(2,1)S(1)}, u32[]{:S(2)}, u32[]{:S(2)}) %collective-permute-start.66) | collective-permute-done | bytes 282656 | tf_op jit(solution)/shard_map/ppermute | solution.py:81
  460.0 8.2 %collective-permute-done.70 = bf16[48,2560]{1,0:T(8,128)(2,1)} collective-permute-done((bf16[48,2560]{1,0:T(8,128)(2,1)S(1)}, bf16[48,2560]{1,0:T(8,128)(2,1)}, u32[]{:S(2)}, u32[]{:S(2)}) %collective-permute-start.70) | collective-permute-done | bytes 245792 | tf_op jit(solution)/shard_map/ppermute | solution.py:81
  486.2 8.3 %collective-permute-done.77 = bf16[48,2560]{1,0:T(8,128)(2,1)} collective-permute-done((bf16[48,2560]{1,0:T(8,128)(2,1)S(1)}, bf16[48,2560]{1,0:T(8,128)(2,1)}, u32[]{:S(2)}, u32[]{:S(2)}) %collective-permute-start.77) | collective-permute-done | bytes 245792 | tf_op jit(solution)/shard_map/ppermute | solution.py:81
  (459 shorter events, 274.8 us)
Async XLA Ops:
  71.6 30.8 %collective-permute-start.12 = (bf16[384,2560]{1,0:T(8,128)(2,1)}, bf16[384,2560]{1,0:T(8,128)(2,1)}, u32[]{:S(2)}, u32[]{:S(2)}) collective-permute-start(bf16[384,2560]{1,0:T(8,128)(2,1)} %pad_maximum_fusion.4), channel_id=1, source_target_pairs={{0,16},{2,18},{4,20},{6,22},{1,17},{3,19},{5,21},{7,23},{8,9},{10,... | collective-permute-start | bytes 5898248 | tf_op jit(solution)/shard_map/ppermute | solution.py:81
  74.5 26.9 %collective-permute-start.13 = (bf16[48,2560]{1,0:T(8,128)(2,1)S(1)}, bf16[48,2560]{1,0:T(8,128)(2,1)S(1)}, u32[]{:S(2)}, u32[]{:S(2)}) collective-permute-start(bf16[48,2560]{1,0:T(8,128)(2,1)S(1)} %get-tuple-element.213), channel_id=1, source_target_pairs={{0,4},{2,6},{4,0},{6,2},{1,5},{3,7},{5,1},{7,3},{8,12},{10,14},{12... | collective-permute-start | bytes 737288 | tf_op jit(solution)/shard_map/ppermute | solution.py:81
  77.3 24.1 %collective-permute-start.14 = (bf16[48,2560]{1,0:T(8,128)(2,1)S(1)}, bf16[48,2560]{1,0:T(8,128)(2,1)S(1)}, u32[]{:S(2)}, u32[]{:S(2)}) collective-permute-start(bf16[48,2560]{1,0:T(8,128)(2,1)S(1)} %get-tuple-element.213), channel_id=1, source_target_pairs={{0,6},{2,4},{4,2},{6,0},{1,7},{3,5},{5,3},{7,1},{8,14},{10,12},{12... | collective-permute-start | bytes 737288 | tf_op jit(solution)/shard_map/ppermute | solution.py:81
  78.0 18.4 %collective-permute-start.16 = (f32[4,512]{1,0:T(4,128)S(1)}, f32[4,512]{1,0:T(4,128)S(1)}, u32[]{:S(2)}, u32[]{:S(2)}) collective-permute-start(f32[4,512]{1,0:T(4,128)S(1)} %pad_maximum_fusion.26), channel_id=1, source_target_pairs={{0,4},{1,5},{2,6},{3,7},{4,0},{5,1},{6,2},{7,3},{8,12},{9,13},{10,... | collective-permute-start | bytes 24584 | tf_op jit(solution)/shard_map/ppermute | solution.py:81
  119.2 25.1 %collective-permute-start.20 = (bf16[384,2560]{1,0:T(8,128)(2,1)S(1)}, bf16[384,2560]{1,0:T(8,128)(2,1)S(1)}, u32[]{:S(2)}, u32[]{:S(2)}) collective-permute-start(bf16[384,2560]{1,0:T(8,128)(2,1)S(1)} %pad_maximum_fusion.5), channel_id=1, source_target_pairs={{0,16},{2,18},{4,20},{6,22},{1,17},{3,19},{5,21},{7,23},{8,9},{10,... | collective-permute-start | bytes 5898248 | tf_op jit(solution)/shard_map/ppermute | solution.py:81
  124.5 19.8 %collective-permute-start.22 = (bf16[48,2560]{1,0:T(8,128)(2,1)S(1)}, bf16[48,2560]{1,0:T(8,128)(2,1)S(1)}, u32[]{:S(2)}, u32[]{:S(2)}) collective-permute-start(bf16[48,2560]{1,0:T(8,128)(2,1)S(1)} %get-tuple-element.226), channel_id=1, source_target_pairs={{0,6},{2,4},{4,2},{6,0},{1,7},{3,5},{5,3},{7,1},{8,14},{10,12},{12... | collective-permute-start | bytes 737288 | tf_op jit(solution)/shard_map/ppermute | solution.py:81
  159.1 25.7 %collective-permute-start.26 = (bf16[384,2560]{1,0:T(8,128)(2,1)S(1)}, bf16[384,2560]{1,0:T(8,128)(2,1)S(1)}, u32[]{:S(2)}, u32[]{:S(2)}) collective-permute-start(bf16[384,2560]{1,0:T(8,128)(2,1)S(1)} %pad_maximum_fusion.6), channel_id=1, source_target_pairs={{0,16},{2,18},{4,20},{6,22},{1,17},{3,19},{5,21},{7,23},{8,9},{10,... | collective-permute-start | bytes 5898248 | tf_op jit(solution)/shard_map/ppermute | solution.py:81
  160.9 19.9 %collective-permute-start.27 = (bf16[48,2560]{1,0:T(8,128)(2,1)S(1)}, bf16[48,2560]{1,0:T(8,128)(2,1)S(1)}, u32[]{:S(2)}, u32[]{:S(2)}) collective-permute-start(bf16[48,2560]{1,0:T(8,128)(2,1)S(1)} %get-tuple-element.237), channel_id=1, source_target_pairs={{0,4},{2,6},{4,0},{6,2},{1,5},{3,7},{5,1},{7,3},{8,12},{10,14},{12... | collective-permute-start | bytes 737288 | tf_op jit(solution)/shard_map/ppermute | solution.py:81
  163.8 20.8 %collective-permute-start.28 = (bf16[48,2560]{1,0:T(8,128)(2,1)S(1)}, bf16[48,2560]{1,0:T(8,128)(2,1)S(1)}, u32[]{:S(2)}, u32[]{:S(2)}) collective-permute-start(bf16[48,2560]{1,0:T(8,128)(2,1)S(1)} %get-tuple-element.237), channel_id=1, source_target_pairs={{0,6},{2,4},{4,2},{6,0},{1,7},{3,5},{5,3},{7,1},{8,14},{10,12},{12... | collective-permute-start | bytes 737288 | tf_op jit(solution)/shard_map/ppermute | solution.py:81
  203.0 24.8 %collective-permute-start.34 = (bf16[384,2560]{1,0:T(8,128)(2,1)S(1)}, bf16[384,2560]{1,0:T(8,128)(2,1)}, u32[]{:S(2)}, u32[]{:S(2)}) collective-permute-start(bf16[384,2560]{1,0:T(8,128)(2,1)S(1)} %pad_maximum_fusion.7), channel_id=1, source_target_pairs={{0,16},{2,18},{4,20},{6,22},{1,17},{3,19},{5,21},{7,23},{8,9},{10,... | collective-permute-start | bytes 5898248 | tf_op jit(solution)/shard_map/ppermute | solution.py:81
  204.7 24.9 %collective-permute-start.36 = (bf16[512,1024]{1,0:T(8,128)(2,1)S(1)}, bf16[512,1024]{1,0:T(8,128)(2,1)S(1)}, u32[]{:S(2)}, u32[]{:S(2)}) collective-permute-start(bf16[512,1024]{1,0:T(8,128)(2,1)S(1)} %copy-done.4), channel_id=1, source_target_pairs={{0,8},{2,10},{4,12},{6,14},{1,9},{3,11},{5,13},{7,15},{8,0},{10,2}... | collective-permute-start | bytes 3145736 | tf_op jit(solution)/shard_map/ppermute | solution.py:81
  204.8 24.9 %collective-permute-start.35 = (bf16[512,1024]{1,0:T(8,128)(2,1)S(1)}, bf16[512,1024]{1,0:T(8,128)(2,1)S(1)}, u32[]{:S(2)}, u32[]{:S(2)}) collective-permute-start(bf16[512,1024]{1,0:T(8,128)(2,1)S(1)} %get-tuple-element.261.refs_2_.refs_1_.normed_ref), channel_id=1, source_target_pairs={{0,8},{2,10},{4,12},{6,14},{1,9},{3,11},{5,13},{7,15},{8,0},{10,2}... | collective-permute-start | bytes 3145736 | tf_op jit(solution)/shard_map/ppermute | solution.py:81
  205.3 24.4 %collective-permute-start.37 = (bf16[512,512]{1,0:T(8,128)(2,1)S(1)}, bf16[512,512]{1,0:T(8,128)(2,1)S(1)}, u32[]{:S(2)}, u32[]{:S(2)}) collective-permute-start(bf16[512,512]{1,0:T(8,128)(2,1)S(1)} %get-tuple-element.262.refs_3_), channel_id=1, source_target_pairs={{0,8},{2,10},{4,12},{6,14},{1,9},{3,11},{5,13},{7,15},{8,0},{10,2}... | collective-permute-start | bytes 1572872 | tf_op jit(solution)/shard_map/ppermute | solution.py:81
  245.0 24.7 %collective-permute-start.40 = (bf16[384,2560]{1,0:T(8,128)(2,1)S(1)}, bf16[384,2560]{1,0:T(8,128)(2,1)S(1)}, u32[]{:S(2)}, u32[]{:S(2)}) collective-permute-start(bf16[384,2560]{1,0:T(8,128)(2,1)S(1)} %slice.306), channel_id=1, source_target_pairs={{0,16},{2,18},{4,20},{6,22},{1,17},{3,19},{5,21},{7,23},{8,9},{10,... | collective-permute-start | bytes 5898248 | tf_op jit(solution)/shard_map/ppermute | solution.py:81
  280.2 21.7 %collective-permute-start.42 = (bf16[192,2560]{1,0:T(8,128)(2,1)}, bf16[192,2560]{1,0:T(8,128)(2,1)}, u32[]{:S(2)}, u32[]{:S(2)}) collective-permute-start(bf16[192,2560]{1,0:T(8,128)(2,1)} %slice.308), channel_id=1, source_target_pairs={{0,1},{2,3},{4,5},{6,7},{1,0},{3,2},{5,4},{7,6},{8,24},{10,26},{12... | collective-permute-start | bytes 2949128 | tf_op jit(solution)/shard_map/ppermute | solution.py:81
  313.5 41.2 %collective-permute-start.49 = (bf16[384,2560]{1,0:T(8,128)(2,1)}, bf16[384,2560]{1,0:T(8,128)(2,1)}, u32[]{:S(2)}, u32[]{:S(2)}) collective-permute-start(bf16[384,2560]{1,0:T(8,128)(2,1)} %slice.314), channel_id=1, source_target_pairs={{0,16},{2,18},{4,20},{6,22},{1,17},{3,19},{5,21},{7,23},{8,9},{10,... | collective-permute-start | bytes 5898248 | tf_op jit(solution)/shard_map/ppermute | solution.py:81
  328.8 29.2 %collective-permute-start.54 = (bf16[3,512,768]{2,1,0:T(8,128)(2,1)}, bf16[3,512,768]{2,1,0:T(8,128)(2,1)S(1)}, u32[]{:S(2)}, u32[]{:S(2)}) collective-permute-start(bf16[3,512,768]{2,1,0:T(8,128)(2,1)} %get-tuple-element.312), channel_id=1, source_target_pairs={{0,8},{2,10},{4,12},{6,14},{1,9},{3,11},{5,13},{7,15},{8,0},{10,2}... | collective-permute-start | bytes 7077896 | tf_op jit(solution)/shard_map/ppermute | solution.py:81
  332.1 22.4 %collective-permute-start.48 = (bf16[48,2560]{1,0:T(8,128)(2,1)S(1)}, bf16[48,2560]{1,0:T(8,128)(2,1)S(1)}, u32[]{:S(2)}, u32[]{:S(2)}) collective-permute-start(bf16[48,2560]{1,0:T(8,128)(2,1)S(1)} %get-tuple-element.400), channel_id=1, source_target_pairs={{0,6},{2,4},{4,2},{6,0},{1,7},{3,5},{5,3},{7,1},{8,14},{10,12},{12... | collective-permute-start | bytes 737288 | tf_op jit(solution)/shard_map/ppermute | solution.py:81
  377.8 27.9 %collective-permute-start.60 = (bf16[384,2944]{1,0:T(8,128)(2,1)S(1)}, bf16[384,2944]{1,0:T(8,128)(2,1)S(1)}, u32[]{:S(2)}, u32[]{:S(2)}) collective-permute-start(bf16[384,2944]{1,0:T(8,128)(2,1)S(1)} %slice.318), channel_id=1, source_target_pairs={{0,16},{2,18},{4,20},{6,22},{1,17},{3,19},{5,21},{7,23},{8,9},{10,... | collective-permute-start | bytes 6782984 | tf_op jit(solution)/shard_map/ppermute | solution.py:81
  422.7 29.7 %collective-permute-start.68 = (bf16[384,2560]{1,0:T(8,128)(2,1)S(1)}, bf16[384,2560]{1,0:T(8,128)(2,1)S(1)}, u32[]{:S(2)}, u32[]{:S(2)}) collective-permute-start(bf16[384,2560]{1,0:T(8,128)(2,1)S(1)} %slice.330), channel_id=1, source_target_pairs={{0,16},{2,18},{4,20},{6,22},{1,17},{3,19},{5,21},{7,23},{8,9},{10,... | collective-permute-start | bytes 5898248 | tf_op jit(solution)/shard_map/ppermute | solution.py:81
  425.1 21.5 %collective-permute-start.66 = (bf16[48,2944]{1,0:T(8,128)(2,1)S(1)}, bf16[48,2944]{1,0:T(8,128)(2,1)S(1)}, u32[]{:S(2)}, u32[]{:S(2)}) collective-permute-start(bf16[48,2944]{1,0:T(8,128)(2,1)S(1)} %get-tuple-element.387), channel_id=1, source_target_pairs={{0,4},{2,6},{4,0},{6,2},{1,5},{3,7},{5,1},{7,3},{8,12},{10,14},{12... | collective-permute-start | bytes 847880 | tf_op jit(solution)/shard_map/ppermute | solution.py:81
  427.3 24.9 %collective-permute-start.67 = (bf16[48,2944]{1,0:T(8,128)(2,1)S(1)}, bf16[48,2944]{1,0:T(8,128)(2,1)S(1)}, u32[]{:S(2)}, u32[]{:S(2)}) collective-permute-start(bf16[48,2944]{1,0:T(8,128)(2,1)S(1)} %get-tuple-element.386), channel_id=1, source_target_pairs={{0,6},{2,4},{4,2},{6,0},{1,7},{3,5},{5,3},{7,1},{8,14},{10,12},{12... | collective-permute-start | bytes 847880 | tf_op jit(solution)/shard_map/ppermute | solution.py:81
  428.6 23.8 %collective-permute-start.69 = (bf16[128,1152]{1,0:T(8,128)(2,1)S(1)}, bf16[128,1152]{1,0:T(8,128)(2,1)S(1)}, u32[]{:S(2)}, u32[]{:S(2)}) collective-permute-start(bf16[128,1152]{1,0:T(8,128)(2,1)S(1)} %slice.332), channel_id=1, source_target_pairs={{0,16},{2,18},{4,20},{6,22},{1,17},{3,19},{5,21},{7,23},{8,9},{10,... | collective-permute-start | bytes 884744 | tf_op jit(solution)/shard_map/ppermute | solution.py:81
  477.5 21.9 %collective-permute-start.78 = (bf16[48,2560]{1,0:T(8,128)(2,1)S(1)}, bf16[48,2560]{1,0:T(8,128)(2,1)}, u32[]{:S(2)}, u32[]{:S(2)}) collective-permute-start(bf16[48,2560]{1,0:T(8,128)(2,1)S(1)} %get-tuple-element.393), channel_id=1, source_target_pairs={{0,6},{2,4},{4,2},{6,0},{1,7},{3,5},{5,3},{7,1},{8,14},{10,12},{12... | collective-permute-start | bytes 737288 | tf_op jit(solution)/shard_map/ppermute | solution.py:81
  (138 other events, 1413.9 us)

commit v5 on v4

--- a/solution.py
+++ b/solution.py
@@ -116,6 +116,12 @@
     for k in range(1, count):
         parts.append(permute(array[k * rows : (k + 1) * rows], pairs[k]))
     return add_parts(parts, dtype or array.dtype)
+
+
+def fold_parts(array, pairs, parts, which):
+    rows = array.shape[0] // len(pairs)
+    cut = {k: array[k * rows : (k + 1) * rows] for k in which}
+    return parts + [permute(cut[k], pairs[k]) if k else cut[k] for k in which]
 
 
 def dot_nn(a, b):
@@ -737,23 +743,20 @@
         return [permute(array, lay.core) for array in arrays]
 
     line_h = stage(head, lay.q)
-    line_h, shard_a = fence(line_h, shard_a)
+    pulled = pulls(shard_a, 0)
+    line_h, shard_a, pulled = fence(line_h, shard_a, pulled)
     plane_h = stage(line_h, lay.p1)
-    pulled = pulls(shard_a, 0)
+    pulled |= pulls(shard_a, 1)
     plane_h, shard_a, pulled = fence(plane_h, shard_a, pulled)
     head_own = stage(plane_h, lay.p2)
-    pulled |= pulls(shard_a, 1)
-    head_own, shard_a, pulled = fence(head_own, shard_a, pulled)
-    head_other = permute(head_own, lay.core)
     pulled |= pulls(shard_a, 2)
-    head_own, head_other, line_a, shard_b = fence(head_own, head_other, line_of(shard_a, pulled), shard_b)
-
+    head_own, line_a, shard_b = fence(head_own, line_of(shard_a, pulled), shard_b)
+    (head_other,) = swap(head_own)
     plane_a = stage(line_a, lay.p1)
     pulled = pulls(shard_b, 0)
+    head_own, head_other, plane_a, shard_b, pulled = fence(head_own, head_other, plane_a, shard_b, pulled)
     wr_all, rows_all = params_call(key, head_own, head_other, width, chan)
     entered = enter_call(0, near, tokens, rows_all, wr_all)
-    held = seq_step(lay, entered[3], 1)
-    plane_a, shard_b, pulled, entered, held = fence(plane_a, shard_b, pulled, entered, held)
 
     def enter(layer, stream, entered, lasts):
         normed, pre_reduce, local_states, _ = entered
@@ -788,14 +791,18 @@
         )
         return [d_normed, d_mixed], mine, peers
 
-    k0 = enter(0, tokens, entered, seq_rest(lay, held))
     a_own = stage(plane_a, lay.p2)
     pulled |= pulls(shard_b, 1, 2)
-    a_own, line_b, k0, shard_c = fence(a_own, line_of(shard_b, pulled), k0, shard_c)
+    a_own, line_b, entered, shard_c = fence(a_own, line_of(shard_b, pulled), entered, shard_c)
+    held = seq_step(lay, entered[3], 1)
     (a_other,) = swap(a_own)
-    plane_b = stage(line_b, lay.p1)
+    plane_b = stage(after(line_b, held), lay.p1)
+    lasts = seq_rest(lay, held)
     pulled = pulls(shard_c, 0)
-    a_own, a_other, plane_b, shard_c, pulled = fence(a_own, a_other, plane_b, shard_c, pulled)
+    a_own, a_other, plane_b, shard_c, pulled, entered, lasts = fence(
+        a_own, a_other, plane_b, shard_c, pulled, entered, lasts
+    )
+    k0 = enter(0, tokens, entered, lasts)
     b_own = stage(plane_b, lay.p2)
     pulled |= pulls(shard_c, 1, 2)
     *save_a, acc = wide_call("fore", a_own, a_other, k0["normed"], k0["mixed"], base=tokens)
@@ -808,10 +815,10 @@
     pulled |= pulls(shard_d, 1, 2)
     *save_b, acc = wide_call("fore", b_own, b_other, k0["normed"], k0["mixed"], base=acc)
     entered = enter_call(1, near, acc, rows_all, wr_all)
-    c_own, line_d, acc, entered = fence(c_own, line_of(shard_d, pulled), acc, entered)
+    held = seq_step(lay, entered[3], 1)
+    c_own, line_d, acc, entered, held = fence(c_own, line_of(shard_d, pulled), acc, entered, held)
     (c_other,) = swap(c_own)
-    held = seq_step(lay, entered[3], 1)
-    plane_d = stage(after(line_d, held), lay.p1)
+    plane_d = stage(line_d, lay.p1)
     k1 = enter(1, acc, entered, seq_rest(lay, held))
     c_own, c_other, plane_d, k1 = fence(c_own, c_other, plane_d, k1)
 
@@ -828,8 +835,8 @@
     output, sums, b1_own, b1_peer = both(d_own, d_other, acc, sums, BF)
     a1, sums, b1_own, b1_peer = fence(a1, sums, b1_own, b1_peer)
 
-    (b1_peer,) = swap(b1_peer)
     back_local, first_row = back_scan_call(1, near, sums[1], rows_all)
+    (b1_peer,) = swap(after(b1_peer, first_row))
     held = seq_step(lay, first_row, 1)
     a1 = fold(after(a1, held), lay.p1)
     b1 = grads_call(b1_own, b1_peer, ins_1, peer_1)
@@ -838,11 +845,13 @@
     a1, b1, upstream, low, head_1 = fence(a1, b1, upstream, low, head_1)
 
     b1 = fold(b1, lay.p2)
-    a1_done = fold(a1, lay.q, F32)
+    cut = (2 * lay.nq + 2) // 3
+    a1_parts = fold_parts(a1, lay.q, [], range(cut))
     peer_0 = swap(k0["normed"], low, k0["mixed"])
     (head_peer,) = swap(head_1[1])
     sums, a0_own, a0_peer = back(a_own, a_other, save_a, None)
-    sums, a0_sent = fence(sums, a0_peer)
+    sums, a0_sent, a1, a1_parts = fence(sums, a0_peer, a1, a1_parts)
+    a1_done = add_parts(fold_parts(a1, lay.q, a1_parts, range(cut, lay.nq)), F32)
     (a0_peer,) = swap(a0_sent)
     sums, b0_own, b0_peer = back(b_own, b_other, save_b, sums)
     a1_done, b1, peer_0, head_peer, a0_own, a0_peer, sums, b0_own, b0_peer = fence(
@@ -859,31 +868,26 @@
 
     held = seq_step(lay, first_row, 1)
     a0 = fold(after(a0, held), lay.p2)
-    b0 = grads_call(b0_own, b0_peer, ins_0, peer_0)
     _, input_grad, (head_own, head_other) = leave(0, k0, sums, (back_local, seq_rest(lay, held)), upstream)
-    a0, b0, b1, head_own, head_other = fence(a0, b0, b1, head_own, head_other)
+    a0, b1, head_own, head_other = fence(a0, b1, head_own, head_other)
 
     a0 = fold(a0, lay.p1)
-    size = b1.shape[0] // lay.nq
-    cut = (2 * lay.nq + 2) // 3
-    b1_parts = [b1[k * size : (k + 1) * size] for k in range(lay.nq)]
-    b1_parts[1:cut] = [permute(b1_parts[k], lay.q[k]) for k in range(1, cut)]
-    h0 = add_parts([head_own, *swap(head_other)], BF)
-    a0, b0, b1_parts, h0 = fence(a0, b0, b1_parts, h0)
+    b1_parts = fold_parts(b1, lay.q, [], range(cut))
+    heads_0 = [head_own, *swap(head_other)]
+    b0 = grads_call(b0_own, b0_peer, ins_0, peer_0, heads=heads_0, head_rows=small_rows)
+    a0, b0, b1, b1_parts = fence(a0, b0, b1, b1_parts)
 
     a0_done = fold(a0, lay.q, F32)
-    b0, h0 = fold(b0, lay.p2), fold(h0, lay.p2)
-    a0_done, b0, b1_parts, h0 = fence(a0_done, b0, b1_parts, h0)
-
-    b1_parts[cut:] = [permute(b1_parts[k], lay.q[k]) for k in range(cut, lay.nq)]
-    b1_done = add_parts(b1_parts, F32)
-    b0, h0 = fold(b0, lay.p1), fold(h0, lay.p1)
-    b1_done, b0, h0 = fence(b1_done, b0, h0)
-    b0_done, h0_done = fold(b0, lay.q, F32), fold(h0, lay.q, F32)
-
-    h1_done = close_lanes(a0_done[:, lanes:], small_rows)
-    grads = [cat(a0_done[:, :lanes], b0_done), cat(a1_done, b1_done)]
-    heads_done = [h0_done, h1_done]
+    b0 = fold(b0, lay.p2)
+    a0_done, b0, b1, b1_parts = fence(a0_done, b0, b1, b1_parts)
+
+    b1_done = add_parts(fold_parts(b1, lay.q, b1_parts, range(cut, lay.nq)), F32)
+    b0 = fold(b0, lay.p1)
+    b1_done, b0 = fence(b1_done, b0)
+    b0_done = fold(b0, lay.q, F32)
+
+    grads = [cat(a0_done[:, :lanes], b0_done[:, :lanes]), cat(a1_done, b1_done)]
+    heads_done = [close_lanes(done[:, lanes:], small_rows) for done in (b0_done, a0_done)]
     vecs = [h[:, width : width + SMALL] for h in heads_done]
     return (
         output,

time: 514 us -> 502 us (0.977)
  waiting for transfers between devices: 208 us -> 187 us
  starting transfers between devices: 85.6 us -> 71.5 us
  local copies, waits for them, and re-layouts: 50.1 us -> 63.1 us
  Pallas kernels: 129 us -> 141 us
    ppermute x79 -> x74, waiting for transfers between devices: 208 us -> 187 us  [permute(): return lax.ppermute(array, AXES, pairs)]
    ppermute x79 -> x74, starting transfers between devices: 85.6 us -> 71.5 us  [permute(): return lax.ppermute(array, AXES, pairs)]
    unnamed x171 -> x193, local copies, waits for them, and re-layouts: 35.5 us -> 47 us
    pallas_call x6, Pallas kernels: 65.9 us -> 76.6 us  [wide_call(): pl.pallas_call(functools.partial(wide_kernel, names, mode, blocks, (width...]
    concatenate x27, other arithmetic: 8.07 us -> 13.7 us  [cat(): return jnp.concatenate(arrays, axis=0)]
  transfers between devices with their start and end apart: 79 -> 74, of which waited for: 43 -> 41; matrix products, arithmetic and copies ran while one was open for 5% -> 5% of each run, Pallas kernels for 24% -> 26%
where the time goes in v5:
time: 502 us; the launch traced here: 495 us
  waiting for transfers between devices  187 us (37%)
  Pallas kernels  141 us (28%)
  starting transfers between devices  71.5 us (14%)
  local copies, waits for them, and re-layouts  63.1 us (13%)
  other arithmetic  30 us (6%)
    ppermute x74, waiting for transfers between devices, permute(): return lax.ppermute(array, AXES, pairs)  187 us
    pallas_call x6, Pallas kernels, wide_call(): pl.pallas_call(functools.partial(wide_kernel, names, mode, blocks, (width...  76.6 us
    ppermute x74, starting transfers between devices, permute(): return lax.ppermute(array, AXES, pairs)  71.5 us
    unnamed x193, local copies, waits for them, and re-layouts  47 us
    pallas_call x4, Pallas kernels, grads_call(): pl.pallas_call(functools.partial(grads_kernel, names, head_rows, sub), gr...  24.5 us
    concatenate x27, other arithmetic, cat(): return jnp.concatenate(arrays, axis=0)  13.7 us
    pallas_call x2, Pallas kernels, leave_call(): pl.pallas_call(functools.partial(leave_kernel, starts.shape[0], layer), o...  12.9 us
  transfers between devices with their start and end apart: 74, of which 41 were waited for; matrix products, arithmetic and copies ran while one was open for 5% of the time, Pallas kernels for 26%

profile of v5, /device:TPU:8, one launch (start us, length us, event | category | flops | bytes accessed | tf_op | source)
XLA Modules:
  0.0 495.2 jit_solution(14746067828770461188)
XLA Ops:
  25.7 6.6 %collective-permute-done.5 = bf16[48,2560]{1,0:T(8,128)(2,1)S(1)} collective-permute-done((bf16[48,2560]{1,0:T(8,128)(2,1)S(1)}, bf16[48,2560]{1,0:T(8,128)(2,1)S(1)}, u32[]{:S(2)}, u32[]{:S(2)}) %collective-permute-start.5) | collective-permute-done | bytes 245792 | tf_op jit(solution)/shard_map/ppermute | solution.py:81
  33.6 11.7 %collective-permute-done.7 = bf16[48,2560]{1,0:T(8,128)(2,1)S(1)} collective-permute-done((bf16[48,2560]{1,0:T(8,128)(2,1)S(1)}, bf16[48,2560]{1,0:T(8,128)(2,1)S(1)}, u32[]{:S(2)}, u32[]{:S(2)}) %collective-permute-start.7) | collective-permute-done | bytes 245792 | tf_op jit(solution)/shard_map/ppermute | solution.py:81
  49.8 9.9 %collective-permute-done.9 = bf16[192,2560]{1,0:T(8,128)(2,1)S(1)} collective-permute-done((bf16[192,2560]{1,0:T(8,128)(2,1)S(1)}, bf16[192,2560]{1,0:T(8,128)(2,1)S(1)}, u32[]{:S(2)}, u32[]{:S(2)}) %collective-permute-start.9) | collective-permute-done | bytes 983072 | tf_op jit(solution)/shard_map/ppermute | solution.py:81
  81.8 6.3 %collective-permute-done.13 = bf16[48,2560]{1,0:T(8,128)(2,1)} collective-permute-done((bf16[48,2560]{1,0:T(8,128)(2,1)}, bf16[48,2560]{1,0:T(8,128)(2,1)}, u32[]{:S(2)}, u32[]{:S(2)}) %collective-permute-start.13) | collective-permute-done | bytes 245792 | tf_op jit(solution)/shard_map/ppermute | solution.py:81
  129.1 7.3 %wide_fore.2 = (f32[512,1536]{1,0:T(8,128)S(1)}, f32[512,1536]{1,0:T(8,128)S(1)}, f32[512,1024]{1,0:T(8,128)S(1)}) custom-call(s32[1]{0:T(128)} %constant.172.clone.1.groups.places, bf16[768,2560]{1,0:T(8,128)(2,1)S(1)} %copy-done.1, bf16[768,2560]{1,0:T(8,128)(2,1)S(1)} %copy-done.15, bf16[512,1024]{1,0:T(8,128)(2,1)S(1)} %get-tuple-element.225.refs_2_.refs_1_.normed_ref, ...), custom_call_target="tpu_custom_call" | custom-call | flops 1000 | bytes 1000 | tf_op jit(solution)/shard_map/wide_fore/pallas_call | solution.py:586
  145.3 12.0 %collective-permute-done.24 = bf16[192,2560]{1,0:T(8,128)(2,1)S(1)} collective-permute-done((bf16[192,2560]{1,0:T(8,128)(2,1)S(1)}, bf16[192,2560]{1,0:T(8,128)(2,1)S(1)}, u32[]{:S(2)}, u32[]{:S(2)}) %collective-permute-start.24) | collective-permute-done | bytes 983072 | tf_op jit(solution)/shard_map/ppermute | solution.py:81
  162.4 7.3 %wide_fore.3 = (f32[512,1536]{1,0:T(8,128)S(1)}, f32[512,1536]{1,0:T(8,128)S(1)}, f32[512,1024]{1,0:T(8,128)S(1)}) custom-call(s32[1]{0:T(128)} %constant.172.clone.1.groups.places, bf16[768,2560]{1,0:T(8,128)(2,1)S(1)} %pad_maximum_fusion.1.refs_0_, bf16[768,2560]{1,0:T(8,128)(2,1)S(1)} %collective-permute-done.23.refs_1_, ...), custom_call_target="tpu_custom_call" | custom-call | flops 1000 | bytes 1000 | tf_op jit(solution)/shard_map/wide_fore/pallas_call | solution.py:586
  198.9 26.4 %wide_both.2 = (f32[512,1024]{1,0:T(8,128)S(1)}, f32[512,1024]{1,0:T(8,128)S(1)}, f32[512,512]{1,0:T(8,128)S(1)}, bf16[3,512,768]{2,1,0:T(8,128)(2,1)S(1)}, bf16[3,512,768]{2,1,0:T(8,128)(2,1)S(1)}) custom-call(s32[1]{0:T(128)} %constant.172.clone.1.groups.places, bf16[768,2560]{1,0:T(8,128)(2,1)S(1)} %pad_maximum_fusion.2.refs_0_, ...), custom_call_target="tpu_custom_call" | custom-call | flops 1000 | bytes 1000 | tf_op jit(solution)/shard_map/wide_both/pallas_call | solution.py:586
  229.9 9.9 %collective-permute-done.39.refs_4_ = bf16[3,512,768]{2,1,0:T(8,128)(2,1)S(1)} collective-permute-done((bf16[3,512,768]{2,1,0:T(8,128)(2,1)}, bf16[3,512,768]{2,1,0:T(8,128)(2,1)S(1)}, u32[]{:S(2)}, u32[]{:S(2)}) %collective-permute-start.39) | collective-permute-done | bytes 2359328 | tf_op jit(solution)/shard_map/ppermute | solution.py:81
  246.4 15.5 %wide_both.3 = (bf16[512,1024]{1,0:T(8,128)(2,1)}, f32[512,1024]{1,0:T(8,128)S(1)}, f32[512,512]{1,0:T(8,128)S(1)}, bf16[3,512,768]{2,1,0:T(8,128)(2,1)S(1)}, bf16[3,512,768]{2,1,0:T(8,128)(2,1)}) custom-call(s32[1]{0:T(128)} %constant.172.clone.1.groups.places, bf16[768,2560]{1,0:T(8,128)(2,1)S(1)} %pad_maximum_fusion.3.refs_0_, ...), custom_call_target="tpu_custom_call" | custom-call | flops 1000 | bytes 1000 | tf_op jit(solution)/shard_map/wide_both/pallas_call | solution.py:586
  261.9 7.8 %collective-permute-done.40 = bf16[384,2560]{1,0:T(8,128)(2,1)S(1)} collective-permute-done((bf16[384,2560]{1,0:T(8,128)(2,1)S(1)}, bf16[384,2560]{1,0:T(8,128)(2,1)S(1)}, u32[]{:S(2)}, u32[]{:S(2)}) %collective-permute-start.40) | collective-permute-done | bytes 1966112 | tf_op jit(solution)/shard_map/ppermute | solution.py:81
  290.3 6.5 %grads.5 = bf16[768,2560]{1,0:T(8,128)(2,1)S(1)} custom-call(s32[1]{0:T(128)} %constant.172.clone.1.groups.places, bf16[3,512,768]{2,1,0:T(8,128)(2,1)S(1)} %copy-done.54, bf16[512,1024]{1,0:T(8,128)(2,1)S(1)} %copy-done.9, bf16[512,1024]{1,0:T(8,128)(2,1)S(1)} %copy-done.6, bf16[512,512]{1,0:T(8,128)(2,1)S(1)} %copy-done.25, ...), custom_call_target="tpu_custom_call" | custom-call | flops 1000 | bytes 1000 | tf_op jit(solution)/shard_map/grads/pallas_call | solution.py:638
  318.4 10.4 %wide_back.2 = (f32[512,1024]{1,0:T(8,128)S(1)}, f32[512,512]{1,0:T(8,128)S(1)}, bf16[3,512,768]{2,1,0:T(8,128)(2,1)S(1)}, bf16[3,512,768]{2,1,0:T(8,128)(2,1)}) custom-call(s32[1]{0:T(128)} %constant.172.clone.1.groups.places, bf16[768,2560]{1,0:T(8,128)(2,1)S(1)} %copy-done.2, bf16[768,2560]{1,0:T(8,128)(2,1)S(1)} %copy-done.16, ...), custom_call_target="tpu_custom_call" | custom-call | flops 1000 | bytes 1000 | tf_op jit(solution)/shard_map/wide_back/pallas_call | solution.py:586
  334.7 9.8 %wide_back.3 = (f32[512,1024]{1,0:T(8,128)S(1)}, f32[512,512]{1,0:T(8,128)S(1)}, bf16[3,512,768]{2,1,0:T(8,128)(2,1)S(1)}, bf16[3,512,768]{2,1,0:T(8,128)(2,1)S(1)}) custom-call(s32[1]{0:T(128)} %constant.172.clone.1.groups.places, bf16[768,2560]{1,0:T(8,128)(2,1)S(1)} %copy-done.4, bf16[768,2560]{1,0:T(8,128)(2,1)S(1)} %copy-done.18, ...), custom_call_target="tpu_custom_call" | custom-call | flops 1000 | bytes 1000 | tf_op jit(solution)/shard_map/wide_back/pallas_call | solution.py:586
  356.7 6.5 %grads.6 = bf16[768,2944]{1,0:T(8,128)(2,1)S(1)} custom-call(s32[1]{0:T(128)} %constant.172.clone.1.groups.places, bf16[3,512,768]{2,1,0:T(8,128)(2,1)S(1)} %copy-done.50, bf16[512,1024]{1,0:T(8,128)(2,1)S(1)} %get-tuple-element.225.refs_2_.refs_1_.normed_ref, bf16[512,1024]{1,0:T(8,128)(2,1)S(1)} %get-tuple-element.300.refs_4_.refs_2_, ...), custom_call_target="tpu_custom_call" | custom-call | flops 1000 | bytes 1000 | tf_op jit(solution)/shard_map/grads/pallas_call | solution.py:638
  378.6 6.8 %leave.3 = (f32[512,1024]{1,0:T(8,128)}, bf16[512,1024]{1,0:T(8,128)(2,1)}, bf16[256,1152]{1,0:T(8,128)(2,1)S(1)}, bf16[256,1152]{1,0:T(8,128)(2,1)S(1)}) custom-call(s32[3]{0:T(128)S(1)} %broadcast_subtract_fusion.scal, f32[8,1]{1,0:T(8,128)S(1)} %convert_select_fusion.1.hops_ref, f32[8,512]{1,0:T(8,128)S(1)} %pad_maximum_fusion.25.firsts_ref, ...), custom_call_target="tpu_custom_call" | custom-call | flops 1000 | bytes 1000 | tf_op jit(solution)/shard_map/leave/pallas_call | solution.py:413
  385.4 10.8 %collective-permute-done.60 = bf16[384,2944]{1,0:T(8,128)(2,1)S(1)} collective-permute-done((bf16[384,2944]{1,0:T(8,128)(2,1)S(1)}, bf16[384,2944]{1,0:T(8,128)(2,1)S(1)}, u32[]{:S(2)}, u32[]{:S(2)}) %collective-permute-start.60) | collective-permute-done | bytes 2261024 | tf_op jit(solution)/shard_map/ppermute | solution.py:81
  400.8 6.5 %grads.7 = bf16[768,2944]{1,0:T(8,128)(2,1)S(1)} custom-call(s32[1]{0:T(128)} %constant.172.clone.1.groups.places, bf16[3,512,768]{2,1,0:T(8,128)(2,1)S(1)} %get-tuple-element.351.refs_0_, bf16[512,1024]{1,0:T(8,128)(2,1)S(1)} %get-tuple-element.225.refs_2_.refs_1_.normed_ref, bf16[512,1024]{1,0:T(8,128)(2,1)S(1)} %get-tuple-element.300.refs_4_.refs_2_, ...), custom_call_target="tpu_custom_call" | custom-call | flops 1000 | bytes 1000 | tf_op jit(solution)/shard_map/grads/pallas_call | solution.py:638
  419.6 7.4 %collective-permute-done.65 = bf16[48,2944]{1,0:T(8,128)(2,1)S(1)} collective-permute-done((bf16[48,2944]{1,0:T(8,128)(2,1)S(1)}, bf16[48,2944]{1,0:T(8,128)(2,1)S(1)}, u32[]{:S(2)}, u32[]{:S(2)}) %collective-permute-start.65) | collective-permute-done | bytes 282656 | tf_op jit(solution)/shard_map/ppermute | solution.py:81
  426.9 9.6 %collective-permute-done.66 = bf16[48,2944]{1,0:T(8,128)(2,1)S(1)} collective-permute-done((bf16[48,2944]{1,0:T(8,128)(2,1)S(1)}, bf16[48,2944]{1,0:T(8,128)(2,1)S(1)}, u32[]{:S(2)}, u32[]{:S(2)}) %collective-permute-start.66) | collective-permute-done | bytes 282656 | tf_op jit(solution)/shard_map/ppermute | solution.py:81
  436.5 6.1 %collective-permute-done.67 = bf16[48,2944]{1,0:T(8,128)(2,1)S(1)} collective-permute-done((bf16[48,2944]{1,0:T(8,128)(2,1)S(1)}, bf16[48,2944]{1,0:T(8,128)(2,1)S(1)}, u32[]{:S(2)}, u32[]{:S(2)}) %collective-permute-start.67) | collective-permute-done | bytes 282656 | tf_op jit(solution)/shard_map/ppermute | solution.py:81
  447.2 11.0 %collective-permute-done.69 = bf16[48,2560]{1,0:T(8,128)(2,1)} collective-permute-done((bf16[48,2560]{1,0:T(8,128)(2,1)}, bf16[48,2560]{1,0:T(8,128)(2,1)}, u32[]{:S(2)}, u32[]{:S(2)}) %collective-permute-start.69) | collective-permute-done | bytes 245792 | tf_op jit(solution)/shard_map/ppermute | solution.py:81
  465.7 6.1 %collective-permute-done.71 = bf16[48,2944]{1,0:T(8,128)(2,1)S(1)} collective-permute-done((bf16[48,2944]{1,0:T(8,128)(2,1)S(1)}, bf16[48,2944]{1,0:T(8,128)(2,1)S(1)}, u32[]{:S(2)}, u32[]{:S(2)}) %collective-permute-start.71) | collective-permute-done | bytes 282656 | tf_op jit(solution)/shard_map/ppermute | solution.py:81
  471.8 11.3 %collective-permute-done.72 = bf16[48,2944]{1,0:T(8,128)(2,1)S(1)} collective-permute-done((bf16[48,2944]{1,0:T(8,128)(2,1)S(1)}, bf16[48,2944]{1,0:T(8,128)(2,1)S(1)}, u32[]{:S(2)}, u32[]{:S(2)}) %collective-permute-start.72) | collective-permute-done | bytes 282656 | tf_op jit(solution)/shard_map/ppermute | solution.py:81
  (470 shorter events, 263.6 us)
Async XLA Ops:
  62.9 26.5 %collective-permute-start.11 = (bf16[384,2560]{1,0:T(8,128)(2,1)}, bf16[384,2560]{1,0:T(8,128)(2,1)}, u32[]{:S(2)}, u32[]{:S(2)}) collective-permute-start(bf16[384,2560]{1,0:T(8,128)(2,1)} %pad_maximum_fusion.4), channel_id=1, source_target_pairs={{0,16},{2,18},{4,20},{6,22},{1,17},{3,19},{5,21},{7,23},{8,9},{10,... | collective-permute-start | bytes 5898248 | tf_op jit(solution)/shard_map/ppermute | solution.py:81
  63.8 18.0 %collective-permute-start.12 = (bf16[48,2560]{1,0:T(8,128)(2,1)}, bf16[48,2560]{1,0:T(8,128)(2,1)}, u32[]{:S(2)}, u32[]{:S(2)}) collective-permute-start(bf16[48,2560]{1,0:T(8,128)(2,1)} %get-tuple-element.202), channel_id=1, source_target_pairs={{0,4},{2,6},{4,0},{6,2},{1,5},{3,7},{5,1},{7,3},{8,12},{10,14},{12... | collective-permute-start | bytes 737288 | tf_op jit(solution)/shard_map/ppermute | solution.py:81
  66.1 22.0 %collective-permute-start.13 = (bf16[48,2560]{1,0:T(8,128)(2,1)}, bf16[48,2560]{1,0:T(8,128)(2,1)}, u32[]{:S(2)}, u32[]{:S(2)}) collective-permute-start(bf16[48,2560]{1,0:T(8,128)(2,1)} %get-tuple-element.202), channel_id=1, source_target_pairs={{0,6},{2,4},{4,2},{6,0},{1,7},{3,5},{5,3},{7,1},{8,14},{10,12},{12... | collective-permute-start | bytes 737288 | tf_op jit(solution)/shard_map/ppermute | solution.py:81
  91.8 21.3 %collective-permute-start.14 = (bf16[768,2560]{1,0:T(8,128)(2,1)S(1)}, bf16[768,2560]{1,0:T(8,128)(2,1)S(1)}, u32[]{:S(2)}, u32[]{:S(2)}) collective-permute-start(bf16[768,2560]{1,0:T(8,128)(2,1)S(1)} %pad_maximum_fusion.refs_0_), channel_id=1, source_target_pairs={{0,8},{2,10},{4,12},{6,14},{1,9},{3,11},{5,13},{7,15},{8,0},{10,2}... | collective-permute-start | bytes 11796488 | tf_op jit(solution)/shard_map/ppermute | solution.py:81
  115.7 24.9 %collective-permute-start.20 = (bf16[384,2560]{1,0:T(8,128)(2,1)}, bf16[384,2560]{1,0:T(8,128)(2,1)}, u32[]{:S(2)}, u32[]{:S(2)}) collective-permute-start(bf16[384,2560]{1,0:T(8,128)(2,1)} %pad_maximum_fusion.5), channel_id=1, source_target_pairs={{0,16},{2,18},{4,20},{6,22},{1,17},{3,19},{5,21},{7,23},{8,9},{10,... | collective-permute-start | bytes 5898248 | tf_op jit(solution)/shard_map/ppermute | solution.py:81
  116.3 21.8 %collective-permute-start.21 = (bf16[48,2560]{1,0:T(8,128)(2,1)}, bf16[48,2560]{1,0:T(8,128)(2,1)}, u32[]{:S(2)}, u32[]{:S(2)}) collective-permute-start(bf16[48,2560]{1,0:T(8,128)(2,1)} %get-tuple-element.221), channel_id=1, source_target_pairs={{0,4},{2,6},{4,0},{6,2},{1,5},{3,7},{5,1},{7,3},{8,12},{10,14},{12... | collective-permute-start | bytes 737288 | tf_op jit(solution)/shard_map/ppermute | solution.py:81
  116.8 22.5 %collective-permute-start.22 = (bf16[48,2560]{1,0:T(8,128)(2,1)}, bf16[48,2560]{1,0:T(8,128)(2,1)}, u32[]{:S(2)}, u32[]{:S(2)}) collective-permute-start(bf16[48,2560]{1,0:T(8,128)(2,1)} %get-tuple-element.221), channel_id=1, source_target_pairs={{0,6},{2,4},{4,2},{6,0},{1,7},{3,5},{5,3},{7,1},{8,14},{10,12},{12... | collective-permute-start | bytes 737288 | tf_op jit(solution)/shard_map/ppermute | solution.py:81
  157.5 24.7 %collective-permute-start.26 = (bf16[384,2560]{1,0:T(8,128)(2,1)S(1)}, bf16[384,2560]{1,0:T(8,128)(2,1)S(1)}, u32[]{:S(2)}, u32[]{:S(2)}) collective-permute-start(bf16[384,2560]{1,0:T(8,128)(2,1)S(1)} %pad_maximum_fusion.6), channel_id=1, source_target_pairs={{0,16},{2,18},{4,20},{6,22},{1,17},{3,19},{5,21},{7,23},{8,9},{10,... | collective-permute-start | bytes 5898248 | tf_op jit(solution)/shard_map/ppermute | solution.py:81
  158.4 22.9 %collective-permute-start.27 = (bf16[48,2560]{1,0:T(8,128)(2,1)S(1)}, bf16[48,2560]{1,0:T(8,128)(2,1)S(1)}, u32[]{:S(2)}, u32[]{:S(2)}) collective-permute-start(bf16[48,2560]{1,0:T(8,128)(2,1)S(1)} %get-tuple-element.235), channel_id=1, source_target_pairs={{0,4},{2,6},{4,0},{6,2},{1,5},{3,7},{5,1},{7,3},{8,12},{10,14},{12... | collective-permute-start | bytes 737288 | tf_op jit(solution)/shard_map/ppermute | solution.py:81
  160.9 21.2 %collective-permute-start.28 = (bf16[48,2560]{1,0:T(8,128)(2,1)S(1)}, bf16[48,2560]{1,0:T(8,128)(2,1)S(1)}, u32[]{:S(2)}, u32[]{:S(2)}) collective-permute-start(bf16[48,2560]{1,0:T(8,128)(2,1)S(1)} %get-tuple-element.235), channel_id=1, source_target_pairs={{0,6},{2,4},{4,2},{6,0},{1,7},{3,5},{5,3},{7,1},{8,14},{10,12},{12... | collective-permute-start | bytes 737288 | tf_op jit(solution)/shard_map/ppermute | solution.py:81
  196.8 29.7 %collective-permute-start.34 = (bf16[384,2560]{1,0:T(8,128)(2,1)S(1)}, bf16[384,2560]{1,0:T(8,128)(2,1)}, u32[]{:S(2)}, u32[]{:S(2)}) collective-permute-start(bf16[384,2560]{1,0:T(8,128)(2,1)S(1)} %pad_maximum_fusion.7), channel_id=1, source_target_pairs={{0,16},{2,18},{4,20},{6,22},{1,17},{3,19},{5,21},{7,23},{8,9},{10,... | collective-permute-start | bytes 5898248 | tf_op jit(solution)/shard_map/ppermute | solution.py:81
  198.4 30.9 %collective-permute-start.36 = (bf16[512,1024]{1,0:T(8,128)(2,1)S(1)}, bf16[512,1024]{1,0:T(8,128)(2,1)S(1)}, u32[]{:S(2)}, u32[]{:S(2)}) collective-permute-start(bf16[512,1024]{1,0:T(8,128)(2,1)S(1)} %copy-done.5), channel_id=1, source_target_pairs={{0,8},{2,10},{4,12},{6,14},{1,9},{3,11},{5,13},{7,15},{8,0},{10,2}... | collective-permute-start | bytes 3145736 | tf_op jit(solution)/shard_map/ppermute | solution.py:81
  198.4 30.9 %collective-permute-start.35 = (bf16[512,1024]{1,0:T(8,128)(2,1)S(1)}, bf16[512,1024]{1,0:T(8,128)(2,1)S(1)}, u32[]{:S(2)}, u32[]{:S(2)}) collective-permute-start(bf16[512,1024]{1,0:T(8,128)(2,1)S(1)} %get-tuple-element.258.refs_2_.refs_1_.normed_ref), channel_id=1, source_target_pairs={{0,8},{2,10},{4,12},{6,14},{1,9},{3,11},{5,13},{7,15},{8,0},{10,2}... | collective-permute-start | bytes 3145736 | tf_op jit(solution)/shard_map/ppermute | solution.py:81
  198.9 30.4 %collective-permute-start.37 = (bf16[512,512]{1,0:T(8,128)(2,1)S(1)}, bf16[512,512]{1,0:T(8,128)(2,1)S(1)}, u32[]{:S(2)}, u32[]{:S(2)}) collective-permute-start(bf16[512,512]{1,0:T(8,128)(2,1)S(1)} %get-tuple-element.259.refs_3_), channel_id=1, source_target_pairs={{0,8},{2,10},{4,12},{6,14},{1,9},{3,11},{5,13},{7,15},{8,0},{10,2}... | collective-permute-start | bytes 1572872 | tf_op jit(solution)/shard_map/ppermute | solution.py:81
  245.0 24.7 %collective-permute-start.40 = (bf16[384,2560]{1,0:T(8,128)(2,1)S(1)}, bf16[384,2560]{1,0:T(8,128)(2,1)S(1)}, u32[]{:S(2)}, u32[]{:S(2)}) collective-permute-start(bf16[384,2560]{1,0:T(8,128)(2,1)S(1)} %slice.297), channel_id=1, source_target_pairs={{0,16},{2,18},{4,20},{6,22},{1,17},{3,19},{5,21},{7,23},{8,9},{10,... | collective-permute-start | bytes 5898248 | tf_op jit(solution)/shard_map/ppermute | solution.py:81
  280.2 22.0 %collective-permute-start.42 = (bf16[192,2560]{1,0:T(8,128)(2,1)}, bf16[192,2560]{1,0:T(8,128)(2,1)}, u32[]{:S(2)}, u32[]{:S(2)}) collective-permute-start(bf16[192,2560]{1,0:T(8,128)(2,1)} %slice.299), channel_id=1, source_target_pairs={{0,1},{2,3},{4,5},{6,7},{1,0},{3,2},{5,4},{7,6},{8,24},{10,26},{12... | collective-permute-start | bytes 2949128 | tf_op jit(solution)/shard_map/ppermute | solution.py:81
  312.7 32.3 %collective-permute-start.49 = (bf16[384,2560]{1,0:T(8,128)(2,1)}, bf16[384,2560]{1,0:T(8,128)(2,1)}, u32[]{:S(2)}, u32[]{:S(2)}) collective-permute-start(bf16[384,2560]{1,0:T(8,128)(2,1)} %slice.305), channel_id=1, source_target_pairs={{0,16},{2,18},{4,20},{6,22},{1,17},{3,19},{5,21},{7,23},{8,9},{10,... | collective-permute-start | bytes 5898248 | tf_op jit(solution)/shard_map/ppermute | solution.py:81
  330.2 18.2 %collective-permute-start.54 = (bf16[3,512,768]{2,1,0:T(8,128)(2,1)}, bf16[3,512,768]{2,1,0:T(8,128)(2,1)S(1)}, u32[]{:S(2)}, u32[]{:S(2)}) collective-permute-start(bf16[3,512,768]{2,1,0:T(8,128)(2,1)} %get-tuple-element.314), channel_id=1, source_target_pairs={{0,8},{2,10},{4,12},{6,14},{1,9},{3,11},{5,13},{7,15},{8,0},{10,2}... | collective-permute-start | bytes 7077896 | tf_op jit(solution)/shard_map/ppermute | solution.py:81
  368.3 27.9 %collective-permute-start.60 = (bf16[384,2944]{1,0:T(8,128)(2,1)S(1)}, bf16[384,2944]{1,0:T(8,128)(2,1)S(1)}, u32[]{:S(2)}, u32[]{:S(2)}) collective-permute-start(bf16[384,2944]{1,0:T(8,128)(2,1)S(1)} %slice.309), channel_id=1, source_target_pairs={{0,16},{2,18},{4,20},{6,22},{1,17},{3,19},{5,21},{7,23},{8,9},{10,... | collective-permute-start | bytes 6782984 | tf_op jit(solution)/shard_map/ppermute | solution.py:81
  413.1 29.7 %collective-permute-start.68 = (bf16[384,2944]{1,0:T(8,128)(2,1)S(1)}, bf16[384,2944]{1,0:T(8,128)(2,1)S(1)}, u32[]{:S(2)}, u32[]{:S(2)}) collective-permute-start(bf16[384,2944]{1,0:T(8,128)(2,1)S(1)} %slice.320), channel_id=1, source_target_pairs={{0,16},{2,18},{4,20},{6,22},{1,17},{3,19},{5,21},{7,23},{8,9},{10,... | collective-permute-start | bytes 6782984 | tf_op jit(solution)/shard_map/ppermute | solution.py:81
  417.2 19.3 %collective-permute-start.66 = (bf16[48,2944]{1,0:T(8,128)(2,1)S(1)}, bf16[48,2944]{1,0:T(8,128)(2,1)S(1)}, u32[]{:S(2)}, u32[]{:S(2)}) collective-permute-start(bf16[48,2944]{1,0:T(8,128)(2,1)S(1)} %get-tuple-element.386), channel_id=1, source_target_pairs={{0,4},{2,6},{4,0},{6,2},{1,5},{3,7},{5,1},{7,3},{8,12},{10,14},{12... | collective-permute-start | bytes 847880 | tf_op jit(solution)/shard_map/ppermute | solution.py:81
  417.2 25.4 %collective-permute-start.67 = (bf16[48,2944]{1,0:T(8,128)(2,1)S(1)}, bf16[48,2944]{1,0:T(8,128)(2,1)S(1)}, u32[]{:S(2)}, u32[]{:S(2)}) collective-permute-start(bf16[48,2944]{1,0:T(8,128)(2,1)S(1)} %get-tuple-element.385), channel_id=1, source_target_pairs={{0,6},{2,4},{4,2},{6,0},{1,7},{3,5},{5,3},{7,1},{8,14},{10,12},{12... | collective-permute-start | bytes 847880 | tf_op jit(solution)/shard_map/ppermute | solution.py:81
  463.0 20.1 %collective-permute-start.72 = (bf16[48,2944]{1,0:T(8,128)(2,1)S(1)}, bf16[48,2944]{1,0:T(8,128)(2,1)S(1)}, u32[]{:S(2)}, u32[]{:S(2)}) collective-permute-start(bf16[48,2944]{1,0:T(8,128)(2,1)S(1)} %get-tuple-element.383), channel_id=1, source_target_pairs={{0,4},{2,6},{4,0},{6,2},{1,5},{3,7},{5,1},{7,3},{8,12},{10,14},{12... | collective-permute-start | bytes 847880 | tf_op jit(solution)/shard_map/ppermute | solution.py:81
  464.2 23.8 %collective-permute-start.73 = (bf16[48,2944]{1,0:T(8,128)(2,1)S(1)}, bf16[48,2944]{1,0:T(8,128)(2,1)S(1)}, u32[]{:S(2)}, u32[]{:S(2)}) collective-permute-start(bf16[48,2944]{1,0:T(8,128)(2,1)S(1)} %get-tuple-element.382), channel_id=1, source_target_pairs={{0,6},{2,4},{4,2},{6,0},{1,7},{3,5},{5,3},{7,1},{8,14},{10,12},{12... | collective-permute-start | bytes 847880 | tf_op jit(solution)/shard_map/ppermute | solution.py:81
  (144 other events, 1355.6 us)

commit v6 on v5

--- a/solution.py
+++ b/solution.py
@@ -869,12 +869,12 @@
     held = seq_step(lay, first_row, 1)
     a0 = fold(after(a0, held), lay.p2)
     _, input_grad, (head_own, head_other) = leave(0, k0, sums, (back_local, seq_rest(lay, held)), upstream)
-    a0, b1, head_own, head_other = fence(a0, b1, head_own, head_other)
+    (head_peer,) = swap(head_other)
+    a0, b1, head_own, head_peer = fence(a0, b1, head_own, head_peer)
 
     a0 = fold(a0, lay.p1)
     b1_parts = fold_parts(b1, lay.q, [], range(cut))
-    heads_0 = [head_own, *swap(head_other)]
-    b0 = grads_call(b0_own, b0_peer, ins_0, peer_0, heads=heads_0, head_rows=small_rows)
+    b0 = grads_call(b0_own, b0_peer, ins_0, peer_0, heads=(head_own, head_peer), head_rows=small_rows)
     a0, b0, b1, b1_parts = fence(a0, b0, b1, b1_parts)
 
     a0_done = fold(a0, lay.q, F32)

time: 502 us -> 499 us (level)
    ppermute x74, waiting for transfers between devices: 187 us -> 182 us  [permute(): return lax.ppermute(array, AXES, pairs)]
  transfers between devices with their start and end apart: 74 -> 74, of which waited for: 41 -> 42; matrix products, arithmetic and copies ran while one was open for 5% -> 5% of each run, Pallas kernels for 26% -> 27%
where the time goes in v6:
time: 499 us; the launch traced here: 492 us
  waiting for transfers between devices  182 us (36%)
  Pallas kernels  141 us (28%)
  starting transfers between devices  73.7 us (15%)
  local copies, waits for them, and re-layouts  63.1 us (13%)
  other arithmetic  30 us (6%)
    ppermute x74, waiting for transfers between devices, permute(): return lax.ppermute(array, AXES, pairs)  182 us
    pallas_call x6, Pallas kernels, wide_call(): pl.pallas_call(functools.partial(wide_kernel, names, mode, blocks, (width...  76.6 us
    ppermute x74, starting transfers between devices, permute(): return lax.ppermute(array, AXES, pairs)  73.7 us
    unnamed x193, local copies, waits for them, and re-layouts  47 us
    pallas_call x4, Pallas kernels, grads_call(): pl.pallas_call(functools.partial(grads_kernel, names, head_rows, sub), gr...  24.5 us
    concatenate x27, other arithmetic, cat(): return jnp.concatenate(arrays, axis=0)  13.7 us
    pallas_call x2, Pallas kernels, leave_call(): pl.pallas_call(functools.partial(leave_kernel, starts.shape[0], layer), o...  12.9 us
  transfers between devices with their start and end apart: 74, of which 42 were waited for; matrix products, arithmetic and copies ran while one was open for 5% of the time, Pallas kernels for 27%

profile of v6, /device:TPU:8, one launch (start us, length us, event | category | flops | bytes accessed | tf_op | source)
XLA Modules:
  0.0 491.9 jit_solution(7604974784322988713)
XLA Ops:
  25.7 6.6 %collective-permute-done.5 = bf16[48,2560]{1,0:T(8,128)(2,1)S(1)} collective-permute-done((bf16[48,2560]{1,0:T(8,128)(2,1)S(1)}, bf16[48,2560]{1,0:T(8,128)(2,1)S(1)}, u32[]{:S(2)}, u32[]{:S(2)}) %collective-permute-start.5) | collective-permute-done | bytes 245792 | tf_op jit(solution)/shard_map/ppermute | solution.py:81
  33.6 11.7 %collective-permute-done.7 = bf16[48,2560]{1,0:T(8,128)(2,1)S(1)} collective-permute-done((bf16[48,2560]{1,0:T(8,128)(2,1)S(1)}, bf16[48,2560]{1,0:T(8,128)(2,1)S(1)}, u32[]{:S(2)}, u32[]{:S(2)}) %collective-permute-start.7) | collective-permute-done | bytes 245792 | tf_op jit(solution)/shard_map/ppermute | solution.py:81
  49.8 9.9 %collective-permute-done.9 = bf16[192,2560]{1,0:T(8,128)(2,1)S(1)} collective-permute-done((bf16[192,2560]{1,0:T(8,128)(2,1)S(1)}, bf16[192,2560]{1,0:T(8,128)(2,1)S(1)}, u32[]{:S(2)}, u32[]{:S(2)}) %collective-permute-start.9) | collective-permute-done | bytes 983072 | tf_op jit(solution)/shard_map/ppermute | solution.py:81
  81.8 6.3 %collective-permute-done.13 = bf16[48,2560]{1,0:T(8,128)(2,1)} collective-permute-done((bf16[48,2560]{1,0:T(8,128)(2,1)}, bf16[48,2560]{1,0:T(8,128)(2,1)}, u32[]{:S(2)}, u32[]{:S(2)}) %collective-permute-start.13) | collective-permute-done | bytes 245792 | tf_op jit(solution)/shard_map/ppermute | solution.py:81
  129.1 7.3 %wide_fore.2 = (f32[512,1536]{1,0:T(8,128)S(1)}, f32[512,1536]{1,0:T(8,128)S(1)}, f32[512,1024]{1,0:T(8,128)S(1)}) custom-call(s32[1]{0:T(128)} %constant.172.clone.1.groups.places, bf16[768,2560]{1,0:T(8,128)(2,1)S(1)} %copy-done.1, bf16[768,2560]{1,0:T(8,128)(2,1)S(1)} %copy-done.15, bf16[512,1024]{1,0:T(8,128)(2,1)S(1)} %get-tuple-element.225.refs_2_.refs_1_.normed_ref, ...), custom_call_target="tpu_custom_call" | custom-call | flops 1000 | bytes 1000 | tf_op jit(solution)/shard_map/wide_fore/pallas_call | solution.py:586
  145.3 12.0 %collective-permute-done.24 = bf16[192,2560]{1,0:T(8,128)(2,1)S(1)} collective-permute-done((bf16[192,2560]{1,0:T(8,128)(2,1)S(1)}, bf16[192,2560]{1,0:T(8,128)(2,1)S(1)}, u32[]{:S(2)}, u32[]{:S(2)}) %collective-permute-start.24) | collective-permute-done | bytes 983072 | tf_op jit(solution)/shard_map/ppermute | solution.py:81
  162.4 7.3 %wide_fore.3 = (f32[512,1536]{1,0:T(8,128)S(1)}, f32[512,1536]{1,0:T(8,128)S(1)}, f32[512,1024]{1,0:T(8,128)S(1)}) custom-call(s32[1]{0:T(128)} %constant.172.clone.1.groups.places, bf16[768,2560]{1,0:T(8,128)(2,1)S(1)} %pad_maximum_fusion.1.refs_0_, bf16[768,2560]{1,0:T(8,128)(2,1)S(1)} %collective-permute-done.23.refs_1_, ...), custom_call_target="tpu_custom_call" | custom-call | flops 1000 | bytes 1000 | tf_op jit(solution)/shard_map/wide_fore/pallas_call | solution.py:586
  198.9 26.4 %wide_both.2 = (f32[512,1024]{1,0:T(8,128)S(1)}, f32[512,1024]{1,0:T(8,128)S(1)}, f32[512,512]{1,0:T(8,128)S(1)}, bf16[3,512,768]{2,1,0:T(8,128)(2,1)S(1)}, bf16[3,512,768]{2,1,0:T(8,128)(2,1)S(1)}) custom-call(s32[1]{0:T(128)} %constant.172.clone.1.groups.places, bf16[768,2560]{1,0:T(8,128)(2,1)S(1)} %pad_maximum_fusion.2.refs_0_, ...), custom_call_target="tpu_custom_call" | custom-call | flops 1000 | bytes 1000 | tf_op jit(solution)/shard_map/wide_both/pallas_call | solution.py:586
  229.9 9.9 %collective-permute-done.39.refs_4_ = bf16[3,512,768]{2,1,0:T(8,128)(2,1)S(1)} collective-permute-done((bf16[3,512,768]{2,1,0:T(8,128)(2,1)}, bf16[3,512,768]{2,1,0:T(8,128)(2,1)S(1)}, u32[]{:S(2)}, u32[]{:S(2)}) %collective-permute-start.39) | collective-permute-done | bytes 2359328 | tf_op jit(solution)/shard_map/ppermute | solution.py:81
  246.4 15.5 %wide_both.3 = (bf16[512,1024]{1,0:T(8,128)(2,1)}, f32[512,1024]{1,0:T(8,128)S(1)}, f32[512,512]{1,0:T(8,128)S(1)}, bf16[3,512,768]{2,1,0:T(8,128)(2,1)S(1)}, bf16[3,512,768]{2,1,0:T(8,128)(2,1)}) custom-call(s32[1]{0:T(128)} %constant.172.clone.1.groups.places, bf16[768,2560]{1,0:T(8,128)(2,1)S(1)} %pad_maximum_fusion.3.refs_0_, ...), custom_call_target="tpu_custom_call" | custom-call | flops 1000 | bytes 1000 | tf_op jit(solution)/shard_map/wide_both/pallas_call | solution.py:586
  261.9 7.8 %collective-permute-done.40 = bf16[384,2560]{1,0:T(8,128)(2,1)S(1)} collective-permute-done((bf16[384,2560]{1,0:T(8,128)(2,1)S(1)}, bf16[384,2560]{1,0:T(8,128)(2,1)S(1)}, u32[]{:S(2)}, u32[]{:S(2)}) %collective-permute-start.40) | collective-permute-done | bytes 1966112 | tf_op jit(solution)/shard_map/ppermute | solution.py:81
  290.3 6.5 %grads.5 = bf16[768,2560]{1,0:T(8,128)(2,1)S(1)} custom-call(s32[1]{0:T(128)} %constant.172.clone.1.groups.places, bf16[3,512,768]{2,1,0:T(8,128)(2,1)S(1)} %copy-done.54, bf16[512,1024]{1,0:T(8,128)(2,1)S(1)} %copy-done.9, bf16[512,1024]{1,0:T(8,128)(2,1)S(1)} %copy-done.6, bf16[512,512]{1,0:T(8,128)(2,1)S(1)} %copy-done.25, ...), custom_call_target="tpu_custom_call" | custom-call | flops 1000 | bytes 1000 | tf_op jit(solution)/shard_map/grads/pallas_call | solution.py:638
  305.2 6.0 %leave.2 = (f32[512,1024]{1,0:T(8,128)S(1)}, bf16[512,1024]{1,0:T(8,128)(2,1)S(1)}, bf16[256,1152]{1,0:T(8,128)(2,1)S(1)}, bf16[256,1152]{1,0:T(8,128)(2,1)S(1)}) custom-call(s32[3]{0:T(128)S(1)} %broadcast_subtract_fusion.scal, f32[8,1]{1,0:T(8,128)S(1)} %convert_select_fusion.1.hops_ref, f32[8,512]{1,0:T(8,128)S(1)} %pad_maximum_fusion.24.firsts_ref, ...), custom_call_target="tpu_custom_call" | custom-call | flops 1000 | bytes 1000 | tf_op jit(solution)/shard_map/leave/pallas_call | solution.py:413
  318.4 10.4 %wide_back.2 = (f32[512,1024]{1,0:T(8,128)S(1)}, f32[512,512]{1,0:T(8,128)S(1)}, bf16[3,512,768]{2,1,0:T(8,128)(2,1)S(1)}, bf16[3,512,768]{2,1,0:T(8,128)(2,1)}) custom-call(s32[1]{0:T(128)} %constant.172.clone.1.groups.places, bf16[768,2560]{1,0:T(8,128)(2,1)S(1)} %copy-done.2, bf16[768,2560]{1,0:T(8,128)(2,1)S(1)} %copy-done.16, ...), custom_call_target="tpu_custom_call" | custom-call | flops 1000 | bytes 1000 | tf_op jit(solution)/shard_map/wide_back/pallas_call | solution.py:586
  334.7 9.8 %wide_back.3 = (f32[512,1024]{1,0:T(8,128)S(1)}, f32[512,512]{1,0:T(8,128)S(1)}, bf16[3,512,768]{2,1,0:T(8,128)(2,1)S(1)}, bf16[3,512,768]{2,1,0:T(8,128)(2,1)S(1)}) custom-call(s32[1]{0:T(128)} %constant.172.clone.1.groups.places, bf16[768,2560]{1,0:T(8,128)(2,1)S(1)} %copy-done.4, bf16[768,2560]{1,0:T(8,128)(2,1)S(1)} %copy-done.18, ...), custom_call_target="tpu_custom_call" | custom-call | flops 1000 | bytes 1000 | tf_op jit(solution)/shard_map/wide_back/pallas_call | solution.py:586
  356.7 6.5 %grads.6 = bf16[768,2944]{1,0:T(8,128)(2,1)S(1)} custom-call(s32[1]{0:T(128)} %constant.172.clone.1.groups.places, bf16[3,512,768]{2,1,0:T(8,128)(2,1)S(1)} %copy-done.50, bf16[512,1024]{1,0:T(8,128)(2,1)S(1)} %get-tuple-element.225.refs_2_.refs_1_.normed_ref, bf16[512,1024]{1,0:T(8,128)(2,1)S(1)} %get-tuple-element.300.refs_4_.refs_2_, ...), custom_call_target="tpu_custom_call" | custom-call | flops 1000 | bytes 1000 | tf_op jit(solution)/shard_map/grads/pallas_call | solution.py:638
  378.6 6.8 %leave.3 = (f32[512,1024]{1,0:T(8,128)}, bf16[512,1024]{1,0:T(8,128)(2,1)}, bf16[256,1152]{1,0:T(8,128)(2,1)S(1)}, bf16[256,1152]{1,0:T(8,128)(2,1)S(1)}) custom-call(s32[3]{0:T(128)S(1)} %broadcast_subtract_fusion.scal, f32[8,1]{1,0:T(8,128)S(1)} %convert_select_fusion.1.hops_ref, f32[8,512]{1,0:T(8,128)S(1)} %pad_maximum_fusion.25.firsts_ref, ...), custom_call_target="tpu_custom_call" | custom-call | flops 1000 | bytes 1000 | tf_op jit(solution)/shard_map/leave/pallas_call | solution.py:413
  385.4 10.7 %collective-permute-done.60 = bf16[384,2944]{1,0:T(8,128)(2,1)S(1)} collective-permute-done((bf16[384,2944]{1,0:T(8,128)(2,1)S(1)}, bf16[384,2944]{1,0:T(8,128)(2,1)S(1)}, u32[]{:S(2)}, u32[]{:S(2)}) %collective-permute-start.60) | collective-permute-done | bytes 2261024 | tf_op jit(solution)/shard_map/ppermute | solution.py:81
  400.7 6.5 %grads.7 = bf16[768,2944]{1,0:T(8,128)(2,1)S(1)} custom-call(s32[1]{0:T(128)} %constant.172.clone.1.groups.places, bf16[3,512,768]{2,1,0:T(8,128)(2,1)S(1)} %get-tuple-element.351.refs_0_, bf16[512,1024]{1,0:T(8,128)(2,1)S(1)} %get-tuple-element.225.refs_2_.refs_1_.normed_ref, bf16[512,1024]{1,0:T(8,128)(2,1)S(1)} %get-tuple-element.300.refs_4_.refs_2_, ...), custom_call_target="tpu_custom_call" | custom-call | flops 1000 | bytes 1000 | tf_op jit(solution)/shard_map/grads/pallas_call | solution.py:638
  420.1 6.7 %collective-permute-done.65 = bf16[48,2944]{1,0:T(8,128)(2,1)S(1)} collective-permute-done((bf16[48,2944]{1,0:T(8,128)(2,1)S(1)}, bf16[48,2944]{1,0:T(8,128)(2,1)S(1)}, u32[]{:S(2)}, u32[]{:S(2)}) %collective-permute-start.65) | collective-permute-done | bytes 282656 | tf_op jit(solution)/shard_map/ppermute | solution.py:81
  426.8 8.6 %collective-permute-done.66 = bf16[48,2944]{1,0:T(8,128)(2,1)S(1)} collective-permute-done((bf16[48,2944]{1,0:T(8,128)(2,1)S(1)}, bf16[48,2944]{1,0:T(8,128)(2,1)S(1)}, u32[]{:S(2)}, u32[]{:S(2)}) %collective-permute-start.66) | collective-permute-done | bytes 282656 | tf_op jit(solution)/shard_map/ppermute | solution.py:81
  446.1 8.4 %collective-permute-done.69 = bf16[48,2560]{1,0:T(8,128)(2,1)} collective-permute-done((bf16[48,2560]{1,0:T(8,128)(2,1)}, bf16[48,2560]{1,0:T(8,128)(2,1)}, u32[]{:S(2)}, u32[]{:S(2)}) %collective-permute-start.69) | collective-permute-done | bytes 245792 | tf_op jit(solution)/shard_map/ppermute | solution.py:81
  464.7 7.7 %collective-permute-done.71 = bf16[48,2944]{1,0:T(8,128)(2,1)S(1)} collective-permute-done((bf16[48,2944]{1,0:T(8,128)(2,1)S(1)}, bf16[48,2944]{1,0:T(8,128)(2,1)S(1)}, u32[]{:S(2)}, u32[]{:S(2)}) %collective-permute-start.71) | collective-permute-done | bytes 282656 | tf_op jit(solution)/shard_map/ppermute | solution.py:81
  472.4 7.1 %collective-permute-done.72 = bf16[48,2944]{1,0:T(8,128)(2,1)S(1)} collective-permute-done((bf16[48,2944]{1,0:T(8,128)(2,1)S(1)}, bf16[48,2944]{1,0:T(8,128)(2,1)S(1)}, u32[]{:S(2)}, u32[]{:S(2)}) %collective-permute-start.72) | collective-permute-done | bytes 282656 | tf_op jit(solution)/shard_map/ppermute | solution.py:81
  (470 shorter events, 267.2 us)
Async XLA Ops:
  62.9 26.5 %collective-permute-start.11 = (bf16[384,2560]{1,0:T(8,128)(2,1)}, bf16[384,2560]{1,0:T(8,128)(2,1)}, u32[]{:S(2)}, u32[]{:S(2)}) collective-permute-start(bf16[384,2560]{1,0:T(8,128)(2,1)} %pad_maximum_fusion.4), channel_id=1, source_target_pairs={{0,16},{2,18},{4,20},{6,22},{1,17},{3,19},{5,21},{7,23},{8,9},{10,... | collective-permute-start | bytes 5898248 | tf_op jit(solution)/shard_map/ppermute | solution.py:81
  63.8 18.0 %collective-permute-start.12 = (bf16[48,2560]{1,0:T(8,128)(2,1)}, bf16[48,2560]{1,0:T(8,128)(2,1)}, u32[]{:S(2)}, u32[]{:S(2)}) collective-permute-start(bf16[48,2560]{1,0:T(8,128)(2,1)} %get-tuple-element.202), channel_id=1, source_target_pairs={{0,4},{2,6},{4,0},{6,2},{1,5},{3,7},{5,1},{7,3},{8,12},{10,14},{12... | collective-permute-start | bytes 737288 | tf_op jit(solution)/shard_map/ppermute | solution.py:81
  66.1 22.0 %collective-permute-start.13 = (bf16[48,2560]{1,0:T(8,128)(2,1)}, bf16[48,2560]{1,0:T(8,128)(2,1)}, u32[]{:S(2)}, u32[]{:S(2)}) collective-permute-start(bf16[48,2560]{1,0:T(8,128)(2,1)} %get-tuple-element.202), channel_id=1, source_target_pairs={{0,6},{2,4},{4,2},{6,0},{1,7},{3,5},{5,3},{7,1},{8,14},{10,12},{12... | collective-permute-start | bytes 737288 | tf_op jit(solution)/shard_map/ppermute | solution.py:81
  91.8 21.3 %collective-permute-start.14 = (bf16[768,2560]{1,0:T(8,128)(2,1)S(1)}, bf16[768,2560]{1,0:T(8,128)(2,1)S(1)}, u32[]{:S(2)}, u32[]{:S(2)}) collective-permute-start(bf16[768,2560]{1,0:T(8,128)(2,1)S(1)} %pad_maximum_fusion.refs_0_), channel_id=1, source_target_pairs={{0,8},{2,10},{4,12},{6,14},{1,9},{3,11},{5,13},{7,15},{8,0},{10,2}... | collective-permute-start | bytes 11796488 | tf_op jit(solution)/shard_map/ppermute | solution.py:81
  115.7 24.9 %collective-permute-start.20 = (bf16[384,2560]{1,0:T(8,128)(2,1)}, bf16[384,2560]{1,0:T(8,128)(2,1)}, u32[]{:S(2)}, u32[]{:S(2)}) collective-permute-start(bf16[384,2560]{1,0:T(8,128)(2,1)} %pad_maximum_fusion.5), channel_id=1, source_target_pairs={{0,16},{2,18},{4,20},{6,22},{1,17},{3,19},{5,21},{7,23},{8,9},{10,... | collective-permute-start | bytes 5898248 | tf_op jit(solution)/shard_map/ppermute | solution.py:81
  116.3 21.8 %collective-permute-start.21 = (bf16[48,2560]{1,0:T(8,128)(2,1)}, bf16[48,2560]{1,0:T(8,128)(2,1)}, u32[]{:S(2)}, u32[]{:S(2)}) collective-permute-start(bf16[48,2560]{1,0:T(8,128)(2,1)} %get-tuple-element.221), channel_id=1, source_target_pairs={{0,4},{2,6},{4,0},{6,2},{1,5},{3,7},{5,1},{7,3},{8,12},{10,14},{12... | collective-permute-start | bytes 737288 | tf_op jit(solution)/shard_map/ppermute | solution.py:81
  116.8 22.5 %collective-permute-start.22 = (bf16[48,2560]{1,0:T(8,128)(2,1)}, bf16[48,2560]{1,0:T(8,128)(2,1)}, u32[]{:S(2)}, u32[]{:S(2)}) collective-permute-start(bf16[48,2560]{1,0:T(8,128)(2,1)} %get-tuple-element.221), channel_id=1, source_target_pairs={{0,6},{2,4},{4,2},{6,0},{1,7},{3,5},{5,3},{7,1},{8,14},{10,12},{12... | collective-permute-start | bytes 737288 | tf_op jit(solution)/shard_map/ppermute | solution.py:81
  157.5 24.7 %collective-permute-start.26 = (bf16[384,2560]{1,0:T(8,128)(2,1)S(1)}, bf16[384,2560]{1,0:T(8,128)(2,1)S(1)}, u32[]{:S(2)}, u32[]{:S(2)}) collective-permute-start(bf16[384,2560]{1,0:T(8,128)(2,1)S(1)} %pad_maximum_fusion.6), channel_id=1, source_target_pairs={{0,16},{2,18},{4,20},{6,22},{1,17},{3,19},{5,21},{7,23},{8,9},{10,... | collective-permute-start | bytes 5898248 | tf_op jit(solution)/shard_map/ppermute | solution.py:81
  158.4 22.9 %collective-permute-start.27 = (bf16[48,2560]{1,0:T(8,128)(2,1)S(1)}, bf16[48,2560]{1,0:T(8,128)(2,1)S(1)}, u32[]{:S(2)}, u32[]{:S(2)}) collective-permute-start(bf16[48,2560]{1,0:T(8,128)(2,1)S(1)} %get-tuple-element.235), channel_id=1, source_target_pairs={{0,4},{2,6},{4,0},{6,2},{1,5},{3,7},{5,1},{7,3},{8,12},{10,14},{12... | collective-permute-start | bytes 737288 | tf_op jit(solution)/shard_map/ppermute | solution.py:81
  160.9 21.2 %collective-permute-start.28 = (bf16[48,2560]{1,0:T(8,128)(2,1)S(1)}, bf16[48,2560]{1,0:T(8,128)(2,1)S(1)}, u32[]{:S(2)}, u32[]{:S(2)}) collective-permute-start(bf16[48,2560]{1,0:T(8,128)(2,1)S(1)} %get-tuple-element.235), channel_id=1, source_target_pairs={{0,6},{2,4},{4,2},{6,0},{1,7},{3,5},{5,3},{7,1},{8,14},{10,12},{12... | collective-permute-start | bytes 737288 | tf_op jit(solution)/shard_map/ppermute | solution.py:81
  196.8 29.7 %collective-permute-start.34 = (bf16[384,2560]{1,0:T(8,128)(2,1)S(1)}, bf16[384,2560]{1,0:T(8,128)(2,1)}, u32[]{:S(2)}, u32[]{:S(2)}) collective-permute-start(bf16[384,2560]{1,0:T(8,128)(2,1)S(1)} %pad_maximum_fusion.7), channel_id=1, source_target_pairs={{0,16},{2,18},{4,20},{6,22},{1,17},{3,19},{5,21},{7,23},{8,9},{10,... | collective-permute-start | bytes 5898248 | tf_op jit(solution)/shard_map/ppermute | solution.py:81
  198.4 30.9 %collective-permute-start.36 = (bf16[512,1024]{1,0:T(8,128)(2,1)S(1)}, bf16[512,1024]{1,0:T(8,128)(2,1)S(1)}, u32[]{:S(2)}, u32[]{:S(2)}) collective-permute-start(bf16[512,1024]{1,0:T(8,128)(2,1)S(1)} %copy-done.5), channel_id=1, source_target_pairs={{0,8},{2,10},{4,12},{6,14},{1,9},{3,11},{5,13},{7,15},{8,0},{10,2}... | collective-permute-start | bytes 3145736 | tf_op jit(solution)/shard_map/ppermute | solution.py:81
  198.4 30.9 %collective-permute-start.35 = (bf16[512,1024]{1,0:T(8,128)(2,1)S(1)}, bf16[512,1024]{1,0:T(8,128)(2,1)S(1)}, u32[]{:S(2)}, u32[]{:S(2)}) collective-permute-start(bf16[512,1024]{1,0:T(8,128)(2,1)S(1)} %get-tuple-element.258.refs_2_.refs_1_.normed_ref), channel_id=1, source_target_pairs={{0,8},{2,10},{4,12},{6,14},{1,9},{3,11},{5,13},{7,15},{8,0},{10,2}... | collective-permute-start | bytes 3145736 | tf_op jit(solution)/shard_map/ppermute | solution.py:81
  198.9 30.4 %collective-permute-start.37 = (bf16[512,512]{1,0:T(8,128)(2,1)S(1)}, bf16[512,512]{1,0:T(8,128)(2,1)S(1)}, u32[]{:S(2)}, u32[]{:S(2)}) collective-permute-start(bf16[512,512]{1,0:T(8,128)(2,1)S(1)} %get-tuple-element.259.refs_3_), channel_id=1, source_target_pairs={{0,8},{2,10},{4,12},{6,14},{1,9},{3,11},{5,13},{7,15},{8,0},{10,2}... | collective-permute-start | bytes 1572872 | tf_op jit(solution)/shard_map/ppermute | solution.py:81
  245.0 24.7 %collective-permute-start.40 = (bf16[384,2560]{1,0:T(8,128)(2,1)S(1)}, bf16[384,2560]{1,0:T(8,128)(2,1)S(1)}, u32[]{:S(2)}, u32[]{:S(2)}) collective-permute-start(bf16[384,2560]{1,0:T(8,128)(2,1)S(1)} %slice.297), channel_id=1, source_target_pairs={{0,16},{2,18},{4,20},{6,22},{1,17},{3,19},{5,21},{7,23},{8,9},{10,... | collective-permute-start | bytes 5898248 | tf_op jit(solution)/shard_map/ppermute | solution.py:81
  280.2 22.0 %collective-permute-start.42 = (bf16[192,2560]{1,0:T(8,128)(2,1)}, bf16[192,2560]{1,0:T(8,128)(2,1)}, u32[]{:S(2)}, u32[]{:S(2)}) collective-permute-start(bf16[192,2560]{1,0:T(8,128)(2,1)} %slice.299), channel_id=1, source_target_pairs={{0,1},{2,3},{4,5},{6,7},{1,0},{3,2},{5,4},{7,6},{8,24},{10,26},{12... | collective-permute-start | bytes 2949128 | tf_op jit(solution)/shard_map/ppermute | solution.py:81
  312.7 32.3 %collective-permute-start.49 = (bf16[384,2560]{1,0:T(8,128)(2,1)}, bf16[384,2560]{1,0:T(8,128)(2,1)}, u32[]{:S(2)}, u32[]{:S(2)}) collective-permute-start(bf16[384,2560]{1,0:T(8,128)(2,1)} %slice.305), channel_id=1, source_target_pairs={{0,16},{2,18},{4,20},{6,22},{1,17},{3,19},{5,21},{7,23},{8,9},{10,... | collective-permute-start | bytes 5898248 | tf_op jit(solution)/shard_map/ppermute | solution.py:81
  330.2 18.2 %collective-permute-start.54 = (bf16[3,512,768]{2,1,0:T(8,128)(2,1)}, bf16[3,512,768]{2,1,0:T(8,128)(2,1)S(1)}, u32[]{:S(2)}, u32[]{:S(2)}) collective-permute-start(bf16[3,512,768]{2,1,0:T(8,128)(2,1)} %get-tuple-element.314), channel_id=1, source_target_pairs={{0,8},{2,10},{4,12},{6,14},{1,9},{3,11},{5,13},{7,15},{8,0},{10,2}... | collective-permute-start | bytes 7077896 | tf_op jit(solution)/shard_map/ppermute | solution.py:81
  368.3 27.9 %collective-permute-start.60 = (bf16[384,2944]{1,0:T(8,128)(2,1)S(1)}, bf16[384,2944]{1,0:T(8,128)(2,1)S(1)}, u32[]{:S(2)}, u32[]{:S(2)}) collective-permute-start(bf16[384,2944]{1,0:T(8,128)(2,1)S(1)} %slice.309), channel_id=1, source_target_pairs={{0,16},{2,18},{4,20},{6,22},{1,17},{3,19},{5,21},{7,23},{8,9},{10,... | collective-permute-start | bytes 6782984 | tf_op jit(solution)/shard_map/ppermute | solution.py:81
  413.0 27.9 %collective-permute-start.68 = (bf16[384,2944]{1,0:T(8,128)(2,1)S(1)}, bf16[384,2944]{1,0:T(8,128)(2,1)S(1)}, u32[]{:S(2)}, u32[]{:S(2)}) collective-permute-start(bf16[384,2944]{1,0:T(8,128)(2,1)S(1)} %slice.320), channel_id=1, source_target_pairs={{0,16},{2,18},{4,20},{6,22},{1,17},{3,19},{5,21},{7,23},{8,9},{10,... | collective-permute-start | bytes 6782984 | tf_op jit(solution)/shard_map/ppermute | solution.py:81
  417.7 17.7 %collective-permute-start.66 = (bf16[48,2944]{1,0:T(8,128)(2,1)S(1)}, bf16[48,2944]{1,0:T(8,128)(2,1)S(1)}, u32[]{:S(2)}, u32[]{:S(2)}) collective-permute-start(bf16[48,2944]{1,0:T(8,128)(2,1)S(1)} %get-tuple-element.386), channel_id=1, source_target_pairs={{0,4},{2,6},{4,0},{6,2},{1,5},{3,7},{5,1},{7,3},{8,12},{10,14},{12... | collective-permute-start | bytes 847880 | tf_op jit(solution)/shard_map/ppermute | solution.py:81
  417.7 22.7 %collective-permute-start.67 = (bf16[48,2944]{1,0:T(8,128)(2,1)S(1)}, bf16[48,2944]{1,0:T(8,128)(2,1)S(1)}, u32[]{:S(2)}, u32[]{:S(2)}) collective-permute-start(bf16[48,2944]{1,0:T(8,128)(2,1)S(1)} %get-tuple-element.385), channel_id=1, source_target_pairs={{0,6},{2,4},{4,2},{6,0},{1,7},{3,5},{5,3},{7,1},{8,14},{10,12},{12... | collective-permute-start | bytes 847880 | tf_op jit(solution)/shard_map/ppermute | solution.py:81
  463.0 16.4 %collective-permute-start.72 = (bf16[48,2944]{1,0:T(8,128)(2,1)S(1)}, bf16[48,2944]{1,0:T(8,128)(2,1)S(1)}, u32[]{:S(2)}, u32[]{:S(2)}) collective-permute-start(bf16[48,2944]{1,0:T(8,128)(2,1)S(1)} %get-tuple-element.383), channel_id=1, source_target_pairs={{0,4},{2,6},{4,0},{6,2},{1,5},{3,7},{5,1},{7,3},{8,12},{10,14},{12... | collective-permute-start | bytes 847880 | tf_op jit(solution)/shard_map/ppermute | solution.py:81
  463.1 21.6 %collective-permute-start.73 = (bf16[48,2944]{1,0:T(8,128)(2,1)S(1)}, bf16[48,2944]{1,0:T(8,128)(2,1)S(1)}, u32[]{:S(2)}, u32[]{:S(2)}) collective-permute-start(bf16[48,2944]{1,0:T(8,128)(2,1)S(1)} %get-tuple-element.382), channel_id=1, source_target_pairs={{0,6},{2,4},{4,2},{6,0},{1,7},{3,5},{5,3},{7,1},{8,14},{10,12},{12... | collective-permute-start | bytes 847880 | tf_op jit(solution)/shard_map/ppermute | solution.py:81
  (144 other events, 1366.0 us)

commit v7 on v6

--- a/solution.py
+++ b/solution.py
@@ -798,11 +798,9 @@
     (a_other,) = swap(a_own)
     plane_b = stage(after(line_b, held), lay.p1)
     lasts = seq_rest(lay, held)
-    pulled = pulls(shard_c, 0)
-    a_own, a_other, plane_b, shard_c, pulled, entered, lasts = fence(
-        a_own, a_other, plane_b, shard_c, pulled, entered, lasts
-    )
+    pulled = pulls(after(shard_c, lasts), 0)
     k0 = enter(0, tokens, entered, lasts)
+    a_own, a_other, plane_b, shard_c, pulled, k0 = fence(a_own, a_other, plane_b, shard_c, pulled, k0)
     b_own = stage(plane_b, lay.p2)
     pulled |= pulls(shard_c, 1, 2)
     *save_a, acc = wide_call("fore", a_own, a_other, k0["normed"], k0["mixed"], base=tokens)

time: 499 us -> 495 us (level)
  local copies, waits for them, and re-layouts: 63.1 us -> 50.4 us
  Pallas kernels: 141 us -> 146 us
    unnamed x193 -> x171, local copies, waits for them, and re-layouts: 47 us -> 34.4 us
  transfers between devices with their start and end apart: 74 -> 74, of which waited for: 42 -> 41; matrix products, arithmetic and copies ran while one was open for 5% -> 5% of each run, Pallas kernels for 27% -> 28%
where the time goes in v7:
time: 495 us; the launch traced here: 489 us
  waiting for transfers between devices  183 us (37%)
  Pallas kernels  146 us (29%)
  starting transfers between devices  77.3 us (16%)
  local copies, waits for them, and re-layouts  50.4 us (10%)
  other arithmetic  30.1 us (6%)
    ppermute x74, waiting for transfers between devices, permute(): return lax.ppermute(array, AXES, pairs)  183 us
    pallas_call x6, Pallas kernels, wide_call(): pl.pallas_call(functools.partial(wide_kernel, names, mode, blocks, (width...  81 us
    ppermute x74, starting transfers between devices, permute(): return lax.ppermute(array, AXES, pairs)  77.3 us
    unnamed x171, local copies, waits for them, and re-layouts  34.4 us
    pallas_call x4, Pallas kernels, grads_call(): pl.pallas_call(functools.partial(grads_kernel, names, head_rows, sub), gr...  24.5 us
    concatenate x27, other arithmetic, cat(): return jnp.concatenate(arrays, axis=0)  13.8 us
    pallas_call x2, Pallas kernels, leave_call(): pl.pallas_call(functools.partial(leave_kernel, starts.shape[0], layer), o...  12.8 us
  transfers between devices with their start and end apart: 74, of which 41 were waited for; matrix products, arithmetic and copies ran while one was open for 5% of the time, Pallas kernels for 28%

profile of v7, /device:TPU:8, one launch (start us, length us, event | category | flops | bytes accessed | tf_op | source)
XLA Modules:
  0.0 488.9 jit_solution(3622488736031612741)
XLA Ops:
  25.7 6.6 %collective-permute-done.5 = bf16[48,2560]{1,0:T(8,128)(2,1)S(1)} collective-permute-done((bf16[48,2560]{1,0:T(8,128)(2,1)S(1)}, bf16[48,2560]{1,0:T(8,128)(2,1)S(1)}, u32[]{:S(2)}, u32[]{:S(2)}) %collective-permute-start.5) | collective-permute-done | bytes 245792 | tf_op jit(solution)/shard_map/ppermute | solution.py:81
  33.6 11.7 %collective-permute-done.7 = bf16[48,2560]{1,0:T(8,128)(2,1)S(1)} collective-permute-done((bf16[48,2560]{1,0:T(8,128)(2,1)S(1)}, bf16[48,2560]{1,0:T(8,128)(2,1)S(1)}, u32[]{:S(2)}, u32[]{:S(2)}) %collective-permute-start.7) | collective-permute-done | bytes 245792 | tf_op jit(solution)/shard_map/ppermute | solution.py:81
  49.8 9.8 %collective-permute-done.9 = bf16[192,2560]{1,0:T(8,128)(2,1)S(1)} collective-permute-done((bf16[192,2560]{1,0:T(8,128)(2,1)S(1)}, bf16[192,2560]{1,0:T(8,128)(2,1)S(1)}, u32[]{:S(2)}, u32[]{:S(2)}) %collective-permute-start.9) | collective-permute-done | bytes 983072 | tf_op jit(solution)/shard_map/ppermute | solution.py:81
  118.4 9.5 %wide_fore.2 = (f32[512,1536]{1,0:T(8,128)S(1)}, f32[512,1536]{1,0:T(8,128)S(1)}, f32[512,1024]{1,0:T(8,128)S(1)}) custom-call(s32[1]{0:T(128)} %constant.172.clone.1.groups.places, bf16[768,2560]{1,0:T(8,128)(2,1)} %pad_maximum_fusion.refs_0_, bf16[768,2560]{1,0:T(8,128)(2,1)} %collective-permute-done.14.refs_1_, ...), custom_call_target="tpu_custom_call" | custom-call | flops 1000 | bytes 1000 | tf_op jit(solution)/shard_map/wide_fore/pallas_call | solution.py:586
  130.4 6.2 %collective-permute-done.22 = bf16[48,2560]{1,0:T(8,128)(2,1)S(1)} collective-permute-done((bf16[48,2560]{1,0:T(8,128)(2,1)S(1)}, bf16[48,2560]{1,0:T(8,128)(2,1)S(1)}, u32[]{:S(2)}, u32[]{:S(2)}) %collective-permute-start.22) | collective-permute-done | bytes 245792 | tf_op jit(solution)/shard_map/ppermute | solution.py:81
  143.5 10.8 %collective-permute-done.24 = bf16[192,2560]{1,0:T(8,128)(2,1)S(1)} collective-permute-done((bf16[192,2560]{1,0:T(8,128)(2,1)S(1)}, bf16[192,2560]{1,0:T(8,128)(2,1)S(1)}, u32[]{:S(2)}, u32[]{:S(2)}) %collective-permute-start.24) | collective-permute-done | bytes 983072 | tf_op jit(solution)/shard_map/ppermute | solution.py:81
  157.8 7.3 %wide_fore.3 = (f32[512,1536]{1,0:T(8,128)S(1)}, f32[512,1536]{1,0:T(8,128)S(1)}, f32[512,1024]{1,0:T(8,128)S(1)}) custom-call(s32[1]{0:T(128)} %constant.172.clone.1.groups.places, bf16[768,2560]{1,0:T(8,128)(2,1)S(1)} %pad_maximum_fusion.1.refs_0_, bf16[768,2560]{1,0:T(8,128)(2,1)S(1)} %collective-permute-done.23.refs_1_, ...), custom_call_target="tpu_custom_call" | custom-call | flops 1000 | bytes 1000 | tf_op jit(solution)/shard_map/wide_fore/pallas_call | solution.py:586
  195.3 26.4 %wide_both.2 = (f32[512,1024]{1,0:T(8,128)S(1)}, f32[512,1024]{1,0:T(8,128)S(1)}, f32[512,512]{1,0:T(8,128)S(1)}, bf16[3,512,768]{2,1,0:T(8,128)(2,1)S(1)}, bf16[3,512,768]{2,1,0:T(8,128)(2,1)S(1)}) custom-call(s32[1]{0:T(128)} %constant.172.clone.1.groups.places, bf16[768,2560]{1,0:T(8,128)(2,1)S(1)} %pad_maximum_fusion.2.refs_0_, ...), custom_call_target="tpu_custom_call" | custom-call | flops 1000 | bytes 1000 | tf_op jit(solution)/shard_map/wide_both/pallas_call | solution.py:586
  226.3 9.9 %collective-permute-done.39.refs_4_ = bf16[3,512,768]{2,1,0:T(8,128)(2,1)S(1)} collective-permute-done((bf16[3,512,768]{2,1,0:T(8,128)(2,1)}, bf16[3,512,768]{2,1,0:T(8,128)(2,1)S(1)}, u32[]{:S(2)}, u32[]{:S(2)}) %collective-permute-start.39) | collective-permute-done | bytes 2359328 | tf_op jit(solution)/shard_map/ppermute | solution.py:81
  243.2 15.5 %wide_both.3 = (bf16[512,1024]{1,0:T(8,128)(2,1)}, f32[512,1024]{1,0:T(8,128)S(1)}, f32[512,512]{1,0:T(8,128)S(1)}, bf16[3,512,768]{2,1,0:T(8,128)(2,1)S(1)}, bf16[3,512,768]{2,1,0:T(8,128)(2,1)}) custom-call(s32[1]{0:T(128)} %constant.172.clone.1.groups.places, bf16[768,2560]{1,0:T(8,128)(2,1)S(1)} %pad_maximum_fusion.3.refs_0_, ...), custom_call_target="tpu_custom_call" | custom-call | flops 1000 | bytes 1000 | tf_op jit(solution)/shard_map/wide_both/pallas_call | solution.py:586
  258.6 7.4 %collective-permute-done.40 = bf16[384,2560]{1,0:T(8,128)(2,1)S(1)} collective-permute-done((bf16[384,2560]{1,0:T(8,128)(2,1)S(1)}, bf16[384,2560]{1,0:T(8,128)(2,1)S(1)}, u32[]{:S(2)}, u32[]{:S(2)}) %collective-permute-start.40) | collective-permute-done | bytes 1966112 | tf_op jit(solution)/shard_map/ppermute | solution.py:81
  286.7 6.5 %grads.5 = bf16[768,2560]{1,0:T(8,128)(2,1)S(1)} custom-call(s32[1]{0:T(128)} %constant.172.clone.1.groups.places, bf16[3,512,768]{2,1,0:T(8,128)(2,1)S(1)} %copy-done.48, bf16[512,1024]{1,0:T(8,128)(2,1)S(1)} %copy-done.6, bf16[512,1024]{1,0:T(8,128)(2,1)S(1)} %copy-done.3, bf16[512,512]{1,0:T(8,128)(2,1)S(1)} %copy-done.19, ...), custom_call_target="tpu_custom_call" | custom-call | flops 1000 | bytes 1000 | tf_op jit(solution)/shard_map/grads/pallas_call | solution.py:638
  301.6 6.1 %leave.2 = (f32[512,1024]{1,0:T(8,128)S(1)}, bf16[512,1024]{1,0:T(8,128)(2,1)S(1)}, bf16[256,1152]{1,0:T(8,128)(2,1)S(1)}, bf16[256,1152]{1,0:T(8,128)(2,1)S(1)}) custom-call(s32[3]{0:T(128)S(1)} %broadcast_subtract_fusion.scal, f32[8,1]{1,0:T(8,128)S(1)} %convert_select_fusion.1.hops_ref, f32[8,512]{1,0:T(8,128)S(1)} %pad_maximum_fusion.24.firsts_ref, ...), custom_call_target="tpu_custom_call" | custom-call | flops 1000 | bytes 1000 | tf_op jit(solution)/shard_map/leave/pallas_call | solution.py:413
  312.9 12.6 %wide_back.2 = (f32[512,1024]{1,0:T(8,128)S(1)}, f32[512,512]{1,0:T(8,128)S(1)}, bf16[3,512,768]{2,1,0:T(8,128)(2,1)S(1)}, bf16[3,512,768]{2,1,0:T(8,128)(2,1)}) custom-call(s32[1]{0:T(128)} %constant.172.clone.1.groups.places, bf16[768,2560]{1,0:T(8,128)(2,1)} %pad_maximum_fusion.refs_0_, bf16[768,2560]{1,0:T(8,128)(2,1)} %collective-permute-done.14.refs_1_, ...), custom_call_target="tpu_custom_call" | custom-call | flops 1000 | bytes 1000 | tf_op jit(solution)/shard_map/wide_back/pallas_call | solution.py:586
  331.9 9.8 %wide_back.3 = (f32[512,1024]{1,0:T(8,128)S(1)}, f32[512,512]{1,0:T(8,128)S(1)}, bf16[3,512,768]{2,1,0:T(8,128)(2,1)S(1)}, bf16[3,512,768]{2,1,0:T(8,128)(2,1)S(1)}) custom-call(s32[1]{0:T(128)} %constant.172.clone.1.groups.places, bf16[768,2560]{1,0:T(8,128)(2,1)S(1)} %copy-done.1, bf16[768,2560]{1,0:T(8,128)(2,1)S(1)} %copy-done.12, ...), custom_call_target="tpu_custom_call" | custom-call | flops 1000 | bytes 1000 | tf_op jit(solution)/shard_map/wide_back/pallas_call | solution.py:586
  354.5 6.5 %grads.6 = bf16[768,2944]{1,0:T(8,128)(2,1)S(1)} custom-call(s32[1]{0:T(128)} %constant.172.clone.1.groups.places, bf16[3,512,768]{2,1,0:T(8,128)(2,1)S(1)} %copy-done.44, bf16[512,1024]{1,0:T(8,128)(2,1)S(1)} %get-tuple-element.232.refs_2_.refs_1_.normed_ref, bf16[512,1024]{1,0:T(8,128)(2,1)S(1)} %get-tuple-element.304.refs_4_.refs_2_, ...), custom_call_target="tpu_custom_call" | custom-call | flops 1000 | bytes 1000 | tf_op jit(solution)/shard_map/grads/pallas_call | solution.py:638
  375.3 6.8 %leave.3 = (f32[512,1024]{1,0:T(8,128)}, bf16[512,1024]{1,0:T(8,128)(2,1)}, bf16[256,1152]{1,0:T(8,128)(2,1)S(1)}, bf16[256,1152]{1,0:T(8,128)(2,1)S(1)}) custom-call(s32[3]{0:T(128)S(1)} %broadcast_subtract_fusion.scal, f32[8,1]{1,0:T(8,128)S(1)} %convert_select_fusion.1.hops_ref, f32[8,512]{1,0:T(8,128)S(1)} %pad_maximum_fusion.25.firsts_ref, ...), custom_call_target="tpu_custom_call" | custom-call | flops 1000 | bytes 1000 | tf_op jit(solution)/shard_map/leave/pallas_call | solution.py:413
  382.1 11.1 %collective-permute-done.60 = bf16[384,2944]{1,0:T(8,128)(2,1)S(1)} collective-permute-done((bf16[384,2944]{1,0:T(8,128)(2,1)S(1)}, bf16[384,2944]{1,0:T(8,128)(2,1)S(1)}, u32[]{:S(2)}, u32[]{:S(2)}) %collective-permute-start.60) | collective-permute-done | bytes 2261024 | tf_op jit(solution)/shard_map/ppermute | solution.py:81
  398.0 6.5 %grads.7 = bf16[768,2944]{1,0:T(8,128)(2,1)S(1)} custom-call(s32[1]{0:T(128)} %constant.172.clone.1.groups.places, bf16[3,512,768]{2,1,0:T(8,128)(2,1)S(1)} %get-tuple-element.357.refs_0_, bf16[512,1024]{1,0:T(8,128)(2,1)S(1)} %get-tuple-element.232.refs_2_.refs_1_.normed_ref, bf16[512,1024]{1,0:T(8,128)(2,1)S(1)} %get-tuple-element.304.refs_4_.refs_2_, ...), custom_call_target="tpu_custom_call" | custom-call | flops 1000 | bytes 1000 | tf_op jit(solution)/shard_map/grads/pallas_call | solution.py:638
  416.2 5.4 %collective-permute-done.65 = bf16[48,2944]{1,0:T(8,128)(2,1)S(1)} collective-permute-done((bf16[48,2944]{1,0:T(8,128)(2,1)S(1)}, bf16[48,2944]{1,0:T(8,128)(2,1)S(1)}, u32[]{:S(2)}, u32[]{:S(2)}) %collective-permute-start.65) | collective-permute-done | bytes 282656 | tf_op jit(solution)/shard_map/ppermute | solution.py:81
  421.6 9.5 %collective-permute-done.66 = bf16[48,2944]{1,0:T(8,128)(2,1)S(1)} collective-permute-done((bf16[48,2944]{1,0:T(8,128)(2,1)S(1)}, bf16[48,2944]{1,0:T(8,128)(2,1)S(1)}, u32[]{:S(2)}, u32[]{:S(2)}) %collective-permute-start.66) | collective-permute-done | bytes 282656 | tf_op jit(solution)/shard_map/ppermute | solution.py:81
  443.6 7.3 %collective-permute-done.69 = bf16[48,2560]{1,0:T(8,128)(2,1)} collective-permute-done((bf16[48,2560]{1,0:T(8,128)(2,1)}, bf16[48,2560]{1,0:T(8,128)(2,1)}, u32[]{:S(2)}, u32[]{:S(2)}) %collective-permute-start.69) | collective-permute-done | bytes 245792 | tf_op jit(solution)/shard_map/ppermute | solution.py:81
  461.9 7.6 %collective-permute-done.71 = bf16[48,2944]{1,0:T(8,128)(2,1)S(1)} collective-permute-done((bf16[48,2944]{1,0:T(8,128)(2,1)S(1)}, bf16[48,2944]{1,0:T(8,128)(2,1)S(1)}, u32[]{:S(2)}, u32[]{:S(2)}) %collective-permute-start.71) | collective-permute-done | bytes 282656 | tf_op jit(solution)/shard_map/ppermute | solution.py:81
  469.5 7.1 %collective-permute-done.72 = bf16[48,2944]{1,0:T(8,128)(2,1)S(1)} collective-permute-done((bf16[48,2944]{1,0:T(8,128)(2,1)S(1)}, bf16[48,2944]{1,0:T(8,128)(2,1)S(1)}, u32[]{:S(2)}, u32[]{:S(2)}) %collective-permute-start.72) | collective-permute-done | bytes 282656 | tf_op jit(solution)/shard_map/ppermute | solution.py:81
  (448 shorter events, 262.6 us)
Async XLA Ops:
  62.8 27.4 %collective-permute-start.11 = (bf16[384,2560]{1,0:T(8,128)(2,1)}, bf16[384,2560]{1,0:T(8,128)(2,1)}, u32[]{:S(2)}, u32[]{:S(2)}) collective-permute-start(bf16[384,2560]{1,0:T(8,128)(2,1)} %pad_maximum_fusion.4), channel_id=1, source_target_pairs={{0,16},{2,18},{4,20},{6,22},{1,17},{3,19},{5,21},{7,23},{8,9},{10,... | collective-permute-start | bytes 5898248 | tf_op jit(solution)/shard_map/ppermute | solution.py:81
  63.7 18.9 %collective-permute-start.12 = (bf16[48,2560]{1,0:T(8,128)(2,1)}, bf16[48,2560]{1,0:T(8,128)(2,1)}, u32[]{:S(2)}, u32[]{:S(2)}) collective-permute-start(bf16[48,2560]{1,0:T(8,128)(2,1)} %get-tuple-element.205), channel_id=1, source_target_pairs={{0,4},{2,6},{4,0},{6,2},{1,5},{3,7},{5,1},{7,3},{8,12},{10,14},{12... | collective-permute-start | bytes 737288 | tf_op jit(solution)/shard_map/ppermute | solution.py:81
  66.0 22.0 %collective-permute-start.13 = (bf16[48,2560]{1,0:T(8,128)(2,1)}, bf16[48,2560]{1,0:T(8,128)(2,1)}, u32[]{:S(2)}, u32[]{:S(2)}) collective-permute-start(bf16[48,2560]{1,0:T(8,128)(2,1)} %get-tuple-element.205), channel_id=1, source_target_pairs={{0,6},{2,4},{4,2},{6,0},{1,7},{3,5},{5,3},{7,1},{8,14},{10,12},{12... | collective-permute-start | bytes 737288 | tf_op jit(solution)/shard_map/ppermute | solution.py:81
  94.6 20.4 %collective-permute-start.14 = (bf16[768,2560]{1,0:T(8,128)(2,1)}, bf16[768,2560]{1,0:T(8,128)(2,1)}, u32[]{:S(2)}, u32[]{:S(2)}) collective-permute-start(bf16[768,2560]{1,0:T(8,128)(2,1)} %pad_maximum_fusion.refs_0_), channel_id=1, source_target_pairs={{0,8},{2,10},{4,12},{6,14},{1,9},{3,11},{5,13},{7,15},{8,0},{10,2}... | collective-permute-start | bytes 11796488 | tf_op jit(solution)/shard_map/ppermute | solution.py:81
  115.0 24.7 %collective-permute-start.20 = (bf16[384,2560]{1,0:T(8,128)(2,1)S(1)}, bf16[384,2560]{1,0:T(8,128)(2,1)S(1)}, u32[]{:S(2)}, u32[]{:S(2)}) collective-permute-start(bf16[384,2560]{1,0:T(8,128)(2,1)S(1)} %pad_maximum_fusion.5), channel_id=1, source_target_pairs={{0,16},{2,18},{4,20},{6,22},{1,17},{3,19},{5,21},{7,23},{8,9},{10,... | collective-permute-start | bytes 5898248 | tf_op jit(solution)/shard_map/ppermute | solution.py:81
  117.0 19.6 %collective-permute-start.22 = (bf16[48,2560]{1,0:T(8,128)(2,1)S(1)}, bf16[48,2560]{1,0:T(8,128)(2,1)S(1)}, u32[]{:S(2)}, u32[]{:S(2)}) collective-permute-start(bf16[48,2560]{1,0:T(8,128)(2,1)S(1)} %copy-done.77), channel_id=1, source_target_pairs={{0,6},{2,4},{4,2},{6,0},{1,7},{3,5},{5,3},{7,1},{8,14},{10,12},{12... | collective-permute-start | bytes 737288 | tf_op jit(solution)/shard_map/ppermute | solution.py:81
  154.4 25.3 %collective-permute-start.26 = (bf16[384,2560]{1,0:T(8,128)(2,1)S(1)}, bf16[384,2560]{1,0:T(8,128)(2,1)S(1)}, u32[]{:S(2)}, u32[]{:S(2)}) collective-permute-start(bf16[384,2560]{1,0:T(8,128)(2,1)S(1)} %pad_maximum_fusion.6), channel_id=1, source_target_pairs={{0,16},{2,18},{4,20},{6,22},{1,17},{3,19},{5,21},{7,23},{8,9},{10,... | collective-permute-start | bytes 5898248 | tf_op jit(solution)/shard_map/ppermute | solution.py:81
  154.9 21.9 %collective-permute-start.27 = (bf16[48,2560]{1,0:T(8,128)(2,1)S(1)}, bf16[48,2560]{1,0:T(8,128)(2,1)S(1)}, u32[]{:S(2)}, u32[]{:S(2)}) collective-permute-start(bf16[48,2560]{1,0:T(8,128)(2,1)S(1)} %get-tuple-element.239), channel_id=1, source_target_pairs={{0,4},{2,6},{4,0},{6,2},{1,5},{3,7},{5,1},{7,3},{8,12},{10,14},{12... | collective-permute-start | bytes 737288 | tf_op jit(solution)/shard_map/ppermute | solution.py:81
  156.3 23.3 %collective-permute-start.28 = (bf16[48,2560]{1,0:T(8,128)(2,1)S(1)}, bf16[48,2560]{1,0:T(8,128)(2,1)S(1)}, u32[]{:S(2)}, u32[]{:S(2)}) collective-permute-start(bf16[48,2560]{1,0:T(8,128)(2,1)S(1)} %get-tuple-element.239), channel_id=1, source_target_pairs={{0,6},{2,4},{4,2},{6,0},{1,7},{3,5},{5,3},{7,1},{8,14},{10,12},{12... | collective-permute-start | bytes 737288 | tf_op jit(solution)/shard_map/ppermute | solution.py:81
  194.4 28.6 %collective-permute-start.34 = (bf16[384,2560]{1,0:T(8,128)(2,1)S(1)}, bf16[384,2560]{1,0:T(8,128)(2,1)}, u32[]{:S(2)}, u32[]{:S(2)}) collective-permute-start(bf16[384,2560]{1,0:T(8,128)(2,1)S(1)} %pad_maximum_fusion.7), channel_id=1, source_target_pairs={{0,16},{2,18},{4,20},{6,22},{1,17},{3,19},{5,21},{7,23},{8,9},{10,... | collective-permute-start | bytes 5898248 | tf_op jit(solution)/shard_map/ppermute | solution.py:81
  194.8 30.9 %collective-permute-start.36 = (bf16[512,1024]{1,0:T(8,128)(2,1)S(1)}, bf16[512,1024]{1,0:T(8,128)(2,1)S(1)}, u32[]{:S(2)}, u32[]{:S(2)}) collective-permute-start(bf16[512,1024]{1,0:T(8,128)(2,1)S(1)} %copy-done.2), channel_id=1, source_target_pairs={{0,8},{2,10},{4,12},{6,14},{1,9},{3,11},{5,13},{7,15},{8,0},{10,2}... | collective-permute-start | bytes 3145736 | tf_op jit(solution)/shard_map/ppermute | solution.py:81
  194.8 30.9 %collective-permute-start.35 = (bf16[512,1024]{1,0:T(8,128)(2,1)S(1)}, bf16[512,1024]{1,0:T(8,128)(2,1)S(1)}, u32[]{:S(2)}, u32[]{:S(2)}) collective-permute-start(bf16[512,1024]{1,0:T(8,128)(2,1)S(1)} %get-tuple-element.262.refs_2_.refs_1_.normed_ref), channel_id=1, source_target_pairs={{0,8},{2,10},{4,12},{6,14},{1,9},{3,11},{5,13},{7,15},{8,0},{10,2}... | collective-permute-start | bytes 3145736 | tf_op jit(solution)/shard_map/ppermute | solution.py:81
  195.3 30.4 %collective-permute-start.37 = (bf16[512,512]{1,0:T(8,128)(2,1)S(1)}, bf16[512,512]{1,0:T(8,128)(2,1)S(1)}, u32[]{:S(2)}, u32[]{:S(2)}) collective-permute-start(bf16[512,512]{1,0:T(8,128)(2,1)S(1)} %get-tuple-element.263.refs_3_), channel_id=1, source_target_pairs={{0,8},{2,10},{4,12},{6,14},{1,9},{3,11},{5,13},{7,15},{8,0},{10,2}... | collective-permute-start | bytes 1572872 | tf_op jit(solution)/shard_map/ppermute | solution.py:81
  241.4 24.7 %collective-permute-start.40 = (bf16[384,2560]{1,0:T(8,128)(2,1)S(1)}, bf16[384,2560]{1,0:T(8,128)(2,1)S(1)}, u32[]{:S(2)}, u32[]{:S(2)}) collective-permute-start(bf16[384,2560]{1,0:T(8,128)(2,1)S(1)} %slice.297), channel_id=1, source_target_pairs={{0,16},{2,18},{4,20},{6,22},{1,17},{3,19},{5,21},{7,23},{8,9},{10,... | collective-permute-start | bytes 5898248 | tf_op jit(solution)/shard_map/ppermute | solution.py:81
  276.5 22.3 %collective-permute-start.42 = (bf16[192,2560]{1,0:T(8,128)(2,1)}, bf16[192,2560]{1,0:T(8,128)(2,1)}, u32[]{:S(2)}, u32[]{:S(2)}) collective-permute-start(bf16[192,2560]{1,0:T(8,128)(2,1)} %slice.299), channel_id=1, source_target_pairs={{0,1},{2,3},{4,5},{6,7},{1,0},{3,2},{5,4},{7,6},{8,24},{10,26},{12... | collective-permute-start | bytes 2949128 | tf_op jit(solution)/shard_map/ppermute | solution.py:81
  309.1 33.0 %collective-permute-start.49 = (bf16[384,2560]{1,0:T(8,128)(2,1)}, bf16[384,2560]{1,0:T(8,128)(2,1)}, u32[]{:S(2)}, u32[]{:S(2)}) collective-permute-start(bf16[384,2560]{1,0:T(8,128)(2,1)} %slice.305), channel_id=1, source_target_pairs={{0,16},{2,18},{4,20},{6,22},{1,17},{3,19},{5,21},{7,23},{8,9},{10,... | collective-permute-start | bytes 5898248 | tf_op jit(solution)/shard_map/ppermute | solution.py:81
  310.8 16.1 %collective-permute-start.46 = (bf16[48,2560]{1,0:T(8,128)(2,1)S(1)}, bf16[48,2560]{1,0:T(8,128)(2,1)S(1)}, u32[]{:S(2)}, u32[]{:S(2)}) collective-permute-start(bf16[48,2560]{1,0:T(8,128)(2,1)S(1)} %get-tuple-element.401), channel_id=1, source_target_pairs={{0,2},{2,0},{4,6},{6,4},{1,3},{3,1},{5,7},{7,5},{8,10},{10,8},{12,... | collective-permute-start | bytes 737288 | tf_op jit(solution)/shard_map/ppermute | solution.py:81
  327.0 18.3 %collective-permute-start.54 = (bf16[3,512,768]{2,1,0:T(8,128)(2,1)}, bf16[3,512,768]{2,1,0:T(8,128)(2,1)S(1)}, u32[]{:S(2)}, u32[]{:S(2)}) collective-permute-start(bf16[3,512,768]{2,1,0:T(8,128)(2,1)} %get-tuple-element.318), channel_id=1, source_target_pairs={{0,8},{2,10},{4,12},{6,14},{1,9},{3,11},{5,13},{7,15},{8,0},{10,2}... | collective-permute-start | bytes 7077896 | tf_op jit(solution)/shard_map/ppermute | solution.py:81
  365.3 27.9 %collective-permute-start.60 = (bf16[384,2944]{1,0:T(8,128)(2,1)S(1)}, bf16[384,2944]{1,0:T(8,128)(2,1)S(1)}, u32[]{:S(2)}, u32[]{:S(2)}) collective-permute-start(bf16[384,2944]{1,0:T(8,128)(2,1)S(1)} %slice.309), channel_id=1, source_target_pairs={{0,16},{2,18},{4,20},{6,22},{1,17},{3,19},{5,21},{7,23},{8,9},{10,... | collective-permute-start | bytes 6782984 | tf_op jit(solution)/shard_map/ppermute | solution.py:81
  410.1 27.9 %collective-permute-start.68 = (bf16[384,2944]{1,0:T(8,128)(2,1)S(1)}, bf16[384,2944]{1,0:T(8,128)(2,1)S(1)}, u32[]{:S(2)}, u32[]{:S(2)}) collective-permute-start(bf16[384,2944]{1,0:T(8,128)(2,1)S(1)} %slice.320), channel_id=1, source_target_pairs={{0,16},{2,18},{4,20},{6,22},{1,17},{3,19},{5,21},{7,23},{8,9},{10,... | collective-permute-start | bytes 6782984 | tf_op jit(solution)/shard_map/ppermute | solution.py:81
  413.8 17.3 %collective-permute-start.66 = (bf16[48,2944]{1,0:T(8,128)(2,1)S(1)}, bf16[48,2944]{1,0:T(8,128)(2,1)S(1)}, u32[]{:S(2)}, u32[]{:S(2)}) collective-permute-start(bf16[48,2944]{1,0:T(8,128)(2,1)S(1)} %get-tuple-element.392), channel_id=1, source_target_pairs={{0,4},{2,6},{4,0},{6,2},{1,5},{3,7},{5,1},{7,3},{8,12},{10,14},{12... | collective-permute-start | bytes 847880 | tf_op jit(solution)/shard_map/ppermute | solution.py:81
  413.8 22.3 %collective-permute-start.67 = (bf16[48,2944]{1,0:T(8,128)(2,1)S(1)}, bf16[48,2944]{1,0:T(8,128)(2,1)S(1)}, u32[]{:S(2)}, u32[]{:S(2)}) collective-permute-start(bf16[48,2944]{1,0:T(8,128)(2,1)S(1)} %get-tuple-element.391), channel_id=1, source_target_pairs={{0,6},{2,4},{4,2},{6,0},{1,7},{3,5},{5,3},{7,1},{8,14},{10,12},{12... | collective-permute-start | bytes 847880 | tf_op jit(solution)/shard_map/ppermute | solution.py:81
  460.2 16.4 %collective-permute-start.72 = (bf16[48,2944]{1,0:T(8,128)(2,1)S(1)}, bf16[48,2944]{1,0:T(8,128)(2,1)S(1)}, u32[]{:S(2)}, u32[]{:S(2)}) collective-permute-start(bf16[48,2944]{1,0:T(8,128)(2,1)S(1)} %get-tuple-element.389), channel_id=1, source_target_pairs={{0,4},{2,6},{4,0},{6,2},{1,5},{3,7},{5,1},{7,3},{8,12},{10,14},{12... | collective-permute-start | bytes 847880 | tf_op jit(solution)/shard_map/ppermute | solution.py:81
  460.2 21.5 %collective-permute-start.73 = (bf16[48,2944]{1,0:T(8,128)(2,1)S(1)}, bf16[48,2944]{1,0:T(8,128)(2,1)S(1)}, u32[]{:S(2)}, u32[]{:S(2)}) collective-permute-start(bf16[48,2944]{1,0:T(8,128)(2,1)S(1)} %get-tuple-element.388), channel_id=1, source_target_pairs={{0,6},{2,4},{4,2},{6,0},{1,7},{3,5},{5,3},{7,1},{8,14},{10,12},{12... | collective-permute-start | bytes 847880 | tf_op jit(solution)/shard_map/ppermute | solution.py:81
  (133 other events, 1282.4 us)
